TPU v7x, 32 devices: a whole 2x2x4 slice. The times are simulated.
32 devices in a mesh: section: 4 (over y, x), dp: 8 (over z, core).
Axes of the slice: x: 2, y: 2, z: 4, core: 2. Of those that a mesh axis runs over, the one named last changes fastest.
Arguments:
- d_out: bfloat16 [4, 384, 4096], P('section', 'dp'), may hold values from -6 to 6
- down_weight: bfloat16 [4, 11264, 4096], P('section', 'dp'), may hold values from -0.0546875 to 0.0546875
- gate_weight: bfloat16 [4, 11264, 4096], P('section', 'dp'), may hold values from -0.0546875 to 0.0546875
- up_weight: bfloat16 [4, 11264, 4096], P('section', 'dp'), may hold values from -0.0546875 to 0.0546875
- gate_pre: bfloat16 [4, 384, 11264], P('section', 'dp'), may hold values from -6 to 6
- up_val: bfloat16 [4, 384, 11264], P('section', 'dp'), may hold values from -6 to 6
- block_rows: int32 [4, 16], P('section'), may hold values from 0 to 87, as said below
- block_cols: int32 [4, 16], P('section'), may hold values from 0 to 31, as said below
- block_owner: int32 [4, 16], P('section'), may hold values from 0 to 7, as said below
Outputs:
- grad_input: bfloat16 [4, 384, 4096], P('section', 'dp')
- block_grads: bfloat16 [4, 24, 128, 128], P('section', 'dp')
Inputs may be any that keep to these rules, and one draw needn't show every extreme that they name: `block_rows`: the 16 (row, column) pairs of a section are all different. `block_cols`: the 16 (row, column) pairs of a section are all different. `block_owner`: in each section no replica owns more than 3 blocks, and one owns exactly 3.
All inputs are finite; a program needn't handle non-finite values.
Results may differ from a plain program's by a relative error of at most 0.018.
Values may be sent and summed in bfloat16 or wider, within the bound.
No kernel may reach another device: no remote copies, remote signals or barrier semaphores. Data moves between devices by JAX's collectives and lax.ppermute only.
A program may use at most 128 MiB of HBM per device.

v0:
```python
import jax
import jax.numpy as jnp
from jax import lax
from jax.sharding import PartitionSpec as P

CAP = 3


def passed_along(value, axis, by):
    devices = lax.axis_size(axis)
    pairs = [(i, i + by) for i in range(devices) if 0 <= i + by < devices]
    return lax.ppermute(value, axis, pairs)


def gelu_pair(values):
    coeff = 0.7978845608
    cubic = values * values * values
    tangent = jnp.tanh(coeff * (values + 0.044715 * cubic))
    activated = 0.5 * values * (1.0 + tangent)
    slope = 0.5 * (1.0 + tangent) + 0.5 * values * (1.0 - tangent * tangent) * coeff * (
        1.0 + 3.0 * 0.044715 * values * values
    )
    return (activated, slope)


def owner_slots(owners):
    count_blocks = owners.shape[0]
    same = owners[:, None] == owners[None, :]
    index_list = jnp.arange(count_blocks, dtype=jnp.int32)
    earlier = index_list[None, :] < index_list[:, None]
    return jnp.sum((same & earlier).astype(jnp.int32), axis=1)


def shards(
    d_out,
    down_weight,
    gate_weight,
    up_weight,
    gate_pre,
    up_val,
    block_rows,
    block_cols,
    block_owner,
):
    grad_rows = d_out[0]
    w_shard = down_weight[0]
    w_gate = gate_weight[0]
    w_up = up_weight[0]
    replicas = lax.axis_size("dp")
    tok_rows = grad_rows.shape[0]
    model_width = grad_rows.shape[1]
    hidden_width = gate_pre.shape[2]
    columns = lax.dot_general(
        lax.all_gather(grad_rows, "dp", axis=0, tiled=True),
        w_shard,
        (((1,), (1,)), ((), ())),
        preferred_element_type=jnp.float32,
    ).astype(jnp.bfloat16)
    returned = lax.all_to_all(columns, "dp", split_axis=0, concat_axis=1, tiled=True)
    gate_val = gate_pre[0].astype(jnp.float32)
    up_vals = up_val[0].astype(jnp.float32)
    activated, slope = gelu_pair(gate_val)
    dh_wide = returned.astype(jnp.float32)
    local_gate = (dh_wide * up_vals * slope).astype(jnp.bfloat16)
    local_up = (dh_wide * activated).astype(jnp.bfloat16)
    gate_units, up_units = (
        lax.all_to_all(local_gate, "dp", split_axis=1, concat_axis=0, tiled=True),
        lax.all_to_all(local_up, "dp", split_axis=1, concat_axis=0, tiled=True),
    )
    summed_input = lax.psum_scatter(
        (
            jnp.dot(gate_units, w_gate, preferred_element_type=jnp.float32)
            + jnp.dot(up_units, w_up, preferred_element_type=jnp.float32)
        ).astype(jnp.bfloat16),
        "dp",
        scatter_dimension=0,
        tiled=True,
    )
    grad_input = passed_along(summed_input, "section", -1)
    hidden = (activated * up_vals).astype(jnp.bfloat16)
    row_ids = block_rows[0]
    col_ids = block_cols[0]
    owners = block_owner[0]
    count_blocks = row_ids.shape[0]
    hidden_sel = jnp.take(hidden.reshape(tok_rows, hidden_width // 128, 128), row_ids, axis=1)
    grad_sel = jnp.take(grad_rows.reshape(tok_rows, model_width // 128, 128), col_ids, axis=1)
    partial_value = jnp.einsum(
        "tnf,tnd->nfd", hidden_sel, grad_sel, preferred_element_type=jnp.float32
    )
    partial_value = lax.optimization_barrier(partial_value.astype(jnp.bfloat16)).astype(jnp.float32)
    slots = owner_slots(owners)
    scale = 1.0 / replicas
    share = lax.psum_scatter(
        partial_value.astype(jnp.bfloat16), "dp", scatter_dimension=0, tiled=True
    ).astype(jnp.float32)
    rounded = (share * scale).astype(jnp.bfloat16)
    every_block = lax.all_gather(rounded, "dp", axis=0, tiled=True)
    owner_index = lax.axis_index("dp")
    slot_list = jnp.arange(CAP, dtype=jnp.int32)
    picked = (owners[None, :] == owner_index) & (slots[None, :] == slot_list[:, None])
    block_list = jnp.arange(count_blocks, dtype=jnp.int32)
    chosen = jnp.sum(jnp.where(picked, block_list[None, :], 0), axis=1)
    present = jnp.any(picked, axis=1)
    result = jnp.where(
        present[:, None, None], jnp.take(every_block, chosen, axis=0), jnp.zeros((), jnp.bfloat16)
    )
    return (grad_input[None], result[None])


def solution(mesh):
    return jax.shard_map(
        shards,
        mesh=mesh,
        in_specs=(
            P("section", "dp", None),
            P("section", "dp", None),
            P("section", "dp", None),
            P("section", "dp", None),
            P("section", "dp", None),
            P("section", "dp", None),
            P("section", None),
            P("section", None),
            P("section", None),
        ),
        out_specs=(P("section", "dp", None), P("section", "dp", None, None)),
        check_vma=False,
    )
```

profile of v0, /device:TPU:0, one launch (start us, length us, event | category | flops | bytes accessed | tf_op | source)
XLA Modules:
  0.0 242.5 jit_solution(11818620248499317119)
XLA Ops:
  7.2 0.7 all-gather.3.cloned.1.call-update
  7.9 42.8 %all-gather.3.cloned.1.call-done = bf16[1,384,4096]{2,1,0:T(8,128)(2,1)} async-done(((bf16[1,48,4096]{2,1,0:T(8,128)(2,1)}), bf16[1,384,4096]{2,1,0:T(8,128)(2,1)}) %all-gather.3.cloned.1.call-update) | async-done | bytes 3145744 | tf_op jit(solution)/shard_map/all_gather | solution.py:54
  50.7 13.5 %fusion.9 = bf16[384,1408]{1,0:T(8,128)(2,1)} fusion(bf16[1,1408,4096]{2,1,0:T(8,128)(2,1)} %param.10, bf16[1,384,4096]{2,1,0:T(8,128)(2,1)} %all-gather.3.cloned.1.call-done), kind=kOutput, calls=%fused_computation.14 | convolution fusion | flops 4429725696 | bytes 15761408 | tf_op jit(solution)/shard_map/dot_general | solution.py:53
  64.1 4.4 %all-to-all-start = ((bf16[8,48,1408]{2,1,0:T(8,128)(2,1)}), bf16[8,48,1408]{2,1,0:T(8,128)(2,1)}, u32[]{:S(2)}, u32[]{:S(2)}) async-start(bf16[8,48,1408]{2,1,0:T(8,128)(2,1)} %bitcast.2), calls=%async_computation | async-start | bytes 2162688 | tf_op jit(solution)/shard_map/all_to_all | solution.py:59
  68.5 0.2 copy.72
  68.7 1.1 copy-done.1
  69.8 1.5 copy.73
  71.3 24.5 %all-to-all-done = bf16[8,48,1408]{2,1,0:T(8,128)(2,1)} async-done(((bf16[8,48,1408]{2,1,0:T(8,128)(2,1)}), bf16[8,48,1408]{2,1,0:T(8,128)(2,1)}, u32[]{:S(2)}, u32[]{:S(2)}) %all-to-all-start) | async-done | bytes 1081376 | tf_op jit(solution)/shard_map/all_to_all | solution.py:59
  95.8 5.1 %fusion.22 = (bf16[48,8,1408]{2,0,1:T(8,128)(2,1)}, bf16[48,8,1408]{2,0,1:T(8,128)(2,1)}) fusion(bf16[8,48,1408]{2,1,0:T(8,128)(2,1)} %all-to-all-done, f32[48,8,1408]{2,1,0:T(8,128)S(1)} %bitcast.84, f32[48,8,1408]{2,1,0:T(8,128)} %bitcast.85), kind=kLoop, calls=%fused_computation.23 | loop fusion | flops 12976128 | bytes 7569408 | tf_op jit(solution)/shard_map/convert_element_type | solution.py:64
  101.0 4.4 %all-to-all-start.2 = ((bf16[48,8,1408]{2,0,1:T(8,128)(2,1)}), bf16[48,8,1408]{2,0,1:T(8,128)(2,1)}, u32[]{:S(2)}, u32[]{:S(2)}) async-start(bf16[48,8,1408]{2,0,1:T(8,128)(2,1)} %get-tuple-element.3), calls=%async_computation.2 | async-start | bytes 2162688 | tf_op jit(solution)/shard_map/all_to_all | solution.py:68
  105.8 0.4 copy.75
  106.1 0.8 copy-done.2
  107.1 1.7 copy.74
  108.9 0.6 gather_fusion.1
  109.5 2.6 %fusion.30 = bf16[48,88,128]{2,0,1:T(8,128)(2,1)S(1)} fusion(f32[48,88,128]{2,1,0:T(8,128)S(1)} %bitcast.83, f32[48,88,128]{2,1,0:T(8,128)} %bitcast.86), kind=kLoop, calls=%fused_computation.31 | loop fusion | flops 5406720 | bytes 5406720 | tf_op jit(solution)/shard_map/convert_element_type | solution.py:80
  112.1 20.5 %all-to-all-done.2 = bf16[48,8,1408]{2,0,1:T(8,128)(2,1)} async-done(((bf16[48,8,1408]{2,0,1:T(8,128)(2,1)}), bf16[48,8,1408]{2,0,1:T(8,128)(2,1)}, u32[]{:S(2)}, u32[]{:S(2)}) %all-to-all-start.2) | async-done | bytes 1081376 | tf_op jit(solution)/shard_map/all_to_all | solution.py:68
  132.6 3.6 %all-to-all-start.1 = ((bf16[48,8,1408]{2,0,1:T(8,128)(2,1)}), bf16[48,8,1408]{2,0,1:T(8,128)(2,1)S(1)}, u32[]{:S(2)}, u32[]{:S(2)}) async-start(bf16[48,8,1408]{2,0,1:T(8,128)(2,1)} %get-tuple-element.2), calls=%async_computation.1 | async-start | bytes 2162688 | tf_op jit(solution)/shard_map/all_to_all | solution.py:67
  136.3 0.6 gather_fusion
  136.9 1.3 convolution_convert_fusion
  138.2 0.2 reduce-scatter.3.cloned.1.call-start
  138.4 9.8 %fusion = f32[384,4096]{1,0:T(8,128)} fusion(bf16[384,1408]{1,0:T(8,128)(2,1)} %bitcast.8, bf16[1,1408,4096]{2,1,0:T(8,128)(2,1)} %param.12), kind=kOutput, calls=%fused_computation.3 | convolution fusion | flops 4429185024 | bytes 18907136 | tf_op jit(solution)/shard_map/dot_general | solution.py:73
  148.3 18.6 %all-to-all-done.1 = bf16[48,8,1408]{2,0,1:T(8,128)(2,1)S(1)} async-done(((bf16[48,8,1408]{2,0,1:T(8,128)(2,1)}), bf16[48,8,1408]{2,0,1:T(8,128)(2,1)S(1)}, u32[]{:S(2)}, u32[]{:S(2)}) %all-to-all-start.1) | async-done | bytes 1081376 | tf_op jit(solution)/shard_map/all_to_all | solution.py:67
  166.9 11.8 %add_convert_fusion = bf16[384,4096]{1,0:T(8,128)(2,1)} fusion(f32[384,4096]{1,0:T(8,128)} %fusion, bf16[384,1408]{1,0:T(8,128)(2,1)S(1)} %bitcast.91, bf16[1,1408,4096]{2,1,0:T(8,128)(2,1)} %param.11), kind=kOutput, calls=%fused_computation.9 | convolution fusion | flops 4432330752 | bytes 22052864 | tf_op jit(solution)/shard_map/dot_general | solution.py:72
  178.7 0.6 copy-done.6
  179.3 0.2 convert_reduce_fusion
  179.8 0.9 multiply_convert_fusion
  180.7 37.3 %reduce-scatter.3.cloned.1.call-done = bf16[48,4096]{1,0:T(8,128)(2,1)} async-done(((bf16[384,4096]{1,0:T(8,128)(2,1)}), bf16[48,4096]{1,0:T(8,128)(2,1)}) %reduce-scatter.3.cloned.1.call-update) | async-done | bytes 393232 | tf_op jit(solution)/shard_map/reduce_scatter | solution.py:70
  218.0 1.3 collective-permute-start
  219.3 14.7 %all_gather.7 = bf16[16,128,128]{2,1,0:T(8,128)(2,1)S(1)} all-gather(bf16[2,128,128]{2,1,0:T(8,128)(2,1)S(1)} %multiply_convert_fusion), channel_id=1, replica_groups=mesh['section'=4,'dp'=8] {'dp'}, dimensions={0}, use_global_device_ids=true | all-gather | bytes 589824 | tf_op jit(solution)/shard_map/all_gather | solution.py:97
  234.0 0.6 gather_fusion.2
  234.5 0.7 fusion.38
  235.3 0.7 copy.83
  (32 shorter events, 1.0 us)
Async XLA Ops:
  7.2 43.5 %all-gather.3.cloned.1.call-start = ((), (), s32[]{:S(2)}) async-start(), calls=%async_computation.7 | async-start | bytes 3538944 | tf_op jit(solution)/shard_map/all_gather | solution.py:54
  64.1 4.4 %copy-start = (bf16[1,48,11264]{2,1,0:T(8,128)(2,1)S(1)}, bf16[1,48,11264]{2,1,0:T(8,128)(2,1)}, u32[]{:S(2)}) copy-start(bf16[1,48,11264]{2,1,0:T(8,128)(2,1)} %param.14) | copy-start | bytes 3244036
  64.1 31.7 %all-to-all-start = ((bf16[8,48,1408]{2,1,0:T(8,128)(2,1)}), bf16[8,48,1408]{2,1,0:T(8,128)(2,1)}, u32[]{:S(2)}, u32[]{:S(2)}) async-start(bf16[8,48,1408]{2,1,0:T(8,128)(2,1)} %bitcast.2), calls=%async_computation | async-start | bytes 2162688 | tf_op jit(solution)/shard_map/all_to_all | solution.py:59
  68.5 1.2 copy-start.1
  101.0 4.4 %copy-start.3 = (bf16[1,48,4096]{2,1,0:T(8,128)(2,1)S(1)}, bf16[1,48,4096]{2,1,0:T(8,128)(2,1)}, u32[]{:S(2)}) copy-start(bf16[1,48,4096]{2,1,0:T(8,128)(2,1)} %param.9) | copy-start | bytes 1179652
  101.0 31.7 %all-to-all-start.2 = ((bf16[48,8,1408]{2,0,1:T(8,128)(2,1)}), bf16[48,8,1408]{2,0,1:T(8,128)(2,1)}, u32[]{:S(2)}, u32[]{:S(2)}) async-start(bf16[48,8,1408]{2,0,1:T(8,128)(2,1)} %get-tuple-element.3), calls=%async_computation.2 | async-start | bytes 2162688 | tf_op jit(solution)/shard_map/all_to_all | solution.py:68
  105.7 1.2 copy-start.2
  107.1 1.7 copy-start.4
  112.1 24.2 %copy-start.5 = (s32[1,16]{1,0:T(1,128)S(1)}, s32[1,16]{1,0:T(1,128)}, u32[]{:S(2)}) copy-start(s32[1,16]{1,0:T(1,128)} %param.15) | copy-start | bytes 196
  132.6 34.3 %all-to-all-start.1 = ((bf16[48,8,1408]{2,0,1:T(8,128)(2,1)}), bf16[48,8,1408]{2,0,1:T(8,128)(2,1)S(1)}, u32[]{:S(2)}, u32[]{:S(2)}) async-start(bf16[48,8,1408]{2,0,1:T(8,128)(2,1)} %get-tuple-element.2), calls=%async_computation.1 | async-start | bytes 2162688 | tf_op jit(solution)/shard_map/all_to_all | solution.py:67
  136.2 43.6 %reduce-scatter.5.cloned.1.call-start = ((), (), s32[]{:S(2)}) async-start(), calls=%async_computation.6 | async-start | bytes 589824 | tf_op jit(solution)/shard_map/reduce_scatter | solution.py:93
  138.2 79.8 %reduce-scatter.3.cloned.1.call-start = ((), (), s32[]{:S(2)}) async-start(), calls=%async_computation.5 | async-start | bytes 3538944 | tf_op jit(solution)/shard_map/reduce_scatter | solution.py:70
  178.7 0.7 copy-start.6
  218.0 17.2 %collective-permute-start = (bf16[48,4096]{1,0:T(8,128)(2,1)}, bf16[48,4096]{1,0:T(8,128)(2,1)S(1)}, u32[]{:S(2)}, u32[]{:S(2)}) collective-permute-start(bf16[48,4096]{1,0:T(8,128)(2,1)} %reduce-scatter.3.cloned.1.call-done), channel_id=1, source_target_pairs={{8,0},{16,8},{24,16},{9,1},{17,9},{25,17},{10,2},{18,10},{26,18},{... | collective-permute-start | bytes 1179656 | tf_op jit(solution)/shard_map/ppermute | solution.py:12
Sparse Core Ops, SparseCore 0:
  9.6 40.9 all-gather.2
  139.3 33.5 reduce-scatter.4
  178.8 39.1 reduce-scatter.2
where the time goes:
time: 244 us; the launch traced here: 243 us
  waiting for transfers between devices  145 us (59%)
  matrix products  36.3 us (15%)
  blocking collectives  14.7 us (6%)
  between operations  14 us (6%)
  starting transfers between devices  13.9 us (6%)
  other arithmetic  10.1 us (4%)
  local copies, waits for them, and re-layouts  9.03 us (4%)
    all_gather x1, waiting for transfers between devices, shards(): lax.all_gather(grad_rows, 'dp', axis=0, tiled=True)  42.8 us
    reduce_scatter x1, waiting for transfers between devices, shards(): lax.psum_scatter((jnp.dot(gate_units, w_gate, preferred_element_type=jnp....  37.3 us
    all_to_all x1, waiting for transfers between devices, shards(): lax.all_to_all(columns, 'dp', split_axis=0, concat_axis=1, tiled=True)  24.5 us
    all_to_all x1, waiting for transfers between devices, shards(): lax.all_to_all(local_up, 'dp', split_axis=1, concat_axis=0, tiled=True)  20.5 us
    all_to_all x1, waiting for transfers between devices, shards(): lax.all_to_all(local_gate, 'dp', split_axis=1, concat_axis=0, tiled=True)  18.6 us
    all_gather x1, blocking collectives, shards(): every_block = lax.all_gather(rounded, 'dp', axis=0, tiled=True)  14.7 us
    dot_general x1, matrix products, shards(): lax.dot_general(lax.all_gather(grad_rows, 'dp', axis=0, tiled=True), w_sh...  13.5 us
    dot_general x1, matrix products, shards(): jnp.dot(gate_units, w_gate, preferred_element_type=jnp.float32)  11.8 us
  transfers between devices with their start and end apart: 7, of which 5 were waited for; matrix products, arithmetic and copies ran while one was open for 14% of the time, Pallas kernels for 0%

commit v1 on v0

v1 whole, which is shorter than its diff:
```python
import jax
import jax.numpy as jnp
from jax import lax
from jax.sharding import PartitionSpec as P

CAP = 3
LANES = 128


def gelu(values):
    coeff = 0.7978845608
    tangent = jnp.tanh(coeff * (values + 0.044715 * (values * values * values)))
    return 0.5 * values * (1.0 + tangent)


def gelu_slope(values):
    coeff = 0.7978845608
    square = values * values
    tangent = jnp.tanh(coeff * (values + 0.044715 * (square * values)))
    return 0.5 * (1.0 + tangent) + 0.5 * values * (1.0 - tangent * tangent) * coeff * (
        1.0 + 3.0 * 0.044715 * square
    )


def owner_table(owners, replicas):
    blocks = jnp.arange(owners.shape[0], dtype=jnp.int32)
    earlier = (owners[:, None] == owners[None, :]) & (blocks[None, :] < blocks[:, None])
    slots = jnp.sum(earlier.astype(jnp.int32), axis=1)
    places = jnp.arange(replicas * CAP, dtype=jnp.int32)
    hit = (owners * CAP + slots)[None, :] == places[:, None]
    chosen = jnp.sum(jnp.where(hit, blocks[None, :], 0), axis=1)
    return chosen.reshape(replicas, CAP), jnp.any(hit, axis=1).reshape(replicas, CAP)


def rotated(value, by):
    devices = lax.axis_size("dp")
    pairs = [(i, (i + 2 * by) % devices) for i in range(devices)]
    return lax.ppermute(value, "dp", pairs)


def swapped(value):
    return lax.ppermute(value, "dp", [(i, i ^ 1) for i in range(lax.axis_size("dp"))])


def relayed(value, by):
    devices, sections = lax.axis_size("dp"), lax.axis_size("section")
    pairs = [
        (s * devices + i, (s - 1) * devices + (i - 2 * by) % devices)
        for s in range(1, sections)
        for i in range(devices)
    ]
    return lax.ppermute(value, ("section", "dp"), pairs)


def shards(d_out, down_weight, gate_weight, up_weight, gate_pre, up_val, rows, cols, owner):
    mine = d_out[0]
    w_down, w_gate, w_up = down_weight[0], gate_weight[0], up_weight[0]
    gate, up = gate_pre[0], up_val[0]
    tokens, width = mine.shape
    units = w_down.shape[0]
    replicas = lax.axis_size("dp")
    chips = replicas // 2
    me = lax.axis_index("dp")
    chip, core = me // 2, me % 2

    same = [mine] + [rotated(mine, r) for r in range(1, chips)]
    other = [swapped(part) for part in same]
    grads = jnp.concatenate(same + other, axis=0)

    chosen, present = owner_table(owner[0], replicas)
    row_ids = jnp.take(rows[0], chosen.reshape(-1))
    col_ids = jnp.take(cols[0], chosen.reshape(-1)).reshape(replicas, CAP)

    def picked(values):
        tiles = values.reshape(tokens, values.shape[1] // LANES, LANES)
        return jnp.take(tiles, row_ids, axis=1).astype(jnp.float32)

    hidden = jnp.where(present.reshape(1, -1, 1), gelu(picked(gate)) * picked(up), 0.0)
    hidden = hidden.astype(jnp.bfloat16).reshape(tokens, replicas, CAP * LANES)

    def columns_of(values, replica):
        return lax.dynamic_slice_in_dim(values, replica * units, units, 1)

    def with_hidden(replica):
        extra = lax.dynamic_index_in_dim(hidden, replica, 1, keepdims=False)
        return jnp.concatenate([columns_of(gate, replica), extra], axis=1)

    def up_columns(replica):
        return columns_of(up, replica)

    def exchanged(part):
        given = jnp.stack([part(2 * ((chip + r) % chips) + 1 - core) for r in range(chips)])
        taken = swapped(given)
        pieces = []
        for r in range(chips):
            both = jnp.stack([part(2 * ((chip + r) % chips) + core), taken[r]])
            pieces.append(both if r == 0 else rotated(both, r))
        return jnp.stack(pieces, axis=1)

    gate_all = exchanged(with_hidden).reshape(replicas * tokens, -1)
    up_all = exchanged(up_columns).reshape(replicas * tokens, -1).astype(jnp.float32)
    hidden_all = gate_all[:, units:]
    gate_all = gate_all[:, :units].astype(jnp.float32)

    dhidden = lax.dot_general(
        grads, w_down, (((1,), (1,)), ((), ())), preferred_element_type=jnp.float32
    ).astype(jnp.bfloat16)
    wide = dhidden.astype(jnp.float32)
    local_up = (wide * gelu(gate_all)).astype(jnp.bfloat16)
    local_gate = (wide * up_all * gelu_slope(gate_all)).astype(jnp.bfloat16)

    halves = 2
    step = width // halves
    results = []
    for h in range(halves):
        part = slice(h * step, (h + 1) * step)
        term = jnp.dot(local_up, w_up[:, part], preferred_element_type=jnp.float32) + jnp.dot(
            local_gate, w_gate[:, part], preferred_element_type=jnp.float32
        )
        term = term.astype(jnp.bfloat16).reshape(2, chips, tokens, step)
        pair = (term[0].astype(jnp.float32) + swapped(term[1]).astype(jnp.float32)).astype(jnp.bfloat16)
        total = jnp.zeros((tokens, step), jnp.float32)
        for r in range(chips):
            total = total + relayed(pair[r], r).astype(jnp.float32)
        results.append(total.astype(jnp.bfloat16))
    grad_input = jnp.concatenate(results, axis=1)

    my_cols = lax.dynamic_index_in_dim(col_ids, me, 0, keepdims=False)
    sums = []
    for k in range(CAP):
        block = lax.dynamic_slice_in_dim(grads, my_cols[k] * LANES, LANES, 1)
        sums.append(
            lax.dot_general(
                hidden_all[:, k * LANES : (k + 1) * LANES],
                block,
                (((0,), (0,)), ((), ())),
                preferred_element_type=jnp.float32,
            )
        )
    block_grads = (jnp.stack(sums) * (1.0 / replicas)).astype(jnp.bfloat16)
    return (grad_input[None], block_grads[None])


def solution(mesh):
    return jax.shard_map(
        shards,
        mesh=mesh,
        in_specs=(P("section", "dp", None),) * 6 + (P("section", None),) * 3,
        out_specs=(P("section", "dp", None), P("section", "dp", None, None)),
        check_vma=False,
    )
```

time: 244 us -> 178 us (0.73)
  waiting for transfers between devices: 145 us -> 79.3 us
  starting transfers between devices: 13.9 us -> 34.9 us
  blocking collectives: 14.7 us -> 0 us
  local copies, waits for them, and re-layouts: 9.03 us -> 21.9 us
  between operations: 14 us -> 3.42 us
  matrix products: 36.3 us -> 29.1 us
    ppermute x1 -> x25, waiting for transfers between devices: 0.01 us -> 79.3 us  [the longest x9 39.7 us: rotated(): return lax.ppermute(value, 'dp', pairs)]
    all_to_all x3 -> x0, waiting for transfers between devices: 63.7 us -> none  [the longest x1 24.5 us: shards(): lax.all_to_all(columns, 'dp', split_axis=0, concat_axis=1, tiled=True)]
    all_gather x1 -> x0, waiting for transfers between devices: 42.8 us -> none  [shards(): lax.all_gather(grad_rows, 'dp', axis=0, tiled=True)]
    reduce_scatter x2 -> x0, waiting for transfers between devices: 37.4 us -> none  [the longest x1 37.3 us: shards(): lax.psum_scatter((jnp.dot(gate_units, w_gate, preferred_element_type=jnp....]
    ppermute x1 -> x25, starting transfers between devices: 1.28 us -> 34.9 us  [the longest x9 22.8 us: rotated(): return lax.ppermute(value, 'dp', pairs)]
    all_gather x1 -> x0, blocking collectives: 14.7 us -> none  [shards(): every_block = lax.all_gather(rounded, 'dp', axis=0, tiled=True)]
    all_to_all x3 -> x0, starting transfers between devices: 12.3 us -> none  [the longest x1 4.39 us: shards(): lax.all_to_all(columns, 'dp', split_axis=0, concat_axis=1, tiled=True)]
    dot_general x4 -> x8, matrix products: 36.3 us -> 29.1 us  [the longest x1 10.4 us: shards(): lax.dot_general(grads, w_down, (((1,), (1,)), ((), ())), preferred_elemen...]
  transfers between devices with their start and end apart: 7 -> 25, of which waited for: 5 -> 10; matrix products, arithmetic and copies ran while one was open for 14% -> 20% of each run, Pallas kernels for 0% -> 0%
where the time goes in v1:
time: 178 us
  waiting for transfers between devices  79.3 us (45%)
  starting transfers between devices  34.9 us (20%)
  matrix products  29.1 us (16%)
  local copies, waits for them, and re-layouts  21.9 us (12%)
  other arithmetic  8.96 us (5%)
  between operations  3.42 us (2%)
    ppermute x9, waiting for transfers between devices, rotated(): return lax.ppermute(value, 'dp', pairs)  39.7 us
    ppermute x8, waiting for transfers between devices, relayed(): return lax.ppermute(value, ('section', 'dp'), pairs)  39.6 us
    ppermute x9, starting transfers between devices, rotated(): return lax.ppermute(value, 'dp', pairs)  22.8 us
    unnamed x37, local copies, waits for them, and re-layouts  13 us
    dot_general x1, matrix products, shards(): lax.dot_general(grads, w_down, (((1,), (1,)), ((), ())), preferred_elemen...  10.4 us
    ppermute x8, starting transfers between devices, relayed(): return lax.ppermute(value, ('section', 'dp'), pairs)  10.3 us
    dot_general x2, matrix products, shards(): jnp.dot(local_gate, w_gate[:, part], preferred_element_type=jnp.float32)  9.55 us
    dot_general x2, matrix products, shards(): jnp.dot(local_up, w_up[:, part], preferred_element_type=jnp.float32)  5.91 us
  transfers between devices with their start and end apart: 25, of which 10 were waited for; matrix products, arithmetic and copies ran while one was open for 20% of the time, Pallas kernels for 0%

profile of v1, /device:TPU:0, one launch (start us, length us, event | category | flops | bytes accessed | tf_op | source)
XLA Modules:
  0.0 177.6 jit_solution(6361029660729052570)
XLA Ops:
  0.6 3.1 %collective-permute-start = (bf16[48,4096]{1,0:T(8,128)(2,1)}, bf16[48,4096]{1,0:T(8,128)(2,1)}, u32[]{:S(2)}, u32[]{:S(2)}) collective-permute-start(bf16[48,4096]{1,0:T(8,128)(2,1)} %bitcast.153), channel_id=1, source_target_pairs={{0,2},{1,3},{2,4},{3,5},{4,6},{5,7},{6,0},{7,1},{8,10},{9,11},{10,... | collective-permute-start | bytes 1179656 | tf_op jit(solution)/shard_map/ppermute | solution.py:38
  3.7 2.6 %collective-permute-start.1 = (bf16[48,4096]{1,0:T(8,128)(2,1)}, bf16[48,4096]{1,0:T(8,128)(2,1)}, u32[]{:S(2)}, u32[]{:S(2)}) collective-permute-start(bf16[48,4096]{1,0:T(8,128)(2,1)} %bitcast.154), channel_id=1, source_target_pairs={{0,4},{1,5},{2,6},{3,7},{4,0},{5,1},{6,2},{7,3},{8,12},{9,13},{10,... | collective-permute-start | bytes 1179656 | tf_op jit(solution)/shard_map/ppermute | solution.py:38
  6.3 1.3 collective-permute-start.2
  10.3 1.5 copy.56
  12.8 1.3 gather_fusion.2
  14.1 1.3 fusion.39
  15.8 1.3 constant_dynamic-slice_fusion.16
  28.6 1.8 %constant_dynamic-update-slice_fusion.6 = bf16[384,4096]{1,0:T(8,128)(2,1)} fusion(bf16[384,4096]{1,0:T(8,128)(2,1)} %constant_dynamic-update-slice_fusion.7, bf16[48,4096]{1,0:T(8,128)(2,1)} %collective-permute-done), kind=kLoop, calls=%fused_computation.117 | loop fusion | bytes 786432
  30.4 1.7 collective-permute-done.1
  32.2 1.8 constant_dynamic-update-slice_fusion.5
  34.4 1.8 %constant_dynamic-update-slice_fusion.4 = bf16[384,4096]{1,0:T(8,128)(2,1)} fusion(bf16[384,4096]{1,0:T(8,128)(2,1)} %constant_dynamic-update-slice_fusion.5, bf16[48,4096]{1,0:T(8,128)(2,1)} %collective-permute-done.2), kind=kLoop, calls=%fused_computation.115 | loop fusion | bytes 786432
  36.2 1.8 constant_dynamic-update-slice_fusion.3
  38.1 7.2 %collective-permute-start.12 = (bf16[2,48,1408]{2,1,0:T(8,128)(2,1)S(1)}, bf16[2,48,1408]{2,1,0:T(8,128)(2,1)S(1)}, u32[]{:S(2)}, u32[]{:S(2)}) collective-permute-start(bf16[2,48,1408]{2,1,0:T(8,128)(2,1)S(1)} %pad_maximum_fusion.6), channel_id=1, source_target_pairs={{0,2},{1,3},{2,4},{3,5},{4,6},{5,7},{6,0},{7,1},{8,10},{9,11},{10,... | collective-permute-start | bytes 811016 | tf_op jit(solution)/shard_map/ppermute | solution.py:38
  45.4 3.4 %collective-permute-start.13 = (bf16[2,48,1408]{2,1,0:T(8,128)(2,1)S(1)}, bf16[2,48,1408]{2,1,0:T(8,128)(2,1)S(1)}, u32[]{:S(2)}, u32[]{:S(2)}) collective-permute-start(bf16[2,48,1408]{2,1,0:T(8,128)(2,1)S(1)} %pad_maximum_fusion.7), channel_id=1, source_target_pairs={{0,4},{1,5},{2,6},{3,7},{4,0},{5,1},{6,2},{7,3},{8,12},{9,13},{10,... | collective-permute-start | bytes 811016 | tf_op jit(solution)/shard_map/ppermute | solution.py:38
  49.9 2.0 %collective-permute-start.8 = (bf16[2,48,1792]{2,1,0:T(8,128)(2,1)S(1)}, bf16[2,48,1792]{2,1,0:T(8,128)(2,1)S(1)}, u32[]{:S(2)}, u32[]{:S(2)}) collective-permute-start(bf16[2,48,1792]{2,1,0:T(8,128)(2,1)S(1)} %pad_maximum_fusion.3), channel_id=1, source_target_pairs={{0,2},{1,3},{2,4},{3,5},{4,6},{5,7},{6,0},{7,1},{8,10},{9,11},{10,... | collective-permute-start | bytes 1032200 | tf_op jit(solution)/shard_map/ppermute | solution.py:38
  52.7 2.8 %collective-permute-done.12 = bf16[2,48,1408]{2,1,0:T(8,128)(2,1)S(1)} collective-permute-done((bf16[2,48,1408]{2,1,0:T(8,128)(2,1)S(1)}, bf16[2,48,1408]{2,1,0:T(8,128)(2,1)S(1)}, u32[]{:S(2)}, u32[]{:S(2)}) %collective-permute-start.12) | collective-permute-done | bytes 270368 | tf_op jit(solution)/shard_map/ppermute | solution.py:38
  55.6 3.1 %collective-permute-start.10 = (bf16[2,48,1792]{2,1,0:T(8,128)(2,1)S(1)}, bf16[2,48,1792]{2,1,0:T(8,128)(2,1)S(1)}, u32[]{:S(2)}, u32[]{:S(2)}) collective-permute-start(bf16[2,48,1792]{2,1,0:T(8,128)(2,1)S(1)} %pad_maximum_fusion.5), channel_id=1, source_target_pairs={{0,6},{1,7},{2,0},{3,1},{4,2},{5,3},{6,4},{7,5},{8,14},{9,15},{10,... | collective-permute-start | bytes 1032200 | tf_op jit(solution)/shard_map/ppermute | solution.py:38
  59.4 7.8 %collective-permute-done.13 = bf16[2,48,1408]{2,1,0:T(8,128)(2,1)S(1)} collective-permute-done((bf16[2,48,1408]{2,1,0:T(8,128)(2,1)S(1)}, bf16[2,48,1408]{2,1,0:T(8,128)(2,1)S(1)}, u32[]{:S(2)}, u32[]{:S(2)}) %collective-permute-start.13) | collective-permute-done | bytes 270368 | tf_op jit(solution)/shard_map/ppermute | solution.py:38
  67.5 7.1 %collective-permute-done.8 = bf16[2,48,1792]{2,1,0:T(8,128)(2,1)S(1)} collective-permute-done((bf16[2,48,1792]{2,1,0:T(8,128)(2,1)S(1)}, bf16[2,48,1792]{2,1,0:T(8,128)(2,1)S(1)}, u32[]{:S(2)}, u32[]{:S(2)}) %collective-permute-start.8) | collective-permute-done | bytes 344096 | tf_op jit(solution)/shard_map/ppermute | solution.py:38
  74.6 20.3 %collective-permute-done.9 = bf16[2,48,1792]{2,1,0:T(8,128)(2,1)S(1)} collective-permute-done((bf16[2,48,1792]{2,1,0:T(8,128)(2,1)S(1)}, bf16[2,48,1792]{2,1,0:T(8,128)(2,1)S(1)}, u32[]{:S(2)}, u32[]{:S(2)}) %collective-permute-start.9) | collective-permute-done | bytes 344096 | tf_op jit(solution)/shard_map/ppermute | solution.py:38
  95.0 10.4 %fusion.29 = (bf16[384,1408]{1,0:T(8,128)(2,1)S(1)}, f32[384,1408]{1,0:T(8,128)S(1)}) fusion(f32[2,4,48,1408]{3,2,1,0:T(8,128)S(1)} %copy.47, bf16[384,1792]{1,0:T(8,128)(2,1)S(1)} %bitcast.145, bf16[384,4096]{1,0:T(8,128)(2,1)} %constant_dynamic-update-slice_fusion, bf16[1,1408,4096]{2,1,0:T(8,128)(2,1)} %param.14), kind=kOutput, calls=%fused_computation.31 | convolution fusion | flops 4441079808 | bytes 21168128 | tf_op jit(solution)/shard_map/dot_general | solution.py:105
  105.5 4.8 %fusion.6 = f32[384,2048]{1,0:T(8,128)S(1)} fusion(bf16[384,1408]{1,0:T(8,128)(2,1)S(1)} %get-tuple-element.53, bf16[1408,4096]{1,0:T(8,128)(2,1)} %bitcast.163), kind=kOutput, calls=%fused_computation.10 | convolution fusion | flops 2214592512 | bytes 9994240 | tf_op jit(solution)/shard_map/dot_general | solution.py:117
  110.2 4.8 %fusion.2 = f32[384,2048]{1,0:T(8,128)S(1)} fusion(bf16[384,1408]{1,0:T(8,128)(2,1)S(1)} %get-tuple-element.53, bf16[1408,4096]{1,0:T(8,128)(2,1)} %bitcast.164), kind=kOutput, calls=%fused_computation.6 | convolution fusion | flops 2214592512 | bytes 9994240 | tf_op jit(solution)/shard_map/dot_general | solution.py:117
  115.1 3.0 %add_convert_fusion.1 = bf16[384,2048]{1,0:T(8,128)(2,1)S(1)} fusion(f32[384,2048]{1,0:T(8,128)S(1)} %fusion.6, bf16[1408,4096]{1,0:T(8,128)(2,1)S(1)} %bitcast.167, f32[384,1408]{1,0:T(8,128)S(1)} %get-tuple-element.54, bf16[384,1792]{1,0:T(8,128)(2,1)S(1)} %bitcast.146), kind=kOutput, calls=%fused_computation.19 | convolution fusion | flops 2222112768 | bytes 13729792 | tf_op jit(solution)/shard_map/dot_general | solution.py:117
  118.3 3.0 %add_convert_fusion = bf16[384,2048]{1,0:T(8,128)(2,1)S(1)} fusion(f32[384,2048]{1,0:T(8,128)S(1)} %fusion.2, bf16[1408,4096]{1,0:T(8,128)(2,1)S(1)} %bitcast.168, f32[384,1408]{1,0:T(8,128)S(1)} %get-tuple-element.54, bf16[384,1792]{1,0:T(8,128)(2,1)S(1)} %bitcast.147), kind=kOutput, calls=%fused_computation.18 | convolution fusion | flops 2222112768 | bytes 13729792 | tf_op jit(solution)/shard_map/dot_general | solution.py:117
  126.3 1.3 collective-permute-start.16
  127.6 1.3 collective-permute-start.17
  133.1 1.9 %collective-permute-done.16 = bf16[48,2048]{1,0:T(8,128)(2,1)S(1)} collective-permute-done((bf16[48,2048]{1,0:T(8,128)(2,1)S(1)}, bf16[48,2048]{1,0:T(8,128)(2,1)S(1)}, u32[]{:S(2)}, u32[]{:S(2)}) %collective-permute-start.16) | collective-permute-done | bytes 196640 | tf_op jit(solution)/shard_map/ppermute | solution.py:52
  136.3 8.0 %collective-permute-done.17 = bf16[48,2048]{1,0:T(8,128)(2,1)S(1)} collective-permute-done((bf16[48,2048]{1,0:T(8,128)(2,1)S(1)}, bf16[48,2048]{1,0:T(8,128)(2,1)S(1)}, u32[]{:S(2)}, u32[]{:S(2)}) %collective-permute-start.17) | collective-permute-done | bytes 196640 | tf_op jit(solution)/shard_map/ppermute | solution.py:52
  145.6 11.7 %collective-permute-done.18 = bf16[48,2048]{1,0:T(8,128)(2,1)S(1)} collective-permute-done((bf16[48,2048]{1,0:T(8,128)(2,1)S(1)}, bf16[48,2048]{1,0:T(8,128)(2,1)S(1)}, u32[]{:S(2)}, u32[]{:S(2)}) %collective-permute-start.18) | collective-permute-done | bytes 196640 | tf_op jit(solution)/shard_map/ppermute | solution.py:52
  158.7 5.3 %collective-permute-done.22 = bf16[48,2048]{1,0:T(8,128)(2,1)S(1)} collective-permute-done((bf16[48,2048]{1,0:T(8,128)(2,1)S(1)}, bf16[48,2048]{1,0:T(8,128)(2,1)S(1)}, u32[]{:S(2)}, u32[]{:S(2)}) %collective-permute-start.22) | collective-permute-done | bytes 196640 | tf_op jit(solution)/shard_map/ppermute | solution.py:52
  164.0 12.7 %collective-permute-done.23 = bf16[48,2048]{1,0:T(8,128)(2,1)S(1)} collective-permute-done((bf16[48,2048]{1,0:T(8,128)(2,1)S(1)}, bf16[48,2048]{1,0:T(8,128)(2,1)S(1)}, u32[]{:S(2)}, u32[]{:S(2)}) %collective-permute-start.23) | collective-permute-done | bytes 196640 | tf_op jit(solution)/shard_map/ppermute | solution.py:52
  (122 shorter events, 31.2 us)
Async XLA Ops:
  0.6 8.9 %copy-start = (s32[1,16]{1,0:T(1,128)S(1)}, s32[1,16]{1,0:T(1,128)}, u32[]{:S(2)}) copy-start(s32[1,16]{1,0:T(1,128)} %param.19) | copy-start | bytes 196
  0.6 27.9 %collective-permute-start = (bf16[48,4096]{1,0:T(8,128)(2,1)}, bf16[48,4096]{1,0:T(8,128)(2,1)}, u32[]{:S(2)}, u32[]{:S(2)}) collective-permute-start(bf16[48,4096]{1,0:T(8,128)(2,1)} %bitcast.153), channel_id=1, source_target_pairs={{0,2},{1,3},{2,4},{3,5},{4,6},{5,7},{6,0},{7,1},{8,10},{9,11},{10,... | collective-permute-start | bytes 1179656 | tf_op jit(solution)/shard_map/ppermute | solution.py:38
  3.7 28.4 %collective-permute-start.1 = (bf16[48,4096]{1,0:T(8,128)(2,1)}, bf16[48,4096]{1,0:T(8,128)(2,1)}, u32[]{:S(2)}, u32[]{:S(2)}) collective-permute-start(bf16[48,4096]{1,0:T(8,128)(2,1)} %bitcast.154), channel_id=1, source_target_pairs={{0,4},{1,5},{2,6},{3,7},{4,0},{5,1},{6,2},{7,3},{8,12},{9,13},{10,... | collective-permute-start | bytes 1179656 | tf_op jit(solution)/shard_map/ppermute | solution.py:38
  6.3 27.6 %collective-permute-start.2 = (bf16[48,4096]{1,0:T(8,128)(2,1)}, bf16[48,4096]{1,0:T(8,128)(2,1)}, u32[]{:S(2)}, u32[]{:S(2)}) collective-permute-start(bf16[48,4096]{1,0:T(8,128)(2,1)} %bitcast.155), channel_id=1, source_target_pairs={{0,6},{1,7},{2,0},{3,1},{4,2},{5,3},{6,4},{7,5},{8,14},{9,15},{10,... | collective-permute-start | bytes 1179656 | tf_op jit(solution)/shard_map/ppermute | solution.py:38
  7.7 28.6 %collective-permute-start.3 = (bf16[48,4096]{1,0:T(8,128)(2,1)}, bf16[48,4096]{1,0:T(8,128)(2,1)}, u32[]{:S(2)}, u32[]{:S(2)}) collective-permute-start(bf16[48,4096]{1,0:T(8,128)(2,1)} %bitcast.156), channel_id=1, source_target_pairs={{0,1},{1,0},{2,3},{3,2},{4,5},{5,4},{6,7},{7,6},{8,9},{9,8},{10,11... | collective-permute-start | bytes 1179656 | tf_op jit(solution)/shard_map/ppermute | solution.py:42
  12.8 4.3 %copy-start.3 = (bf16[1,48,11264]{2,1,0:T(8,128)(2,1)S(1)}, bf16[1,48,11264]{2,1,0:T(8,128)(2,1)}, u32[]{:S(2)}) copy-start(bf16[1,48,11264]{2,1,0:T(8,128)(2,1)} %param.17) | copy-start | bytes 3244036
  18.2 27.2 %collective-permute-start.7 = (bf16[4,48,1792]{2,1,0:T(8,128)(2,1)S(1)}, bf16[4,48,1792]{2,1,0:T(8,128)(2,1)S(1)}, u32[]{:S(2)}, u32[]{:S(2)}) collective-permute-start(bf16[4,48,1792]{2,1,0:T(8,128)(2,1)S(1)} %pad_maximum_fusion.1), channel_id=1, source_target_pairs={{0,1},{1,0},{2,3},{3,2},{4,5},{5,4},{6,7},{7,6},{8,9},{9,8},{10,11... | collective-permute-start | bytes 2064392 | tf_op jit(solution)/shard_map/ppermute | solution.py:42
  28.5 9.5 %copy-start.5 = (bf16[1,48,1408]{2,1,0:T(8,128)(2,1)S(1)}, bf16[1,48,1408]{2,1,0:T(8,128)(2,1)}, u32[]{:S(2)}) copy-start(bf16[1,48,1408]{2,1,0:T(8,128)(2,1)} %get-tuple-element.19) | copy-start | bytes 405508
  28.5 9.5 %collective-permute-start.11 = (bf16[4,48,1408]{2,1,0:T(8,128)(2,1)S(1)}, bf16[4,48,1408]{2,1,0:T(8,128)(2,1)S(1)}, u32[]{:S(2)}, u32[]{:S(2)}) collective-permute-start(bf16[4,48,1408]{2,1,0:T(8,128)(2,1)S(1)} %pad_maximum_fusion.2), channel_id=1, source_target_pairs={{0,1},{1,0},{2,3},{3,2},{4,5},{5,4},{6,7},{7,6},{8,9},{9,8},{10,11... | collective-permute-start | bytes 1622024 | tf_op jit(solution)/shard_map/ppermute | solution.py:42
  32.2 16.9 %collective-permute-start.4 = (bf16[48,4096]{1,0:T(8,128)(2,1)}, bf16[48,4096]{1,0:T(8,128)(2,1)S(1)}, u32[]{:S(2)}, u32[]{:S(2)}) collective-permute-start(bf16[48,4096]{1,0:T(8,128)(2,1)} %collective-permute-done), channel_id=1, source_target_pairs={{0,1},{1,0},{2,3},{3,2},{4,5},{5,4},{6,7},{7,6},{8,9},{9,8},{10,11... | collective-permute-start | bytes 1179656 | tf_op jit(solution)/shard_map/ppermute | solution.py:42
  33.9 16.0 %collective-permute-start.5 = (bf16[48,4096]{1,0:T(8,128)(2,1)}, bf16[48,4096]{1,0:T(8,128)(2,1)S(1)}, u32[]{:S(2)}, u32[]{:S(2)}) collective-permute-start(bf16[48,4096]{1,0:T(8,128)(2,1)} %collective-permute-done.1), channel_id=1, source_target_pairs={{0,1},{1,0},{2,3},{3,2},{4,5},{5,4},{6,7},{7,6},{8,9},{9,8},{10,11... | collective-permute-start | bytes 1179656 | tf_op jit(solution)/shard_map/ppermute | solution.py:42
  36.2 16.5 %collective-permute-start.6 = (bf16[48,4096]{1,0:T(8,128)(2,1)}, bf16[48,4096]{1,0:T(8,128)(2,1)S(1)}, u32[]{:S(2)}, u32[]{:S(2)}) collective-permute-start(bf16[48,4096]{1,0:T(8,128)(2,1)} %collective-permute-done.2), channel_id=1, source_target_pairs={{0,1},{1,0},{2,3},{3,2},{4,5},{5,4},{6,7},{7,6},{8,9},{9,8},{10,11... | collective-permute-start | bytes 1179656 | tf_op jit(solution)/shard_map/ppermute | solution.py:42
  38.1 17.4 %collective-permute-start.12 = (bf16[2,48,1408]{2,1,0:T(8,128)(2,1)S(1)}, bf16[2,48,1408]{2,1,0:T(8,128)(2,1)S(1)}, u32[]{:S(2)}, u32[]{:S(2)}) collective-permute-start(bf16[2,48,1408]{2,1,0:T(8,128)(2,1)S(1)} %pad_maximum_fusion.6), channel_id=1, source_target_pairs={{0,2},{1,3},{2,4},{3,5},{4,6},{5,7},{6,0},{7,1},{8,10},{9,11},{10,... | collective-permute-start | bytes 811016 | tf_op jit(solution)/shard_map/ppermute | solution.py:38
  45.4 21.7 %collective-permute-start.13 = (bf16[2,48,1408]{2,1,0:T(8,128)(2,1)S(1)}, bf16[2,48,1408]{2,1,0:T(8,128)(2,1)S(1)}, u32[]{:S(2)}, u32[]{:S(2)}) collective-permute-start(bf16[2,48,1408]{2,1,0:T(8,128)(2,1)S(1)} %pad_maximum_fusion.7), channel_id=1, source_target_pairs={{0,4},{1,5},{2,6},{3,7},{4,0},{5,1},{6,2},{7,3},{8,12},{9,13},{10,... | collective-permute-start | bytes 811016 | tf_op jit(solution)/shard_map/ppermute | solution.py:38
  49.1 18.1 %collective-permute-start.14 = (bf16[2,48,1408]{2,1,0:T(8,128)(2,1)S(1)}, bf16[2,48,1408]{2,1,0:T(8,128)(2,1)S(1)}, u32[]{:S(2)}, u32[]{:S(2)}) collective-permute-start(bf16[2,48,1408]{2,1,0:T(8,128)(2,1)S(1)} %pad_maximum_fusion.8), channel_id=1, source_target_pairs={{0,6},{1,7},{2,0},{3,1},{4,2},{5,3},{6,4},{7,5},{8,14},{9,15},{10,... | collective-permute-start | bytes 811016 | tf_op jit(solution)/shard_map/ppermute | solution.py:38
  49.9 24.6 %collective-permute-start.8 = (bf16[2,48,1792]{2,1,0:T(8,128)(2,1)S(1)}, bf16[2,48,1792]{2,1,0:T(8,128)(2,1)S(1)}, u32[]{:S(2)}, u32[]{:S(2)}) collective-permute-start(bf16[2,48,1792]{2,1,0:T(8,128)(2,1)S(1)} %pad_maximum_fusion.3), channel_id=1, source_target_pairs={{0,2},{1,3},{2,4},{3,5},{4,6},{5,7},{6,0},{7,1},{8,10},{9,11},{10,... | collective-permute-start | bytes 1032200 | tf_op jit(solution)/shard_map/ppermute | solution.py:38
  52.7 42.2 %collective-permute-start.9 = (bf16[2,48,1792]{2,1,0:T(8,128)(2,1)S(1)}, bf16[2,48,1792]{2,1,0:T(8,128)(2,1)S(1)}, u32[]{:S(2)}, u32[]{:S(2)}) collective-permute-start(bf16[2,48,1792]{2,1,0:T(8,128)(2,1)S(1)} %pad_maximum_fusion.4), channel_id=1, source_target_pairs={{0,4},{1,5},{2,6},{3,7},{4,0},{5,1},{6,2},{7,3},{8,12},{9,13},{10,... | collective-permute-start | bytes 1032200 | tf_op jit(solution)/shard_map/ppermute | solution.py:38
  55.6 39.3 %collective-permute-start.10 = (bf16[2,48,1792]{2,1,0:T(8,128)(2,1)S(1)}, bf16[2,48,1792]{2,1,0:T(8,128)(2,1)S(1)}, u32[]{:S(2)}, u32[]{:S(2)}) collective-permute-start(bf16[2,48,1792]{2,1,0:T(8,128)(2,1)S(1)} %pad_maximum_fusion.5), channel_id=1, source_target_pairs={{0,6},{1,7},{2,0},{3,1},{4,2},{5,3},{6,4},{7,5},{8,14},{9,15},{10,... | collective-permute-start | bytes 1032200 | tf_op jit(solution)/shard_map/ppermute | solution.py:38
  105.4 9.6 %slice-start = ((s8[11534336]{0:T(1024)(128)(4,1)}), s8[4194304]{0:T(1024)(128)(4,1)S(1)}, s32[]{:S(2)}) async-start(s8[11534336]{0:T(1024)(128)(4,1)} %bitcast.165), calls=%async_computation | async-start | bytes 8388608
  105.4 9.6 %slice-start.1 = ((s8[11534336]{0:T(1024)(128)(4,1)}), s8[4194304]{0:T(1024)(128)(4,1)S(1)}, s32[]{:S(2)}) async-start(s8[11534336]{0:T(1024)(128)(4,1)} %bitcast.165), calls=%async_computation.1 | async-start | bytes 8388608
  110.2 4.8 %slice-start.2 = ((s8[11534336]{0:T(1024)(128)(4,1)}), s8[3145728]{0:T(1024)(128)(4,1)S(1)}, s32[]{:S(2)}) async-start(s8[11534336]{0:T(1024)(128)(4,1)} %bitcast.165), calls=%async_computation.2 | async-start | bytes 6291456
  118.2 7.7 %collective-permute-start.15 = (bf16[4,48,2048]{2,1,0:T(8,128)(2,1)S(1)}, bf16[4,48,2048]{2,1,0:T(8,128)(2,1)S(1)}, u32[]{:S(2)}, u32[]{:S(2)}) collective-permute-start(bf16[4,48,2048]{2,1,0:T(8,128)(2,1)S(1)} %bitcast.152), channel_id=1, source_target_pairs={{0,1},{1,0},{2,3},{3,2},{4,5},{5,4},{6,7},{7,6},{8,9},{9,8},{10,11... | collective-permute-start | bytes 2359304 | tf_op jit(solution)/shard_map/ppermute | solution.py:42
  121.4 10.1 %collective-permute-start.20 = (bf16[4,48,2048]{2,1,0:T(8,128)(2,1)S(1)}, bf16[4,48,2048]{2,1,0:T(8,128)(2,1)S(1)}, u32[]{:S(2)}, u32[]{:S(2)}) collective-permute-start(bf16[4,48,2048]{2,1,0:T(8,128)(2,1)S(1)} %bitcast.151), channel_id=1, source_target_pairs={{0,1},{1,0},{2,3},{3,2},{4,5},{5,4},{6,7},{7,6},{8,9},{9,8},{10,11... | collective-permute-start | bytes 2359304 | tf_op jit(solution)/shard_map/ppermute | solution.py:42
  126.3 8.7 %collective-permute-start.16 = (bf16[48,2048]{1,0:T(8,128)(2,1)S(1)}, bf16[48,2048]{1,0:T(8,128)(2,1)S(1)}, u32[]{:S(2)}, u32[]{:S(2)}) collective-permute-start(bf16[48,2048]{1,0:T(8,128)(2,1)S(1)} %get-tuple-element.26), channel_id=1, source_target_pairs={{8,0},{9,1},{10,2},{11,3},{12,4},{13,5},{14,6},{15,7},{16,8},{17,9... | collective-permute-start | bytes 589832 | tf_op jit(solution)/shard_map/ppermute | solution.py:52
  127.6 16.7 %collective-permute-start.17 = (bf16[48,2048]{1,0:T(8,128)(2,1)S(1)}, bf16[48,2048]{1,0:T(8,128)(2,1)S(1)}, u32[]{:S(2)}, u32[]{:S(2)}) collective-permute-start(bf16[48,2048]{1,0:T(8,128)(2,1)S(1)} %get-tuple-element.29), channel_id=1, source_target_pairs={{8,6},{9,7},{10,0},{11,1},{12,2},{13,3},{14,4},{15,5},{16,14},{17,... | collective-permute-start | bytes 589832 | tf_op jit(solution)/shard_map/ppermute | solution.py:52
  128.9 28.4 %collective-permute-start.18 = (bf16[48,2048]{1,0:T(8,128)(2,1)S(1)}, bf16[48,2048]{1,0:T(8,128)(2,1)S(1)}, u32[]{:S(2)}, u32[]{:S(2)}) collective-permute-start(bf16[48,2048]{1,0:T(8,128)(2,1)S(1)} %get-tuple-element.28), channel_id=1, source_target_pairs={{8,4},{9,5},{10,6},{11,7},{12,0},{13,1},{14,2},{15,3},{16,12},{17,... | collective-permute-start | bytes 589832 | tf_op jit(solution)/shard_map/ppermute | solution.py:52
  130.2 28.4 %collective-permute-start.19 = (bf16[48,2048]{1,0:T(8,128)(2,1)S(1)}, bf16[48,2048]{1,0:T(8,128)(2,1)S(1)}, u32[]{:S(2)}, u32[]{:S(2)}) collective-permute-start(bf16[48,2048]{1,0:T(8,128)(2,1)S(1)} %get-tuple-element.27), channel_id=1, source_target_pairs={{8,2},{9,3},{10,4},{11,5},{12,6},{13,7},{14,0},{15,1},{16,10},{17,... | collective-permute-start | bytes 589832 | tf_op jit(solution)/shard_map/ppermute | solution.py:52
  131.5 46.1 %copy-start.1 = (s32[1,16]{1,0:T(1,128)S(1)}, s32[1,16]{1,0:T(1,128)}, u32[]{:S(2)}) copy-start(s32[1,16]{1,0:T(1,128)} %param.19) | copy-start | bytes 196
  131.8 26.8 %collective-permute-start.21 = (bf16[48,2048]{1,0:T(8,128)(2,1)S(1)}, bf16[48,2048]{1,0:T(8,128)(2,1)S(1)}, u32[]{:S(2)}, u32[]{:S(2)}) collective-permute-start(bf16[48,2048]{1,0:T(8,128)(2,1)S(1)} %get-tuple-element.30), channel_id=1, source_target_pairs={{8,0},{9,1},{10,2},{11,3},{12,4},{13,5},{14,6},{15,7},{16,8},{17,9... | collective-permute-start | bytes 589832 | tf_op jit(solution)/shard_map/ppermute | solution.py:52
  135.0 29.0 %collective-permute-start.22 = (bf16[48,2048]{1,0:T(8,128)(2,1)S(1)}, bf16[48,2048]{1,0:T(8,128)(2,1)S(1)}, u32[]{:S(2)}, u32[]{:S(2)}) collective-permute-start(bf16[48,2048]{1,0:T(8,128)(2,1)S(1)} %get-tuple-element.33), channel_id=1, source_target_pairs={{8,6},{9,7},{10,0},{11,1},{12,2},{13,3},{14,4},{15,5},{16,14},{17,... | collective-permute-start | bytes 589832 | tf_op jit(solution)/shard_map/ppermute | solution.py:52
  144.3 32.4 %collective-permute-start.23 = (bf16[48,2048]{1,0:T(8,128)(2,1)S(1)}, bf16[48,2048]{1,0:T(8,128)(2,1)S(1)}, u32[]{:S(2)}, u32[]{:S(2)}) collective-permute-start(bf16[48,2048]{1,0:T(8,128)(2,1)S(1)} %get-tuple-element.32), channel_id=1, source_target_pairs={{8,4},{9,5},{10,6},{11,7},{12,0},{13,1},{14,2},{15,3},{16,12},{17,... | collective-permute-start | bytes 589832 | tf_op jit(solution)/shard_map/ppermute | solution.py:52
  157.2 19.5 %collective-permute-start.24 = (bf16[48,2048]{1,0:T(8,128)(2,1)S(1)}, bf16[48,2048]{1,0:T(8,128)(2,1)S(1)}, u32[]{:S(2)}, u32[]{:S(2)}) collective-permute-start(bf16[48,2048]{1,0:T(8,128)(2,1)S(1)} %get-tuple-element.31), channel_id=1, source_target_pairs={{8,2},{9,3},{10,4},{11,5},{12,6},{13,7},{14,0},{15,1},{16,10},{17,... | collective-permute-start | bytes 589832 | tf_op jit(solution)/shard_map/ppermute | solution.py:52
  (5 other events, 9.5 us)

commit v2 on v1

v2 whole, which is shorter than its diff:
```python
import functools

import jax
import jax.numpy as jnp
from jax import lax
from jax.experimental import pallas as pl
from jax.experimental.pallas import tpu as pltpu
from jax.sharding import PartitionSpec as P

CAP = 3
LANES = 128
VMEM = 40 * 1024 * 1024
COST = pl.CostEstimate(flops=0, bytes_accessed=0, transcendentals=0)


def gelu(values):
    coeff = 0.7978845608
    tangent = jnp.tanh(coeff * (values + 0.044715 * (values * values * values)))
    return 0.5 * values * (1.0 + tangent)


def gelu_pair(values):
    coeff = 0.7978845608
    square = values * values
    tangent = jnp.tanh(coeff * (values + 0.044715 * (square * values)))
    activated = 0.5 * values * (1.0 + tangent)
    slope = 0.5 * (1.0 + tangent) + 0.5 * values * (1.0 - tangent * tangent) * coeff * (
        1.0 + 3.0 * 0.044715 * square
    )
    return activated, slope


def rotated(value, by):
    devices = lax.axis_size("dp")
    pairs = [(i, (i + 2 * by) % devices) for i in range(devices)]
    return lax.ppermute(value, "dp", pairs)


def swapped(value):
    return lax.ppermute(value, "dp", [(i, i ^ 1) for i in range(lax.axis_size("dp"))])


def relayed(value, by):
    devices, sections = lax.axis_size("dp"), lax.axis_size("section")
    pairs = [
        (s * devices + i, (s - 1) * devices + (i - 2 * by) % devices)
        for s in range(1, sections)
        for i in range(devices)
    ]
    return lax.ppermute(value, ("section", "dp"), pairs)


def after(value, *earlier):
    return lax.optimization_barrier((value,) + earlier)[0]


def hidden_kernel(rows_ref, owner_ref, gate_ref, up_ref, out_ref, count_ref):
    out_ref[...] = jnp.zeros_like(out_ref)
    for replica in range(count_ref.shape[0]):
        count_ref[replica] = 0

    def block(i, carry):
        replica = owner_ref[i]
        slot = count_ref[replica]
        count_ref[replica] = slot + 1
        part = pl.ds(pl.multiple_of(rows_ref[i] * LANES, LANES), LANES)
        value = gelu(gate_ref[:, part].astype(jnp.float32)) * up_ref[:, part].astype(jnp.float32)
        place = pl.ds(pl.multiple_of((replica * CAP + slot) * LANES, LANES), LANES)
        out_ref[:, place] = value.astype(jnp.bfloat16)
        return carry

    lax.fori_loop(0, rows_ref.shape[0], block, 0)


def hidden_blocks(rows, owner, gate, up, replicas):
    tokens = gate.shape[0]
    return pl.pallas_call(
        hidden_kernel,
        in_specs=[pl.BlockSpec(memory_space=pltpu.SMEM)] * 2 + [pl.BlockSpec(memory_space=pltpu.VMEM)] * 2,
        out_specs=pl.BlockSpec(memory_space=pltpu.VMEM),
        out_shape=jax.ShapeDtypeStruct((tokens, replicas * CAP * LANES), jnp.bfloat16),
        scratch_shapes=[pltpu.SMEM((replicas,), jnp.int32)],
        compiler_params=pltpu.CompilerParams(vmem_limit_bytes=VMEM),
        cost_estimate=COST,
        name="hidden_blocks",
    )(rows, owner, gate, up)


def hidden_grad_kernel(*refs):
    grads, (w_ref, out_ref, sum_ref) = refs[:-3], refs[-3:]
    rows = grads[0].shape[0]
    step = pl.program_id(0)
    value = lax.dot_general(
        jnp.concatenate([ref[...] for ref in grads], axis=0),
        w_ref[...],
        (((1,), (1,)), ((), ())),
        preferred_element_type=jnp.float32,
    )

    @pl.when(step == 0)
    def _():
        sum_ref[...] = value

    @pl.when(step > 0)
    def _():
        sum_ref[...] += value

    @pl.when(step == pl.num_programs(0) - 1)
    def _():
        out_ref[...] = sum_ref[...].astype(jnp.bfloat16)


def hidden_grad(grads, weight):
    rows, width = grads[0].shape
    units = weight.shape[0]
    tile = 4 * LANES
    out = (len(grads) * rows, units)
    return pl.pallas_call(
        hidden_grad_kernel,
        grid=(width // tile,),
        in_specs=[pl.BlockSpec((rows, tile), lambda i: (0, i))] * len(grads)
        + [pl.BlockSpec((units, tile), lambda i: (0, i))],
        out_specs=pl.BlockSpec(out, lambda i: (0, 0)),
        out_shape=jax.ShapeDtypeStruct(out, jnp.bfloat16),
        scratch_shapes=[pltpu.VMEM(out, jnp.float32)],
        compiler_params=pltpu.CompilerParams(vmem_limit_bytes=VMEM),
        cost_estimate=COST,
        name="hidden_grad",
    )(*grads, weight)


def gradients_kernel(dh_ref, *refs):
    given, (lg_ref, lu_ref) = refs[:-2], refs[-2:]
    units = dh_ref.shape[1]
    rows = given[0].shape[1]
    skip = CAP * LANES
    padded = (given[0].shape[2] - skip) // 2
    for f in range(2):
        for p, ref in enumerate(given):
            part = slice((f * len(given) + p) * rows, (f * len(given) + p + 1) * rows)
            wide = dh_ref[part, :].astype(jnp.float32)
            gate = ref[f, :, skip : skip + units].astype(jnp.float32)
            up = ref[f, :, skip + padded : skip + padded + units].astype(jnp.float32)
            activated, slope = gelu_pair(gate)
            lg_ref[part, :] = (wide * up * slope).astype(jnp.bfloat16)
            lu_ref[part, :] = (wide * activated).astype(jnp.bfloat16)


def local_gradients(dhidden, given):
    out = jax.ShapeDtypeStruct(dhidden.shape, jnp.bfloat16)
    return pl.pallas_call(
        gradients_kernel,
        in_specs=[pl.BlockSpec(memory_space=pltpu.VMEM)] * (1 + len(given)),
        out_specs=[pl.BlockSpec(memory_space=pltpu.VMEM)] * 2,
        out_shape=[out, out],
        compiler_params=pltpu.CompilerParams(vmem_limit_bytes=VMEM),
        cost_estimate=COST,
        name="local_gradients",
    )(dhidden, *given)


def term_kernel(lg_ref, lu_ref, wg_ref, wu_ref, same_ref, other_ref):
    term = jnp.dot(lg_ref[...], wg_ref[...], preferred_element_type=jnp.float32)
    term += jnp.dot(lu_ref[...], wu_ref[...], preferred_element_type=jnp.float32)
    term = term.astype(jnp.bfloat16).reshape(2, *same_ref.shape)
    same_ref[...] = term[0]
    other_ref[...] = term[1]


def terms(local_gate, local_up, w_gate, w_up, chips, first, width):
    rows, units = local_gate.shape
    tile = 4 * LANES
    out = (chips, rows // (2 * chips))
    return pl.pallas_call(
        term_kernel,
        grid=(width // tile,),
        in_specs=[pl.BlockSpec((rows, units), lambda i: (0, 0))] * 2
        + [pl.BlockSpec((units, tile), lambda i: (0, i + first // tile))] * 2,
        out_specs=[pl.BlockSpec(out + (tile,), lambda i: (0, 0, i))] * 2,
        out_shape=[jax.ShapeDtypeStruct(out + (width,), jnp.bfloat16)] * 2,
        compiler_params=pltpu.CompilerParams(vmem_limit_bytes=VMEM),
        cost_estimate=COST,
        name="terms",
    )(local_gate, local_up, w_gate, w_up)


def block_kernel(scale, cols_ref, *refs):
    out_ref = refs[-1]
    refs = refs[:-1]
    grads, hidden = refs[: len(refs) * 2 // 3], refs[len(refs) * 2 // 3 :]
    left = jnp.concatenate([ref[f] for ref in hidden for f in range(2)], axis=0)
    right = jnp.concatenate([ref[...] for ref in grads], axis=0)
    value = lax.dot_general(left, right, (((0,), (0,)), ((), ())), preferred_element_type=jnp.float32)
    out_ref[0] = (value * scale).astype(jnp.bfloat16)


def block_sums(cols, grads, hidden, scale):
    rows = grads[0].shape[0]
    return pl.pallas_call(
        functools.partial(block_kernel, scale),
        grid_spec=pltpu.PrefetchScalarGridSpec(
            num_scalar_prefetch=1,
            grid=(CAP,),
            in_specs=[pl.BlockSpec((rows, LANES), lambda k, cols_ref: (0, cols_ref[k]))] * len(grads)
            + [pl.BlockSpec((2, rows, LANES), lambda k, cols_ref: (0, 0, k))] * len(hidden),
            out_specs=pl.BlockSpec((1, LANES, LANES), lambda k, cols_ref: (k, 0, 0)),
        ),
        out_shape=jax.ShapeDtypeStruct((CAP, LANES, LANES), jnp.bfloat16),
        compiler_params=pltpu.CompilerParams(vmem_limit_bytes=VMEM),
        cost_estimate=COST,
        name="block_sums",
    )(cols, *grads, *hidden)


def summed(*values):
    total = values[0].astype(jnp.float32)
    for value in values[1:]:
        total = total + value.astype(jnp.float32)
    return total.astype(jnp.bfloat16)


def own_columns(rows_owner, cols, me):
    blocks = jnp.arange(cols.shape[0], dtype=jnp.int32)
    own = rows_owner == me
    earlier = own[None, :] & (blocks[None, :] < blocks[:, None])
    slots = jnp.sum(earlier.astype(jnp.int32), axis=1)
    hit = own[None, :] & (slots[None, :] == jnp.arange(CAP, dtype=jnp.int32)[:, None])
    return jnp.sum(jnp.where(hit, cols[None, :], 0), axis=1)


def shards(d_out, down_weight, gate_weight, up_weight, gate_pre, up_val, rows, cols, owner):
    mine = d_out[0]
    w_down, w_gate, w_up = down_weight[0], gate_weight[0], up_weight[0]
    gate, up = gate_pre[0], up_val[0]
    tokens = mine.shape[0]
    units = w_down.shape[0]
    replicas = lax.axis_size("dp")
    chips = replicas // 2
    me = lax.axis_index("dp")
    chip, core = me // 2, me % 2

    same = [mine] + [None] * (chips - 1)
    same[1] = rotated(mine, 1)
    if chips > 2:
        same[chips - 1] = rotated(mine, -1)
    for r in range(2, chips - 1):
        same[r] = rotated(same[r - 1], 1)

    slots = hidden_blocks(rows[0], owner[0], gate, up, replicas)
    fill = jnp.zeros((tokens, -units % LANES), jnp.bfloat16)

    def held(replica):
        parts = [lax.dynamic_slice_in_dim(slots, replica * CAP * LANES, CAP * LANES, 1)]
        for values in (gate, up):
            parts += [lax.dynamic_slice_in_dim(values, replica * units, units, 1), fill]
        return jnp.concatenate(parts, axis=1)

    def ahead(r, other):
        return 2 * ((chip + r) % chips) + (1 - core if other else core)

    taken = swapped(jnp.stack([held(ahead(r, True)) for r in range(chips)]))
    order = [0] + list(range(chips - 2, 0, -1)) + ([chips - 1] if chips > 2 else [])
    sent = {r: jnp.stack([held(ahead(r, False)), taken[r]]) for r in order}
    given = {r: rotated(after(sent[r], same[1], same[chips - 1]), r) if r else sent[r] for r in order}

    other = {r: swapped(same[r]) for r in order}
    grads = [part[r] for part in (same, other) for r in order]
    dhidden = hidden_grad([after(grads[0], *sent.values())] + grads[1:], w_down)
    local_gate, local_up = local_gradients(dhidden, [given[r] for r in order])

    parts = 2
    width = mine.shape[1] // parts
    pieces, earlier = [], []
    for part in range(parts):
        last = part == parts - 1
        kept, passed = terms(local_gate, local_up, w_gate, w_up, chips, part * width, width)
        passed = swapped(after(passed, *earlier) if earlier else passed)
        sums = {r: summed(kept[i], passed[i]) for i, r in enumerate(order)}
        step = relayed if last else lambda value, by: rotated(value, -by)
        total, running = [relayed(sums[0], 0) if last else sums[0]], None
        if chips > 1:
            total.append(step(sums[chips - 1], chips - 1))
        earlier = total[1:]
        for r in range(chips - 2, 0, -1):
            value = sums[r] if running is None else summed(sums[r], running)
            if r == 1:
                total.append(step(value, 1))
            else:
                running = rotated(value, -1)
                if len(earlier) < 2:
                    earlier.append(running)
        pieces.append(summed(*total) if last else relayed(summed(*total), 0))
    grad_input = jnp.concatenate(pieces, axis=1)

    block_grads = block_sums(
        after(own_columns(owner[0], cols[0], me), *sums.values()),
        [part[r] for r in order for part in (same, other)],
        [given[r] for r in order],
        1.0 / replicas,
    )
    return (grad_input[None], block_grads[None])


def solution(mesh):
    return jax.shard_map(
        shards,
        mesh=mesh,
        in_specs=(P("section", "dp", None),) * 6 + (P("section", None),) * 3,
        out_specs=(P("section", "dp", None), P("section", "dp", None, None)),
        check_vma=False,
    )
```

time: 178 us -> 140 us (0.79)
  Pallas kernels: 0 us -> 32.3 us
  matrix products: 29.1 us -> 0 us
  local copies, waits for them, and re-layouts: 21.9 us -> 4.28 us
  waiting for transfers between devices: 79.3 us -> 67.5 us
  other arithmetic: 8.96 us -> 2.23 us
  between operations: 3.42 us -> 0.91 us
  starting transfers between devices: 34.9 us -> 32.7 us
    pallas_call x0 -> x6, Pallas kernels: none -> 32.3 us  [the longest x2 15.9 us: terms(): pl.pallas_call(term_kernel, grid=(width // tile,), in_specs=[pl.BlockSpec...]
    ppermute x8 -> x4, waiting for transfers between devices: 39.6 us -> 9.31 us  [relayed(): return lax.ppermute(value, ('section', 'dp'), pairs)]
    dot_general x8 -> x0, matrix products: 29.1 us -> none  [the longest x1 10.4 us: shards(): lax.dot_general(grads, w_down, (((1,), (1,)), ((), ())), preferred_elemen...]
    ppermute x9 -> x10, waiting for transfers between devices: 39.7 us -> 52.2 us  [rotated(): return lax.ppermute(value, 'dp', pairs)]
    unnamed x37 -> x14, local copies, waits for them, and re-layouts: 13 us -> 3.8 us
    ppermute x8 -> x7, waiting for transfers between devices: 0.02 us -> 5.95 us  [swapped(): lax.ppermute(value, 'dp', [(i, i ^ 1) for i in range(lax.axis_size('dp'))])]
    ppermute x8 -> x4, starting transfers between devices: 10.3 us -> 5.16 us  [relayed(): return lax.ppermute(value, ('section', 'dp'), pairs)]
    ppermute x9 -> x10, starting transfers between devices: 22.8 us -> 26.6 us  [rotated(): return lax.ppermute(value, 'dp', pairs)]
  transfers between devices with their start and end apart: 25 -> 21, of which waited for: 10 -> 13; matrix products, arithmetic and copies ran while one was open for 20% -> 1% of each run, Pallas kernels for 0% -> 16%
where the time goes in v2:
time: 140 us
  waiting for transfers between devices  67.5 us (48%)
  starting transfers between devices  32.7 us (23%)
  Pallas kernels  32.3 us (23%)
  local copies, waits for them, and re-layouts  4.28 us (3%)
  other arithmetic  2.23 us (2%)
    ppermute x10, waiting for transfers between devices, rotated(): return lax.ppermute(value, 'dp', pairs)  52.2 us
    ppermute x10, starting transfers between devices, rotated(): return lax.ppermute(value, 'dp', pairs)  26.6 us
    pallas_call x2, Pallas kernels, terms(): pl.pallas_call(term_kernel, grid=(width // tile,), in_specs=[pl.BlockSpec...  15.9 us
    pallas_call x1, Pallas kernels, hidden_grad(): pl.pallas_call(hidden_grad_kernel, grid=(width // tile,), in_specs=[pl.Bl...  11 us
    ppermute x4, waiting for transfers between devices, relayed(): return lax.ppermute(value, ('section', 'dp'), pairs)  9.31 us
    ppermute x7, waiting for transfers between devices, swapped(): lax.ppermute(value, 'dp', [(i, i ^ 1) for i in range(lax.axis_size('dp'))])  5.95 us
    ppermute x4, starting transfers between devices, relayed(): return lax.ppermute(value, ('section', 'dp'), pairs)  5.16 us
    unnamed x14, local copies, waits for them, and re-layouts  3.8 us
  transfers between devices with their start and end apart: 21, of which 13 were waited for; matrix products, arithmetic and copies ran while one was open for 1% of the time, Pallas kernels for 16%

profile of v2, /device:TPU:0, one launch (start us, length us, event | category | flops | bytes accessed | tf_op | source)
XLA Modules:
  0.0 139.9 jit_solution(14294047219893107248)
XLA Ops:
  1.1 4.7 %collective-permute-start.3 = (bf16[48,4096]{1,0:T(8,128)(2,1)}, bf16[48,4096]{1,0:T(8,128)(2,1)S(1)}, u32[]{:S(2)}, u32[]{:S(2)}) collective-permute-start(bf16[48,4096]{1,0:T(8,128)(2,1)} %bitcast.88), channel_id=1, source_target_pairs={{0,6},{1,7},{2,0},{3,1},{4,2},{5,3},{6,4},{7,5},{8,14},{9,15},{10,... | collective-permute-start | bytes 1179656 | tf_op jit(solution)/shard_map/ppermute | solution.py:36
  5.8 1.2 copy-done
  7.1 1.2 copy-done.1
  9.6 0.9 hidden_blocks.1
  11.6 4.0 %collective-permute-done.3.refs_3_.refs_6_ = bf16[48,4096]{1,0:T(8,128)(2,1)S(1)} collective-permute-done((bf16[48,4096]{1,0:T(8,128)(2,1)}, bf16[48,4096]{1,0:T(8,128)(2,1)S(1)}, u32[]{:S(2)}, u32[]{:S(2)}) %collective-permute-start.3) | collective-permute-done | bytes 393248 | tf_op jit(solution)/shard_map/ppermute | solution.py:36
  15.6 8.7 %collective-permute-done.1.refs_2_.refs_4_ = bf16[48,4096]{1,0:T(8,128)(2,1)S(1)} collective-permute-done((bf16[48,4096]{1,0:T(8,128)(2,1)}, bf16[48,4096]{1,0:T(8,128)(2,1)S(1)}, u32[]{:S(2)}, u32[]{:S(2)}) %collective-permute-start.1) | collective-permute-done | bytes 393248 | tf_op jit(solution)/shard_map/ppermute | solution.py:36
  24.3 1.6 %collective-permute-start.2 = (bf16[48,4096]{1,0:T(8,128)(2,1)S(1)}, bf16[48,4096]{1,0:T(8,128)(2,1)S(1)}, u32[]{:S(2)}, u32[]{:S(2)}) collective-permute-start(bf16[48,4096]{1,0:T(8,128)(2,1)S(1)} %collective-permute-done.1.refs_2_.refs_4_), channel_id=1, source_target_pairs={{0,2},{1,3},{2,4},{3,5},{4,6},{5,7},{6,0},{7,1},{8,10},{9,11},{10,... | collective-permute-start | bytes 1179656 | tf_op jit(solution)/shard_map/ppermute | solution.py:36
  27.0 2.1 %collective-permute-start.9 = (bf16[2,48,3200]{2,1,0:T(8,128)(2,1)S(1)}, bf16[2,48,3200]{2,1,0:T(8,128)(2,1)S(1)}, u32[]{:S(2)}, u32[]{:S(2)}) collective-permute-start(bf16[2,48,3200]{2,1,0:T(8,128)(2,1)S(1)} %pad_maximum_fusion.3), channel_id=1, source_target_pairs={{0,2},{1,3},{2,4},{3,5},{4,6},{5,7},{6,0},{7,1},{8,10},{9,11},{10,... | collective-permute-start | bytes 1843208 | tf_op jit(solution)/shard_map/ppermute | solution.py:36
  29.1 1.7 %collective-permute-start.10 = (bf16[2,48,3200]{2,1,0:T(8,128)(2,1)S(1)}, bf16[2,48,3200]{2,1,0:T(8,128)(2,1)S(1)}, u32[]{:S(2)}, u32[]{:S(2)}) collective-permute-start(bf16[2,48,3200]{2,1,0:T(8,128)(2,1)S(1)} %pad_maximum_fusion.4), channel_id=1, source_target_pairs={{0,6},{1,7},{2,0},{3,1},{4,2},{5,3},{6,4},{7,5},{8,14},{9,15},{10,... | collective-permute-start | bytes 1843208 | tf_op jit(solution)/shard_map/ppermute | solution.py:36
  31.0 7.3 %collective-permute-done.2.refs_1_.refs_2_ = bf16[48,4096]{1,0:T(8,128)(2,1)S(1)} collective-permute-done((bf16[48,4096]{1,0:T(8,128)(2,1)S(1)}, bf16[48,4096]{1,0:T(8,128)(2,1)S(1)}, u32[]{:S(2)}, u32[]{:S(2)}) %collective-permute-start.2) | collective-permute-done | bytes 393248 | tf_op jit(solution)/shard_map/ppermute | solution.py:36
  38.4 1.6 %collective-permute-done.5.refs_5_.refs_3_ = bf16[48,4096]{1,0:T(8,128)(2,1)S(1)} collective-permute-done((bf16[48,4096]{1,0:T(8,128)(2,1)S(1)}, bf16[48,4096]{1,0:T(8,128)(2,1)S(1)}, u32[]{:S(2)}, u32[]{:S(2)}) %collective-permute-start.5) | collective-permute-done | bytes 393248 | tf_op jit(solution)/shard_map/ppermute | solution.py:40
  40.0 11.0 %hidden_grad.1.dh_ref = bf16[384,1408]{1,0:T(8,128)(2,1)S(1)} custom-call(bf16[48,4096]{1,0:T(8,128)(2,1)S(1)} %bitcast.90, bf16[48,4096]{1,0:T(8,128)(2,1)S(1)} %collective-permute-done.2.refs_1_.refs_2_, bf16[48,4096]{1,0:T(8,128)(2,1)S(1)} %collective-permute-done.1.refs_2_.refs_4_, bf16[48,4096]{1,0:T(8,128)(2,1)S(1)} %collective-permute-done.3.refs_3_.refs_6_, ...), custom_call_target="tpu_custom_call" | custom-call | tf_op jit(solution)/shard_map/hidden_grad/pallas_call | solution.py:118
  51.0 25.4 %collective-permute-done.8.refs_1_.refs_9_ = bf16[2,48,3200]{2,1,0:T(8,128)(2,1)S(1)} collective-permute-done((bf16[2,48,3200]{2,1,0:T(8,128)(2,1)S(1)}, bf16[2,48,3200]{2,1,0:T(8,128)(2,1)S(1)}, u32[]{:S(2)}, u32[]{:S(2)}) %collective-permute-start.8) | collective-permute-done | bytes 614432 | tf_op jit(solution)/shard_map/ppermute | solution.py:36
  76.4 2.0 %local_gradients.1 = (bf16[384,1408]{1,0:T(8,128)(2,1)S(1)}, bf16[384,1408]{1,0:T(8,128)(2,1)S(1)}) custom-call(bf16[384,1408]{1,0:T(8,128)(2,1)S(1)} %hidden_grad.1.dh_ref, bf16[2,48,3200]{2,1,0:T(8,128)(2,1)S(1)} %pad_maximum_fusion.1.refs_0_.refs_8_, bf16[2,48,3200]{2,1,0:T(8,128)(2,1)S(1)} %collective-permute-done.8.refs_1_.refs_9_, ...), custom_call_target="tpu_custom_call" | custom-call | tf_op jit(solution)/shard_map/local_gradients/pallas_call | solution.py:151
  78.4 7.9 %terms.2 = (bf16[4,48,2048]{2,1,0:T(8,128)(2,1)S(1)}, bf16[4,48,2048]{2,1,0:T(8,128)(2,1)S(1)}) custom-call(bf16[384,1408]{1,0:T(8,128)(2,1)S(1)} %get-tuple-element.18.lg_ref, bf16[384,1408]{1,0:T(8,128)(2,1)S(1)} %get-tuple-element.19.lu_ref, bf16[1408,4096]{1,0:T(8,128)(2,1)} %bitcast.94, bf16[1408,4096]{1,0:T(8,128)(2,1)} %bitcast.96), custom_call_target="tpu_custom_call" | custom-call | tf_op jit(solution)/shard_map/terms/pallas_call | solution.py:174
  86.5 2.3 %collective-permute-done.11 = bf16[4,48,2048]{2,1,0:T(8,128)(2,1)S(1)} collective-permute-done((bf16[4,48,2048]{2,1,0:T(8,128)(2,1)S(1)}, bf16[4,48,2048]{2,1,0:T(8,128)(2,1)S(1)}, u32[]{:S(2)}, u32[]{:S(2)}) %collective-permute-start.11) | collective-permute-done | bytes 786464 | tf_op jit(solution)/shard_map/ppermute | solution.py:40
  88.9 1.7 %collective-permute-start.13 = (bf16[48,2048]{1,0:T(8,128)(2,1)S(1)}, bf16[48,2048]{1,0:T(8,128)(2,1)S(1)}, u32[]{:S(2)}, u32[]{:S(2)}) collective-permute-start(bf16[48,2048]{1,0:T(8,128)(2,1)S(1)} %get-tuple-element.31), channel_id=1, source_target_pairs={{0,6},{1,7},{2,0},{3,1},{4,2},{5,3},{6,4},{7,5},{8,14},{9,15},{10,... | collective-permute-start | bytes 589832 | tf_op jit(solution)/shard_map/ppermute | solution.py:36
  90.5 12.1 %collective-permute-start.12 = (bf16[48,2048]{1,0:T(8,128)(2,1)S(1)}, bf16[48,2048]{1,0:T(8,128)(2,1)S(1)}, u32[]{:S(2)}, u32[]{:S(2)}) collective-permute-start(bf16[48,2048]{1,0:T(8,128)(2,1)S(1)} %get-tuple-element.32), channel_id=1, source_target_pairs={{0,2},{1,3},{2,4},{3,5},{4,6},{5,7},{6,0},{7,1},{8,10},{9,11},{10,... | collective-permute-start | bytes 589832 | tf_op jit(solution)/shard_map/ppermute | solution.py:36
  102.6 8.0 %terms.3 = (bf16[4,48,2048]{2,1,0:T(8,128)(2,1)S(1)}, bf16[4,48,2048]{2,1,0:T(8,128)(2,1)S(1)}) custom-call(bf16[384,1408]{1,0:T(8,128)(2,1)S(1)} %get-tuple-element.18.lg_ref, bf16[384,1408]{1,0:T(8,128)(2,1)S(1)} %get-tuple-element.19.lu_ref, bf16[1408,4096]{1,0:T(8,128)(2,1)} %bitcast.95, bf16[1408,4096]{1,0:T(8,128)(2,1)} %bitcast.97), custom_call_target="tpu_custom_call" | custom-call | tf_op jit(solution)/shard_map/terms/pallas_call | solution.py:174
  110.6 1.6 %collective-permute-done.12 = bf16[48,2048]{1,0:T(8,128)(2,1)S(1)} collective-permute-done((bf16[48,2048]{1,0:T(8,128)(2,1)S(1)}, bf16[48,2048]{1,0:T(8,128)(2,1)S(1)}, u32[]{:S(2)}, u32[]{:S(2)}) %collective-permute-start.12) | collective-permute-done | bytes 196640 | tf_op jit(solution)/shard_map/ppermute | solution.py:36
  112.5 2.0 %collective-permute-done.16 = bf16[4,48,2048]{2,1,0:T(8,128)(2,1)S(1)} collective-permute-done((bf16[4,48,2048]{2,1,0:T(8,128)(2,1)S(1)}, bf16[4,48,2048]{2,1,0:T(8,128)(2,1)S(1)}, u32[]{:S(2)}, u32[]{:S(2)}) %collective-permute-start.16) | collective-permute-done | bytes 786464 | tf_op jit(solution)/shard_map/ppermute | solution.py:40
  114.8 2.0 %collective-permute-start.14 = (bf16[48,2048]{1,0:T(8,128)(2,1)S(1)}, bf16[48,2048]{1,0:T(8,128)(2,1)S(1)}, u32[]{:S(2)}, u32[]{:S(2)}) collective-permute-start(bf16[48,2048]{1,0:T(8,128)(2,1)S(1)} %fusion), channel_id=1, source_target_pairs={{0,6},{1,7},{2,0},{3,1},{4,2},{5,3},{6,4},{7,5},{8,14},{9,15},{10,... | collective-permute-start | bytes 589832 | tf_op jit(solution)/shard_map/ppermute | solution.py:36
  116.8 1.3 collective-permute-start.17
  118.0 1.3 collective-permute-start.18
  119.3 3.1 %collective-permute-done.19 = bf16[48,2048]{1,0:T(8,128)(2,1)S(1)} collective-permute-done((bf16[48,2048]{1,0:T(8,128)(2,1)S(1)}, bf16[48,2048]{1,0:T(8,128)(2,1)S(1)}, u32[]{:S(2)}, u32[]{:S(2)}) %collective-permute-start.19) | collective-permute-done | bytes 196640 | tf_op jit(solution)/shard_map/ppermute | solution.py:36
  122.5 1.3 collective-permute-start.20
  123.8 2.0 %collective-permute-done.14 = bf16[48,2048]{1,0:T(8,128)(2,1)S(1)} collective-permute-done((bf16[48,2048]{1,0:T(8,128)(2,1)S(1)}, bf16[48,2048]{1,0:T(8,128)(2,1)S(1)}, u32[]{:S(2)}, u32[]{:S(2)}) %collective-permute-start.14) | collective-permute-done | bytes 196640 | tf_op jit(solution)/shard_map/ppermute | solution.py:36
  126.0 1.3 collective-permute-start.15
  127.3 2.5 %block_sums.1 = bf16[3,128,128]{2,1,0:T(8,128)(2,1)} custom-call(s32[3]{0:T(128)S(1)} %select_reduce_fusion.cols_ref, bf16[48,4096]{1,0:T(8,128)(2,1)S(1)} %bitcast.91, bf16[48,4096]{1,0:T(8,128)(2,1)S(1)} %collective-permute-done.4.refs_4_.refs_1_, bf16[48,4096]{1,0:T(8,128)(2,1)S(1)} %collective-permute-done.2.refs_1_.refs_2_, ...), custom_call_target="tpu_custom_call" | custom-call | tf_op jit(solution)/shard_map/block_sums/pallas_call | solution.py:199
  129.7 2.0 %collective-permute-done.18 = bf16[48,2048]{1,0:T(8,128)(2,1)S(1)} collective-permute-done((bf16[48,2048]{1,0:T(8,128)(2,1)S(1)}, bf16[48,2048]{1,0:T(8,128)(2,1)S(1)}, u32[]{:S(2)}, u32[]{:S(2)}) %collective-permute-start.18) | collective-permute-done | bytes 196640 | tf_op jit(solution)/shard_map/ppermute | solution.py:50
  131.8 3.5 %collective-permute-done.20 = bf16[48,2048]{1,0:T(8,128)(2,1)S(1)} collective-permute-done((bf16[48,2048]{1,0:T(8,128)(2,1)S(1)}, bf16[48,2048]{1,0:T(8,128)(2,1)S(1)}, u32[]{:S(2)}, u32[]{:S(2)}) %collective-permute-start.20) | collective-permute-done | bytes 196640 | tf_op jit(solution)/shard_map/ppermute | solution.py:50
  135.3 3.8 %collective-permute-done.15 = bf16[48,2048]{1,0:T(8,128)(2,1)S(1)} collective-permute-done((bf16[48,2048]{1,0:T(8,128)(2,1)S(1)}, bf16[48,2048]{1,0:T(8,128)(2,1)S(1)}, u32[]{:S(2)}, u32[]{:S(2)}) %collective-permute-start.15) | collective-permute-done | bytes 196640 | tf_op jit(solution)/shard_map/ppermute | solution.py:50
  (56 shorter events, 5.8 us)
Async XLA Ops:
  0.6 28.5 %collective-permute-start.4 = (bf16[48,4096]{1,0:T(8,128)(2,1)}, bf16[48,4096]{1,0:T(8,128)(2,1)S(1)}, u32[]{:S(2)}, u32[]{:S(2)}) collective-permute-start(bf16[48,4096]{1,0:T(8,128)(2,1)} %bitcast.87), channel_id=1, source_target_pairs={{0,1},{1,0},{2,3},{3,2},{4,5},{5,4},{6,7},{7,6},{8,9},{9,8},{10,11... | collective-permute-start | bytes 1179656 | tf_op jit(solution)/shard_map/ppermute | solution.py:40
  1.1 14.5 %collective-permute-start.3 = (bf16[48,4096]{1,0:T(8,128)(2,1)}, bf16[48,4096]{1,0:T(8,128)(2,1)S(1)}, u32[]{:S(2)}, u32[]{:S(2)}) collective-permute-start(bf16[48,4096]{1,0:T(8,128)(2,1)} %bitcast.88), channel_id=1, source_target_pairs={{0,6},{1,7},{2,0},{3,1},{4,2},{5,3},{6,4},{7,5},{8,14},{9,15},{10,... | collective-permute-start | bytes 1179656 | tf_op jit(solution)/shard_map/ppermute | solution.py:36
  5.8 18.5 %collective-permute-start.1 = (bf16[48,4096]{1,0:T(8,128)(2,1)}, bf16[48,4096]{1,0:T(8,128)(2,1)S(1)}, u32[]{:S(2)}, u32[]{:S(2)}) collective-permute-start(bf16[48,4096]{1,0:T(8,128)(2,1)} %bitcast.89), channel_id=1, source_target_pairs={{0,2},{1,3},{2,4},{3,5},{4,6},{5,7},{6,0},{7,1},{8,10},{9,11},{10,... | collective-permute-start | bytes 1179656 | tf_op jit(solution)/shard_map/ppermute | solution.py:36
  5.8 1.2 copy-start
  7.1 1.2 copy-start.1
  8.3 0.7 copy-start.3
  8.9 0.7 copy-start.4
  11.3 14.7 %collective-permute-start = (bf16[4,48,3200]{2,1,0:T(8,128)(2,1)S(1)}, bf16[4,48,3200]{2,1,0:T(8,128)(2,1)S(1)}, u32[]{:S(2)}, u32[]{:S(2)}) collective-permute-start(bf16[4,48,3200]{2,1,0:T(8,128)(2,1)S(1)} %pad_maximum_fusion), channel_id=1, source_target_pairs={{0,1},{1,0},{2,3},{3,2},{4,5},{5,4},{6,7},{7,6},{8,9},{9,8},{10,11... | collective-permute-start | bytes 3686408 | tf_op jit(solution)/shard_map/ppermute | solution.py:40
  15.6 15.3 %collective-permute-start.7 = (bf16[48,4096]{1,0:T(8,128)(2,1)S(1)}, bf16[48,4096]{1,0:T(8,128)(2,1)S(1)}, u32[]{:S(2)}, u32[]{:S(2)}) collective-permute-start(bf16[48,4096]{1,0:T(8,128)(2,1)S(1)} %collective-permute-done.3.refs_3_.refs_6_), channel_id=1, source_target_pairs={{0,1},{1,0},{2,3},{3,2},{4,5},{5,4},{6,7},{7,6},{8,9},{9,8},{10,11... | collective-permute-start | bytes 1179656 | tf_op jit(solution)/shard_map/ppermute | solution.py:40
  24.3 14.0 %collective-permute-start.2 = (bf16[48,4096]{1,0:T(8,128)(2,1)S(1)}, bf16[48,4096]{1,0:T(8,128)(2,1)S(1)}, u32[]{:S(2)}, u32[]{:S(2)}) collective-permute-start(bf16[48,4096]{1,0:T(8,128)(2,1)S(1)} %collective-permute-done.1.refs_2_.refs_4_), channel_id=1, source_target_pairs={{0,2},{1,3},{2,4},{3,5},{4,6},{5,7},{6,0},{7,1},{8,10},{9,11},{10,... | collective-permute-start | bytes 1179656 | tf_op jit(solution)/shard_map/ppermute | solution.py:36
  26.3 13.8 %copy-start.2 = (bf16[1,48,4096]{2,1,0:T(8,128)(2,1)S(1)}, bf16[1,48,4096]{2,1,0:T(8,128)(2,1)}, u32[]{:S(2)}) copy-start(bf16[1,48,4096]{2,1,0:T(8,128)(2,1)} %param.9) | copy-start | bytes 1179652
  26.3 50.1 %collective-permute-start.8 = (bf16[2,48,3200]{2,1,0:T(8,128)(2,1)S(1)}, bf16[2,48,3200]{2,1,0:T(8,128)(2,1)S(1)}, u32[]{:S(2)}, u32[]{:S(2)}) collective-permute-start(bf16[2,48,3200]{2,1,0:T(8,128)(2,1)S(1)} %pad_maximum_fusion.2), channel_id=1, source_target_pairs={{0,4},{1,5},{2,6},{3,7},{4,0},{5,1},{6,2},{7,3},{8,12},{9,13},{10,... | collective-permute-start | bytes 1843208 | tf_op jit(solution)/shard_map/ppermute | solution.py:36
  27.0 49.4 %collective-permute-start.9 = (bf16[2,48,3200]{2,1,0:T(8,128)(2,1)S(1)}, bf16[2,48,3200]{2,1,0:T(8,128)(2,1)S(1)}, u32[]{:S(2)}, u32[]{:S(2)}) collective-permute-start(bf16[2,48,3200]{2,1,0:T(8,128)(2,1)S(1)} %pad_maximum_fusion.3), channel_id=1, source_target_pairs={{0,2},{1,3},{2,4},{3,5},{4,6},{5,7},{6,0},{7,1},{8,10},{9,11},{10,... | collective-permute-start | bytes 1843208 | tf_op jit(solution)/shard_map/ppermute | solution.py:36
  29.1 47.3 %collective-permute-start.10 = (bf16[2,48,3200]{2,1,0:T(8,128)(2,1)S(1)}, bf16[2,48,3200]{2,1,0:T(8,128)(2,1)S(1)}, u32[]{:S(2)}, u32[]{:S(2)}) collective-permute-start(bf16[2,48,3200]{2,1,0:T(8,128)(2,1)S(1)} %pad_maximum_fusion.4), channel_id=1, source_target_pairs={{0,6},{1,7},{2,0},{3,1},{4,2},{5,3},{6,4},{7,5},{8,14},{9,15},{10,... | collective-permute-start | bytes 1843208 | tf_op jit(solution)/shard_map/ppermute | solution.py:36
  30.9 7.5 %collective-permute-start.6 = (bf16[48,4096]{1,0:T(8,128)(2,1)S(1)}, bf16[48,4096]{1,0:T(8,128)(2,1)S(1)}, u32[]{:S(2)}, u32[]{:S(2)}) collective-permute-start(bf16[48,4096]{1,0:T(8,128)(2,1)S(1)} %collective-permute-done.1.refs_2_.refs_4_), channel_id=1, source_target_pairs={{0,1},{1,0},{2,3},{3,2},{4,5},{5,4},{6,7},{7,6},{8,9},{9,8},{10,11... | collective-permute-start | bytes 1179656 | tf_op jit(solution)/shard_map/ppermute | solution.py:40
  38.3 1.7 %collective-permute-start.5 = (bf16[48,4096]{1,0:T(8,128)(2,1)S(1)}, bf16[48,4096]{1,0:T(8,128)(2,1)S(1)}, u32[]{:S(2)}, u32[]{:S(2)}) collective-permute-start(bf16[48,4096]{1,0:T(8,128)(2,1)S(1)} %collective-permute-done.2.refs_1_.refs_2_), channel_id=1, source_target_pairs={{0,1},{1,0},{2,3},{3,2},{4,5},{5,4},{6,7},{7,6},{8,9},{9,8},{10,11... | collective-permute-start | bytes 1179656 | tf_op jit(solution)/shard_map/ppermute | solution.py:40
  86.4 2.4 %collective-permute-start.11 = (bf16[4,48,2048]{2,1,0:T(8,128)(2,1)S(1)}, bf16[4,48,2048]{2,1,0:T(8,128)(2,1)S(1)}, u32[]{:S(2)}, u32[]{:S(2)}) collective-permute-start(bf16[4,48,2048]{2,1,0:T(8,128)(2,1)S(1)} %get-tuple-element.21), channel_id=1, source_target_pairs={{0,1},{1,0},{2,3},{3,2},{4,5},{5,4},{6,7},{7,6},{8,9},{9,8},{10,11... | collective-permute-start | bytes 2359304 | tf_op jit(solution)/shard_map/ppermute | solution.py:40
  88.9 21.7 %collective-permute-start.13 = (bf16[48,2048]{1,0:T(8,128)(2,1)S(1)}, bf16[48,2048]{1,0:T(8,128)(2,1)S(1)}, u32[]{:S(2)}, u32[]{:S(2)}) collective-permute-start(bf16[48,2048]{1,0:T(8,128)(2,1)S(1)} %get-tuple-element.31), channel_id=1, source_target_pairs={{0,6},{1,7},{2,0},{3,1},{4,2},{5,3},{6,4},{7,5},{8,14},{9,15},{10,... | collective-permute-start | bytes 589832 | tf_op jit(solution)/shard_map/ppermute | solution.py:36
  90.5 21.7 %copy-start.5 = (s32[1,16]{1,0:T(1,128)S(1)}, s32[1,16]{1,0:T(1,128)}, u32[]{:S(2)}) copy-start(s32[1,16]{1,0:T(1,128)} %param.17) | copy-start | bytes 196
  90.5 21.8 %copy-start.6 = (s32[1,16]{1,0:T(1,128)S(1)}, s32[1,16]{1,0:T(1,128)}, u32[]{:S(2)}) copy-start(s32[1,16]{1,0:T(1,128)} %param.16) | copy-start | bytes 196
  90.5 21.7 %collective-permute-start.12 = (bf16[48,2048]{1,0:T(8,128)(2,1)S(1)}, bf16[48,2048]{1,0:T(8,128)(2,1)S(1)}, u32[]{:S(2)}, u32[]{:S(2)}) collective-permute-start(bf16[48,2048]{1,0:T(8,128)(2,1)S(1)} %get-tuple-element.32), channel_id=1, source_target_pairs={{0,2},{1,3},{2,4},{3,5},{4,6},{5,7},{6,0},{7,1},{8,10},{9,11},{10,... | collective-permute-start | bytes 589832 | tf_op jit(solution)/shard_map/ppermute | solution.py:36
  112.2 2.3 %collective-permute-start.16 = (bf16[4,48,2048]{2,1,0:T(8,128)(2,1)S(1)}, bf16[4,48,2048]{2,1,0:T(8,128)(2,1)S(1)}, u32[]{:S(2)}, u32[]{:S(2)}) collective-permute-start(bf16[4,48,2048]{2,1,0:T(8,128)(2,1)S(1)} %get-tuple-element.24), channel_id=1, source_target_pairs={{0,1},{1,0},{2,3},{3,2},{4,5},{5,4},{6,7},{7,6},{8,9},{9,8},{10,11... | collective-permute-start | bytes 2359304 | tf_op jit(solution)/shard_map/ppermute | solution.py:40
  114.6 7.8 %collective-permute-start.19 = (bf16[48,2048]{1,0:T(8,128)(2,1)S(1)}, bf16[48,2048]{1,0:T(8,128)(2,1)S(1)}, u32[]{:S(2)}, u32[]{:S(2)}) collective-permute-start(bf16[48,2048]{1,0:T(8,128)(2,1)S(1)} %get-tuple-element.29), channel_id=1, source_target_pairs={{0,6},{1,7},{2,0},{3,1},{4,2},{5,3},{6,4},{7,5},{8,14},{9,15},{10,... | collective-permute-start | bytes 589832 | tf_op jit(solution)/shard_map/ppermute | solution.py:36
  114.8 11.1 %collective-permute-start.14 = (bf16[48,2048]{1,0:T(8,128)(2,1)S(1)}, bf16[48,2048]{1,0:T(8,128)(2,1)S(1)}, u32[]{:S(2)}, u32[]{:S(2)}) collective-permute-start(bf16[48,2048]{1,0:T(8,128)(2,1)S(1)} %fusion), channel_id=1, source_target_pairs={{0,6},{1,7},{2,0},{3,1},{4,2},{5,3},{6,4},{7,5},{8,14},{9,15},{10,... | collective-permute-start | bytes 589832 | tf_op jit(solution)/shard_map/ppermute | solution.py:36
  116.8 13.0 %collective-permute-start.17 = (bf16[48,2048]{1,0:T(8,128)(2,1)S(1)}, bf16[48,2048]{1,0:T(8,128)(2,1)S(1)}, u32[]{:S(2)}, u32[]{:S(2)}) collective-permute-start(bf16[48,2048]{1,0:T(8,128)(2,1)S(1)} %get-tuple-element.28), channel_id=1, source_target_pairs={{8,0},{9,1},{10,2},{11,3},{12,4},{13,5},{14,6},{15,7},{16,8},{17,9... | collective-permute-start | bytes 589832 | tf_op jit(solution)/shard_map/ppermute | solution.py:50
  118.0 13.7 %collective-permute-start.18 = (bf16[48,2048]{1,0:T(8,128)(2,1)S(1)}, bf16[48,2048]{1,0:T(8,128)(2,1)S(1)}, u32[]{:S(2)}, u32[]{:S(2)}) collective-permute-start(bf16[48,2048]{1,0:T(8,128)(2,1)S(1)} %get-tuple-element.30), channel_id=1, source_target_pairs={{8,2},{9,3},{10,4},{11,5},{12,6},{13,7},{14,0},{15,1},{16,10},{17,... | collective-permute-start | bytes 589832 | tf_op jit(solution)/shard_map/ppermute | solution.py:50
  122.5 12.7 %collective-permute-start.20 = (bf16[48,2048]{1,0:T(8,128)(2,1)S(1)}, bf16[48,2048]{1,0:T(8,128)(2,1)S(1)}, u32[]{:S(2)}, u32[]{:S(2)}) collective-permute-start(bf16[48,2048]{1,0:T(8,128)(2,1)S(1)} %add_convert_fusion.1), channel_id=1, source_target_pairs={{8,6},{9,7},{10,0},{11,1},{12,2},{13,3},{14,4},{15,5},{16,14},{17,... | collective-permute-start | bytes 589832 | tf_op jit(solution)/shard_map/ppermute | solution.py:50
  126.0 13.2 %collective-permute-start.15 = (bf16[48,2048]{1,0:T(8,128)(2,1)S(1)}, bf16[48,2048]{1,0:T(8,128)(2,1)S(1)}, u32[]{:S(2)}, u32[]{:S(2)}) collective-permute-start(bf16[48,2048]{1,0:T(8,128)(2,1)S(1)} %fusion.2), channel_id=1, source_target_pairs={{8,0},{9,1},{10,2},{11,3},{12,4},{13,5},{14,6},{15,7},{16,8},{17,9... | collective-permute-start | bytes 589832 | tf_op jit(solution)/shard_map/ppermute | solution.py:50

commit v3 on v2

--- a/solution.py
+++ b/solution.py
@@ -40,14 +40,18 @@
     return lax.ppermute(value, "dp", [(i, i ^ 1) for i in range(lax.axis_size("dp"))])
 
 
-def relayed(value, by):
-    devices, sections = lax.axis_size("dp"), lax.axis_size("section")
+def moved(value, routes):
+    devices = lax.axis_size("dp")
     pairs = [
-        (s * devices + i, (s - 1) * devices + (i - 2 * by) % devices)
-        for s in range(1, sections)
+        (first * devices + i, last * devices + (i + 2 * by) % devices)
+        for first, last, by in routes
         for i in range(devices)
     ]
     return lax.ppermute(value, ("section", "dp"), pairs)
+
+
+def relayed(value, by):
+    return moved(value, [(s, s - 1, -by) for s in range(1, lax.axis_size("section"))])
 
 
 def after(value, *earlier):
@@ -87,11 +91,10 @@
 
 
 def hidden_grad_kernel(*refs):
-    grads, (w_ref, out_ref, sum_ref) = refs[:-3], refs[-3:]
-    rows = grads[0].shape[0]
+    same, (other_ref, w_ref, out_ref, sum_ref) = refs[:-4], refs[-4:]
     step = pl.program_id(0)
     value = lax.dot_general(
-        jnp.concatenate([ref[...] for ref in grads], axis=0),
+        jnp.concatenate([ref[...] for ref in same] + [other_ref[p] for p in range(len(same))], axis=0),
         w_ref[...],
         (((1,), (1,)), ((), ())),
         preferred_element_type=jnp.float32,
@@ -110,46 +113,44 @@
         out_ref[...] = sum_ref[...].astype(jnp.bfloat16)
 
 
-def hidden_grad(grads, weight):
-    rows, width = grads[0].shape
+def hidden_grad(same, other, weight):
+    rows, width = same[0].shape
     units = weight.shape[0]
-    tile = 4 * LANES
-    out = (len(grads) * rows, units)
+    tile = 8 * LANES
+    out = (2 * len(same) * rows, units)
     return pl.pallas_call(
         hidden_grad_kernel,
         grid=(width // tile,),
-        in_specs=[pl.BlockSpec((rows, tile), lambda i: (0, i))] * len(grads)
-        + [pl.BlockSpec((units, tile), lambda i: (0, i))],
+        in_specs=[pl.BlockSpec((rows, tile), lambda i: (0, i))] * len(same)
+        + [pl.BlockSpec((len(same), rows, tile), lambda i: (0, 0, i)), pl.BlockSpec((units, tile), lambda i: (0, i))],
         out_specs=pl.BlockSpec(out, lambda i: (0, 0)),
         out_shape=jax.ShapeDtypeStruct(out, jnp.bfloat16),
         scratch_shapes=[pltpu.VMEM(out, jnp.float32)],
         compiler_params=pltpu.CompilerParams(vmem_limit_bytes=VMEM),
         cost_estimate=COST,
         name="hidden_grad",
-    )(*grads, weight)
-
-
-def gradients_kernel(dh_ref, *refs):
+    )(*same, other, weight)
+
+
+def gradients_kernel(blocks, dh_ref, *refs):
     given, (lg_ref, lu_ref) = refs[:-2], refs[-2:]
     units = dh_ref.shape[1]
     rows = given[0].shape[1]
-    skip = CAP * LANES
-    padded = (given[0].shape[2] - skip) // 2
-    for f in range(2):
-        for p, ref in enumerate(given):
-            part = slice((f * len(given) + p) * rows, (f * len(given) + p + 1) * rows)
-            wide = dh_ref[part, :].astype(jnp.float32)
-            gate = ref[f, :, skip : skip + units].astype(jnp.float32)
-            up = ref[f, :, skip + padded : skip + padded + units].astype(jnp.float32)
-            activated, slope = gelu_pair(gate)
-            lg_ref[part, :] = (wide * up * slope).astype(jnp.bfloat16)
-            lu_ref[part, :] = (wide * activated).astype(jnp.bfloat16)
-
-
-def local_gradients(dhidden, given):
+    padded = given[0].shape[2] // 2
+    for b, (i, f) in enumerate(blocks):
+        part = slice(b * rows, (b + 1) * rows)
+        wide = dh_ref[part, :].astype(jnp.float32)
+        gate = given[i][f, :, :units].astype(jnp.float32)
+        up = given[i][f, :, padded : padded + units].astype(jnp.float32)
+        activated, slope = gelu_pair(gate)
+        lg_ref[part, :] = (wide * up * slope).astype(jnp.bfloat16)
+        lu_ref[part, :] = (wide * activated).astype(jnp.bfloat16)
+
+
+def local_gradients(dhidden, given, blocks):
     out = jax.ShapeDtypeStruct(dhidden.shape, jnp.bfloat16)
     return pl.pallas_call(
-        gradients_kernel,
+        functools.partial(gradients_kernel, blocks),
         in_specs=[pl.BlockSpec(memory_space=pltpu.VMEM)] * (1 + len(given)),
         out_specs=[pl.BlockSpec(memory_space=pltpu.VMEM)] * 2,
         out_shape=[out, out],
@@ -184,24 +185,24 @@
     )(local_gate, local_up, w_gate, w_up)
 
 
-def block_kernel(scale, cols_ref, *refs):
-    out_ref = refs[-1]
-    refs = refs[:-1]
-    grads, hidden = refs[: len(refs) * 2 // 3], refs[len(refs) * 2 // 3 :]
-    left = jnp.concatenate([ref[f] for ref in hidden for f in range(2)], axis=0)
-    right = jnp.concatenate([ref[...] for ref in grads], axis=0)
+def block_kernel(scale, cols_ref, other_ref, *refs):
+    refs, out_ref = refs[:-1], refs[-1]
+    same, hidden = refs[: len(refs) // 2], refs[len(refs) // 2 :]
+    left = jnp.concatenate([ref[f] for f in range(2) for ref in hidden], axis=0)
+    right = jnp.concatenate([ref[...] for ref in same] + [other_ref[p] for p in range(len(same))], axis=0)
     value = lax.dot_general(left, right, (((0,), (0,)), ((), ())), preferred_element_type=jnp.float32)
     out_ref[0] = (value * scale).astype(jnp.bfloat16)
 
 
-def block_sums(cols, grads, hidden, scale):
-    rows = grads[0].shape[0]
+def block_sums(cols, same, other, hidden, scale):
+    rows = same[0].shape[0]
     return pl.pallas_call(
         functools.partial(block_kernel, scale),
         grid_spec=pltpu.PrefetchScalarGridSpec(
             num_scalar_prefetch=1,
             grid=(CAP,),
-            in_specs=[pl.BlockSpec((rows, LANES), lambda k, cols_ref: (0, cols_ref[k]))] * len(grads)
+            in_specs=[pl.BlockSpec((len(same), rows, LANES), lambda k, cols_ref: (0, 0, cols_ref[k]))]
+            + [pl.BlockSpec((rows, LANES), lambda k, cols_ref: (0, cols_ref[k]))] * len(same)
             + [pl.BlockSpec((2, rows, LANES), lambda k, cols_ref: (0, 0, k))] * len(hidden),
             out_specs=pl.BlockSpec((1, LANES, LANES), lambda k, cols_ref: (k, 0, 0)),
         ),
@@ -209,7 +210,7 @@
         compiler_params=pltpu.CompilerParams(vmem_limit_bytes=VMEM),
         cost_estimate=COST,
         name="block_sums",
-    )(cols, *grads, *hidden)
+    )(cols, other, *same, *hidden)
 
 
 def summed(*values):
@@ -239,18 +240,22 @@
     me = lax.axis_index("dp")
     chip, core = me // 2, me % 2
 
+    sections = lax.axis_size("section")
+    section = lax.axis_index("section")
+
     same = [mine] + [None] * (chips - 1)
     same[1] = rotated(mine, 1)
     if chips > 2:
         same[chips - 1] = rotated(mine, -1)
-    for r in range(2, chips - 1):
-        same[r] = rotated(same[r - 1], 1)
+    for r in range(chips - 2, 1, -1):
+        same[r] = rotated(after(same[r + 1], same[1]) if r == chips - 2 else same[r + 1], -1)
 
     slots = hidden_blocks(rows[0], owner[0], gate, up, replicas)
+    skip = CAP * LANES
     fill = jnp.zeros((tokens, -units % LANES), jnp.bfloat16)
 
     def held(replica):
-        parts = [lax.dynamic_slice_in_dim(slots, replica * CAP * LANES, CAP * LANES, 1)]
+        parts = [lax.dynamic_slice_in_dim(slots, replica * skip, skip, 1)]
         for values in (gate, up):
             parts += [lax.dynamic_slice_in_dim(values, replica * units, units, 1), fill]
         return jnp.concatenate(parts, axis=1)
@@ -259,43 +264,64 @@
         return 2 * ((chip + r) % chips) + (1 - core if other else core)
 
     taken = swapped(jnp.stack([held(ahead(r, True)) for r in range(chips)]))
+    both = [jnp.stack([held(ahead(r, False)), taken[r]]) for r in range(chips)]
+    columns = [value[:, :, skip:] for value in both]
+
+    far = chips // 2
+    needed = range(1, sections)
     order = [0] + list(range(chips - 2, 0, -1)) + ([chips - 1] if chips > 2 else [])
-    sent = {r: jnp.stack([held(ahead(r, False)), taken[r]]) for r in order}
-    given = {r: rotated(after(sent[r], same[1], same[chips - 1]), r) if r else sent[r] for r in order}
-
-    other = {r: swapped(same[r]) for r in order}
-    grads = [part[r] for part in (same, other) for r in order]
-    dhidden = hidden_grad([after(grads[0], *sent.values())] + grads[1:], w_down)
-    local_gate, local_up = local_gradients(dhidden, [given[r] for r in order])
-
-    parts = 2
+    passing = {s: moved(columns[far][:1], [(s, 0, 0)]) for s in needed}
+    sent, arrived = [], {0: columns[0]}
+    for r in order[1:]:
+        if r != far:
+            sent.append(after(columns[r], same[1], same[chips - 1]))
+            arrived[r] = moved(sent[-1], [(s, s, r) for s in needed])
+    halves = [jnp.zeros_like(passing[s]) for s in range(1, 3)]
+    for k in range(sections - 1):
+        through, direct = 1 + k, 1 + (k + 1) % (sections - 1)
+        value = jnp.where(section == 0, passing[through], columns[far][1:])
+        sent.append(after(value, same[1], same[chips - 1]))
+        value = moved(sent[-1], [(0, through, far), (direct, direct, far)])
+        halves = [jnp.where(section == s, value, half) for s, half in zip((through, direct), halves)]
+    given = [arrived[r] for r in order if r != far] + halves
+    blocks = []
+    for f in range(2):
+        nth = iter(range(chips))
+        blocks += [(chips - 1 + f, 0) if r == far else (next(nth), f) for r in order]
+
+    other = swapped(jnp.stack([same[r] for r in order]))
+    dhidden = hidden_grad([after(same[0], *sent)] + [same[r] for r in order[1:]], other, w_down)
+    local_gate, local_up = local_gradients(dhidden, given, blocks)
+    hidden = [both[0][:, :, :skip]]
+    hidden += [rotated(after(both[r][:, :, :skip], dhidden), r) for r in order[1:]]
+
+    parts = 1
     width = mine.shape[1] // parts
-    pieces, earlier = [], []
+    pieces, earlier = [], hidden[1:]
     for part in range(parts):
-        last = part == parts - 1
         kept, passed = terms(local_gate, local_up, w_gate, w_up, chips, part * width, width)
         passed = swapped(after(passed, *earlier) if earlier else passed)
         sums = {r: summed(kept[i], passed[i]) for i, r in enumerate(order)}
-        step = relayed if last else lambda value, by: rotated(value, -by)
-        total, running = [relayed(sums[0], 0) if last else sums[0]], None
+        total, running = [relayed(sums[0], 0)], None
         if chips > 1:
-            total.append(step(sums[chips - 1], chips - 1))
-        earlier = total[1:]
+            total.append(relayed(sums[chips - 1], chips - 1))
+        earlier = total[:]
         for r in range(chips - 2, 0, -1):
             value = sums[r] if running is None else summed(sums[r], running)
             if r == 1:
-                total.append(step(value, 1))
+                total.append(relayed(value, 1))
             else:
                 running = rotated(value, -1)
-                if len(earlier) < 2:
+                if len(earlier) < 3:
                     earlier.append(running)
-        pieces.append(summed(*total) if last else relayed(summed(*total), 0))
+        pieces.append(summed(*total))
     grad_input = jnp.concatenate(pieces, axis=1)
 
     block_grads = block_sums(
         after(own_columns(owner[0], cols[0], me), *sums.values()),
-        [part[r] for r in order for part in (same, other)],
-        [given[r] for r in order],
+        [same[r] for r in order],
+        other,
+        hidden,
         1.0 / replicas,
     )
     return (grad_input[None], block_grads[None])

time: 140 us -> 133 us (0.950); the launches traced: 140 us -> 131 us
  waiting for transfers between devices: 67.5 us -> 38.3 us
  starting transfers between devices: 32.7 us -> 50.8 us
  other arithmetic: 2.23 us -> 6.89 us
  Pallas kernels: 32.3 us -> 28.7 us
    ppermute x10 -> x7, waiting for transfers between devices: 52.2 us -> 18.1 us  [rotated(): return lax.ppermute(value, 'dp', pairs)]
    ppermute x4 -> x11, starting transfers between devices: 5.16 us -> 17.4 us  [moved(): return lax.ppermute(value, ('section', 'dp'), pairs)]
    ppermute x4 -> x11, waiting for transfers between devices: 9.31 us -> 16.8 us  [moved(): return lax.ppermute(value, ('section', 'dp'), pairs)]
    ppermute x10 -> x7, starting transfers between devices: 26.6 us -> 33.3 us  [rotated(): return lax.ppermute(value, 'dp', pairs)]
    ppermute x7 -> x3, waiting for transfers between devices: 5.95 us -> 3.4 us  [swapped(): lax.ppermute(value, 'dp', [(i, i ^ 1) for i in range(lax.axis_size('dp'))])]
    another operation x8 -> x12, other arithmetic: 0.37 us -> 2.8 us  [the longest x11 2.6 us: shards(): both = [jnp.stack([held(ahead(r, False)), taken[r]]) for r in range(chips)]]
    pallas_call x1, Pallas kernels: 11 us -> 8.83 us  [hidden_grad(): pl.pallas_call(hidden_grad_kernel, grid=(width // tile,), in_specs=[pl.Bl...]
    pallas_call x2 -> x1, Pallas kernels: 15.9 us -> 14.5 us  [terms(): pl.pallas_call(term_kernel, grid=(width // tile,), in_specs=[pl.BlockSpec...]
  transfers between devices with their start and end apart: 21 -> 21, of which waited for: 13 -> 5; matrix products, arithmetic and copies ran while one was open for 1% -> 6% of each run, Pallas kernels for 16% -> 22%
where the time goes in v3:
time: 133 us; the launch traced here: 131 us
  starting transfers between devices  50.8 us (38%)
  waiting for transfers between devices  38.3 us (29%)
  Pallas kernels  28.7 us (22%)
  other arithmetic  6.89 us (5%)
  local copies, waits for them, and re-layouts  5.65 us (4%)
    ppermute x7, starting transfers between devices, rotated(): return lax.ppermute(value, 'dp', pairs)  33.3 us
    ppermute x7, waiting for transfers between devices, rotated(): return lax.ppermute(value, 'dp', pairs)  18.1 us
    ppermute x11, starting transfers between devices, moved(): return lax.ppermute(value, ('section', 'dp'), pairs)  17.4 us
    ppermute x11, waiting for transfers between devices, moved(): return lax.ppermute(value, ('section', 'dp'), pairs)  16.8 us
    pallas_call x1, Pallas kernels, terms(): pl.pallas_call(term_kernel, grid=(width // tile,), in_specs=[pl.BlockSpec...  14.5 us
    pallas_call x1, Pallas kernels, hidden_grad(): pl.pallas_call(hidden_grad_kernel, grid=(width // tile,), in_specs=[pl.Bl...  8.83 us
    unnamed x14, local copies, waits for them, and re-layouts  3.8 us
    ppermute x3, waiting for transfers between devices, swapped(): lax.ppermute(value, 'dp', [(i, i ^ 1) for i in range(lax.axis_size('dp'))])  3.4 us
  transfers between devices with their start and end apart: 21, of which 5 were waited for; matrix products, arithmetic and copies ran while one was open for 6% of the time, Pallas kernels for 22%

profile of v3, /device:TPU:0, one launch (start us, length us, event | category | flops | bytes accessed | tf_op | source)
XLA Modules:
  0.0 131.4 jit_solution(462277693501390363)
XLA Ops:
  0.6 5.1 %collective-permute-start.2 = (bf16[48,4096]{1,0:T(8,128)(2,1)}, bf16[48,4096]{1,0:T(8,128)(2,1)S(1)}, u32[]{:S(2)}, u32[]{:S(2)}) collective-permute-start(bf16[48,4096]{1,0:T(8,128)(2,1)} %bitcast.76), channel_id=1, source_target_pairs={{0,6},{1,7},{2,0},{3,1},{4,2},{5,3},{6,4},{7,5},{8,14},{9,15},{10,... | collective-permute-start | bytes 1179656 | tf_op jit(solution)/shard_map/ppermute | solution.py:36
  5.7 1.2 copy-done
  7.0 1.2 copy-done.1
  9.5 0.9 hidden_blocks.1
  12.3 1.3 collective-permute-start.5
  13.6 1.3 collective-permute-start.4
  15.0 1.2 pad_maximum_fusion.1
  16.2 0.8 maximum_bitcast_fusion.7
  17.0 0.8 maximum_bitcast_fusion.5
  17.8 1.3 collective-permute-start.3
  19.1 4.5 %collective-permute-done.1.refs_2_ = bf16[48,4096]{1,0:T(8,128)(2,1)S(1)} collective-permute-done((bf16[48,4096]{1,0:T(8,128)(2,1)}, bf16[48,4096]{1,0:T(8,128)(2,1)S(1)}, u32[]{:S(2)}, u32[]{:S(2)}) %collective-permute-start.1) | collective-permute-done | bytes 393248 | tf_op jit(solution)/shard_map/ppermute | solution.py:36
  23.6 1.7 %collective-permute-start.6 = (bf16[48,4096]{1,0:T(8,128)(2,1)S(1)}, bf16[48,4096]{1,0:T(8,128)(2,1)S(1)}, u32[]{:S(2)}, u32[]{:S(2)}) collective-permute-start(bf16[48,4096]{1,0:T(8,128)(2,1)S(1)} %collective-permute-done.2.refs_3_), channel_id=1, source_target_pairs={{0,6},{1,7},{2,0},{3,1},{4,2},{5,3},{6,4},{7,5},{8,14},{9,15},{10,... | collective-permute-start | bytes 1179656 | tf_op jit(solution)/shard_map/ppermute | solution.py:36
  25.4 0.8 maximum_bitcast_fusion
  26.2 7.5 %collective-permute-done.6.refs_1_ = bf16[48,4096]{1,0:T(8,128)(2,1)S(1)} collective-permute-done((bf16[48,4096]{1,0:T(8,128)(2,1)S(1)}, bf16[48,4096]{1,0:T(8,128)(2,1)S(1)}, u32[]{:S(2)}, u32[]{:S(2)}) %collective-permute-start.6) | collective-permute-done | bytes 393248 | tf_op jit(solution)/shard_map/ppermute | solution.py:36
  34.1 1.1 broadcast_select_fusion
  35.3 2.4 %collective-permute-start.12 = (bf16[1,48,2816]{2,1,0:T(8,128)(2,1)S(1)}, bf16[1,48,2816]{2,1,0:T(8,128)(2,1)S(1)}, u32[]{:S(2)}, u32[]{:S(2)}) collective-permute-start(bf16[1,48,2816]{2,1,0:T(8,128)(2,1)S(1)} %get-tuple-element.20), channel_id=1, source_target_pairs={{0,12},{1,13},{2,14},{3,15},{4,8},{5,9},{6,10},{7,11},{16,20},{17,... | collective-permute-start | bytes 811016 | tf_op jit(solution)/shard_map/ppermute | solution.py:50
  37.8 4.2 %collective-permute-start.11 = (bf16[1,48,2816]{2,1,0:T(8,128)(2,1)S(1)}, bf16[1,48,2816]{2,1,0:T(8,128)(2,1)S(1)}, u32[]{:S(2)}, u32[]{:S(2)}) collective-permute-start(bf16[1,48,2816]{2,1,0:T(8,128)(2,1)S(1)} %get-tuple-element.21), channel_id=1, source_target_pairs={{0,20},{1,21},{2,22},{3,23},{4,16},{5,17},{6,18},{7,19},{24,28},{2... | collective-permute-start | bytes 811016 | tf_op jit(solution)/shard_map/ppermute | solution.py:50
  42.0 1.6 %collective-permute-start.10 = (bf16[1,48,2816]{2,1,0:T(8,128)(2,1)S(1)}, bf16[1,48,2816]{2,1,0:T(8,128)(2,1)S(1)}, u32[]{:S(2)}, u32[]{:S(2)}) collective-permute-start(bf16[1,48,2816]{2,1,0:T(8,128)(2,1)S(1)} %get-tuple-element.22), channel_id=1, source_target_pairs={{0,28},{1,29},{2,30},{3,31},{4,24},{5,25},{6,26},{7,27},{8,12},{9,... | collective-permute-start | bytes 811016 | tf_op jit(solution)/shard_map/ppermute | solution.py:50
  45.1 8.8 %hidden_grad.1.dh_ref = bf16[384,1408]{1,0:T(8,128)(2,1)S(1)} custom-call(bf16[48,4096]{1,0:T(8,128)(2,1)S(1)} %bitcast.78, bf16[48,4096]{1,0:T(8,128)(2,1)S(1)} %collective-permute-done.6.refs_1_, bf16[48,4096]{1,0:T(8,128)(2,1)S(1)} %collective-permute-done.1.refs_2_, bf16[48,4096]{1,0:T(8,128)(2,1)S(1)} %collective-permute-done.2.refs_3_, ...), custom_call_target="tpu_custom_call" | custom-call | tf_op jit(solution)/shard_map/hidden_grad/pallas_call | solution.py:121
  54.0 10.2 %collective-permute-start.13 = (bf16[2,48,384]{2,1,0:T(8,128)(2,1)S(1)}, bf16[2,48,384]{2,1,0:T(8,128)(2,1)S(1)}, u32[]{:S(2)}, u32[]{:S(2)}) collective-permute-start(bf16[2,48,384]{2,1,0:T(8,128)(2,1)S(1)} %pad_maximum_fusion.5), channel_id=1, source_target_pairs={{0,4},{1,5},{2,6},{3,7},{4,0},{5,1},{6,2},{7,3},{8,12},{9,13},{10,... | collective-permute-start | bytes 221192 | tf_op jit(solution)/shard_map/ppermute | solution.py:36
  64.2 6.2 %collective-permute-start.14 = (bf16[2,48,384]{2,1,0:T(8,128)(2,1)S(1)}, bf16[2,48,384]{2,1,0:T(8,128)(2,1)S(1)}, u32[]{:S(2)}, u32[]{:S(2)}) collective-permute-start(bf16[2,48,384]{2,1,0:T(8,128)(2,1)S(1)} %pad_maximum_fusion.4), channel_id=1, source_target_pairs={{0,2},{1,3},{2,4},{3,5},{4,6},{5,7},{6,0},{7,1},{8,10},{9,11},{10,... | collective-permute-start | bytes 221192 | tf_op jit(solution)/shard_map/ppermute | solution.py:36
  70.5 2.0 %local_gradients.1 = (bf16[384,1408]{1,0:T(8,128)(2,1)S(1)}, bf16[384,1408]{1,0:T(8,128)(2,1)S(1)}) custom-call(bf16[384,1408]{1,0:T(8,128)(2,1)S(1)} %hidden_grad.1.dh_ref, bf16[2,48,2816]{2,1,0:T(8,128)(2,1)S(1)} %fusion.refs_0_, bf16[2,48,2816]{2,1,0:T(8,128)(2,1)S(1)} %collective-permute-done.8.refs_1_, ...), custom_call_target="tpu_custom_call" | custom-call | tf_op jit(solution)/shard_map/local_gradients/pallas_call | solution.py:152
  72.5 14.5 %terms.1 = (bf16[4,48,4096]{2,1,0:T(8,128)(2,1)S(1)}, bf16[4,48,4096]{2,1,0:T(8,128)(2,1)S(1)}) custom-call(bf16[384,1408]{1,0:T(8,128)(2,1)S(1)} %get-tuple-element.25.lg_ref, bf16[384,1408]{1,0:T(8,128)(2,1)S(1)} %get-tuple-element.26.lu_ref, bf16[1408,4096]{1,0:T(8,128)(2,1)} %bitcast.85, bf16[1408,4096]{1,0:T(8,128)(2,1)} %bitcast.86), custom_call_target="tpu_custom_call" | custom-call | tf_op jit(solution)/shard_map/terms/pallas_call | solution.py:175
  87.2 3.4 %collective-permute-done.16 = bf16[4,48,4096]{2,1,0:T(8,128)(2,1)S(1)} collective-permute-done((bf16[4,48,4096]{2,1,0:T(8,128)(2,1)S(1)}, bf16[4,48,4096]{2,1,0:T(8,128)(2,1)S(1)}, u32[]{:S(2)}, u32[]{:S(2)}) %collective-permute-start.16) | collective-permute-done | bytes 1572896 | tf_op jit(solution)/shard_map/ppermute | solution.py:40
  90.9 10.1 %collective-permute-start.19 = (bf16[48,4096]{1,0:T(8,128)(2,1)S(1)}, bf16[48,4096]{1,0:T(8,128)(2,1)S(1)}, u32[]{:S(2)}, u32[]{:S(2)}) collective-permute-start(bf16[48,4096]{1,0:T(8,128)(2,1)S(1)} %get-tuple-element.37), channel_id=1, source_target_pairs={{0,6},{1,7},{2,0},{3,1},{4,2},{5,3},{6,4},{7,5},{8,14},{9,15},{10,... | collective-permute-start | bytes 1179656 | tf_op jit(solution)/shard_map/ppermute | solution.py:36
  100.9 1.3 collective-permute-start.17
  102.2 1.3 collective-permute-start.18
  103.5 6.1 %collective-permute-done.19 = bf16[48,4096]{1,0:T(8,128)(2,1)S(1)} collective-permute-done((bf16[48,4096]{1,0:T(8,128)(2,1)S(1)}, bf16[48,4096]{1,0:T(8,128)(2,1)S(1)}, u32[]{:S(2)}, u32[]{:S(2)}) %collective-permute-start.19) | collective-permute-done | bytes 393248 | tf_op jit(solution)/shard_map/ppermute | solution.py:36
  109.7 1.3 collective-permute-start.20
  111.3 2.4 %block_sums.1 = bf16[3,128,128]{2,1,0:T(8,128)(2,1)} custom-call(s32[3]{0:T(128)S(1)} %select_reduce_fusion.cols_ref, bf16[4,48,4096]{2,1,0:T(8,128)(2,1)S(1)} %collective-permute-done.7.refs_4_.other_ref, bf16[48,4096]{1,0:T(8,128)(2,1)S(1)} %bitcast.79, bf16[48,4096]{1,0:T(8,128)(2,1)S(1)} %collective-permute-done.6.refs_1_, ...), custom_call_target="tpu_custom_call" | custom-call | tf_op jit(solution)/shard_map/block_sums/pallas_call | solution.py:199
  113.8 16.8 %collective-permute-done.17 = bf16[48,4096]{1,0:T(8,128)(2,1)S(1)} collective-permute-done((bf16[48,4096]{1,0:T(8,128)(2,1)S(1)}, bf16[48,4096]{1,0:T(8,128)(2,1)S(1)}, u32[]{:S(2)}, u32[]{:S(2)}) %collective-permute-start.17) | collective-permute-done | bytes 393248 | tf_op jit(solution)/shard_map/ppermute | solution.py:50
  130.5 0.9 fusion.7
  (58 shorter events, 6.0 us)
Async XLA Ops:
  0.6 17.2 %collective-permute-start.2 = (bf16[48,4096]{1,0:T(8,128)(2,1)}, bf16[48,4096]{1,0:T(8,128)(2,1)S(1)}, u32[]{:S(2)}, u32[]{:S(2)}) collective-permute-start(bf16[48,4096]{1,0:T(8,128)(2,1)} %bitcast.76), channel_id=1, source_target_pairs={{0,6},{1,7},{2,0},{3,1},{4,2},{5,3},{6,4},{7,5},{8,14},{9,15},{10,... | collective-permute-start | bytes 1179656 | tf_op jit(solution)/shard_map/ppermute | solution.py:36
  5.7 17.9 %collective-permute-start.1 = (bf16[48,4096]{1,0:T(8,128)(2,1)}, bf16[48,4096]{1,0:T(8,128)(2,1)S(1)}, u32[]{:S(2)}, u32[]{:S(2)}) collective-permute-start(bf16[48,4096]{1,0:T(8,128)(2,1)} %bitcast.77), channel_id=1, source_target_pairs={{0,2},{1,3},{2,4},{3,5},{4,6},{5,7},{6,0},{7,1},{8,10},{9,11},{10,... | collective-permute-start | bytes 1179656 | tf_op jit(solution)/shard_map/ppermute | solution.py:36
  5.7 1.2 copy-start
  7.0 1.2 copy-start.1
  8.2 0.7 copy-start.3
  8.9 0.7 copy-start.4
  12.3 21.8 %collective-permute-start.5 = (bf16[1,48,2816]{2,1,0:T(8,128)(2,1)}, bf16[1,48,2816]{2,1,0:T(8,128)(2,1)}, u32[]{:S(2)}, u32[]{:S(2)}) collective-permute-start(bf16[1,48,2816]{2,1,0:T(8,128)(2,1)} %slice.100), channel_id=1, source_target_pairs={{24,0},{25,1},{26,2},{27,3},{28,4},{29,5},{30,6},{31,7}} | collective-permute-start | bytes 811016 | tf_op jit(solution)/shard_map/ppermute | solution.py:50
  13.6 20.5 %collective-permute-start.4 = (bf16[1,48,2816]{2,1,0:T(8,128)(2,1)}, bf16[1,48,2816]{2,1,0:T(8,128)(2,1)}, u32[]{:S(2)}, u32[]{:S(2)}) collective-permute-start(bf16[1,48,2816]{2,1,0:T(8,128)(2,1)} %slice.100), channel_id=1, source_target_pairs={{16,0},{17,1},{18,2},{19,3},{20,4},{21,5},{22,6},{23,7}} | collective-permute-start | bytes 811016 | tf_op jit(solution)/shard_map/ppermute | solution.py:50
  15.0 18.7 %copy-start.2 = (bf16[1,48,4096]{2,1,0:T(8,128)(2,1)S(1)}, bf16[1,48,4096]{2,1,0:T(8,128)(2,1)}, u32[]{:S(2)}) copy-start(bf16[1,48,4096]{2,1,0:T(8,128)(2,1)} %param.9) | copy-start | bytes 1179652
  16.2 17.7 %collective-permute-start = (bf16[4,48,3200]{2,1,0:T(8,128)(2,1)}, bf16[4,48,3200]{2,1,0:T(8,128)(2,1)S(1)}, u32[]{:S(2)}, u32[]{:S(2)}) collective-permute-start(bf16[4,48,3200]{2,1,0:T(8,128)(2,1)} %pad_maximum_fusion.1), channel_id=1, source_target_pairs={{0,1},{1,0},{2,3},{3,2},{4,5},{5,4},{6,7},{7,6},{8,9},{9,8},{10,11... | collective-permute-start | bytes 3686408 | tf_op jit(solution)/shard_map/ppermute | solution.py:40
  17.8 16.2 %collective-permute-start.3 = (bf16[1,48,2816]{2,1,0:T(8,128)(2,1)}, bf16[1,48,2816]{2,1,0:T(8,128)(2,1)S(1)}, u32[]{:S(2)}, u32[]{:S(2)}) collective-permute-start(bf16[1,48,2816]{2,1,0:T(8,128)(2,1)} %slice.100), channel_id=1, source_target_pairs={{8,0},{9,1},{10,2},{11,3},{12,4},{13,5},{14,6},{15,7}} | collective-permute-start | bytes 811016 | tf_op jit(solution)/shard_map/ppermute | solution.py:50
  23.6 10.0 %collective-permute-start.6 = (bf16[48,4096]{1,0:T(8,128)(2,1)S(1)}, bf16[48,4096]{1,0:T(8,128)(2,1)S(1)}, u32[]{:S(2)}, u32[]{:S(2)}) collective-permute-start(bf16[48,4096]{1,0:T(8,128)(2,1)S(1)} %collective-permute-done.2.refs_3_), channel_id=1, source_target_pairs={{0,6},{1,7},{2,0},{3,1},{4,2},{5,3},{6,4},{7,5},{8,14},{9,15},{10,... | collective-permute-start | bytes 1179656 | tf_op jit(solution)/shard_map/ppermute | solution.py:36
  33.9 10.6 %collective-permute-start.7 = (bf16[4,48,4096]{2,1,0:T(8,128)(2,1)S(1)}, bf16[4,48,4096]{2,1,0:T(8,128)(2,1)S(1)}, u32[]{:S(2)}, u32[]{:S(2)}) collective-permute-start(bf16[4,48,4096]{2,1,0:T(8,128)(2,1)S(1)} %pad_maximum_fusion), channel_id=1, source_target_pairs={{0,1},{1,0},{2,3},{3,2},{4,5},{5,4},{6,7},{7,6},{8,9},{9,8},{10,11... | collective-permute-start | bytes 4718600 | tf_op jit(solution)/shard_map/ppermute | solution.py:40
  35.3 18.6 %collective-permute-start.12 = (bf16[1,48,2816]{2,1,0:T(8,128)(2,1)S(1)}, bf16[1,48,2816]{2,1,0:T(8,128)(2,1)S(1)}, u32[]{:S(2)}, u32[]{:S(2)}) collective-permute-start(bf16[1,48,2816]{2,1,0:T(8,128)(2,1)S(1)} %get-tuple-element.20), channel_id=1, source_target_pairs={{0,12},{1,13},{2,14},{3,15},{4,8},{5,9},{6,10},{7,11},{16,20},{17,... | collective-permute-start | bytes 811016 | tf_op jit(solution)/shard_map/ppermute | solution.py:50
  37.8 26.4 %collective-permute-start.11 = (bf16[1,48,2816]{2,1,0:T(8,128)(2,1)S(1)}, bf16[1,48,2816]{2,1,0:T(8,128)(2,1)S(1)}, u32[]{:S(2)}, u32[]{:S(2)}) collective-permute-start(bf16[1,48,2816]{2,1,0:T(8,128)(2,1)S(1)} %get-tuple-element.21), channel_id=1, source_target_pairs={{0,20},{1,21},{2,22},{3,23},{4,16},{5,17},{6,18},{7,19},{24,28},{2... | collective-permute-start | bytes 811016 | tf_op jit(solution)/shard_map/ppermute | solution.py:50
  42.0 28.4 %collective-permute-start.10 = (bf16[1,48,2816]{2,1,0:T(8,128)(2,1)S(1)}, bf16[1,48,2816]{2,1,0:T(8,128)(2,1)S(1)}, u32[]{:S(2)}, u32[]{:S(2)}) collective-permute-start(bf16[1,48,2816]{2,1,0:T(8,128)(2,1)S(1)} %get-tuple-element.22), channel_id=1, source_target_pairs={{0,28},{1,29},{2,30},{3,31},{4,24},{5,25},{6,26},{7,27},{8,12},{9,... | collective-permute-start | bytes 811016 | tf_op jit(solution)/shard_map/ppermute | solution.py:50
  43.6 26.9 %collective-permute-start.8 = (bf16[2,48,2816]{2,1,0:T(8,128)(2,1)S(1)}, bf16[2,48,2816]{2,1,0:T(8,128)(2,1)S(1)}, u32[]{:S(2)}, u32[]{:S(2)}) collective-permute-start(bf16[2,48,2816]{2,1,0:T(8,128)(2,1)S(1)} %fusion.2), channel_id=1, source_target_pairs={{8,10},{9,11},{10,12},{11,13},{12,14},{13,15},{14,8},{15,9},{16,18... | collective-permute-start | bytes 1622024 | tf_op jit(solution)/shard_map/ppermute | solution.py:50
  44.4 26.0 %collective-permute-start.9 = (bf16[2,48,2816]{2,1,0:T(8,128)(2,1)S(1)}, bf16[2,48,2816]{2,1,0:T(8,128)(2,1)S(1)}, u32[]{:S(2)}, u32[]{:S(2)}) collective-permute-start(bf16[2,48,2816]{2,1,0:T(8,128)(2,1)S(1)} %fusion.1), channel_id=1, source_target_pairs={{8,14},{9,15},{10,8},{11,9},{12,10},{13,11},{14,12},{15,13},{16,22... | collective-permute-start | bytes 1622024 | tf_op jit(solution)/shard_map/ppermute | solution.py:50
  54.0 33.1 %collective-permute-start.13 = (bf16[2,48,384]{2,1,0:T(8,128)(2,1)S(1)}, bf16[2,48,384]{2,1,0:T(8,128)(2,1)S(1)}, u32[]{:S(2)}, u32[]{:S(2)}) collective-permute-start(bf16[2,48,384]{2,1,0:T(8,128)(2,1)S(1)} %pad_maximum_fusion.5), channel_id=1, source_target_pairs={{0,4},{1,5},{2,6},{3,7},{4,0},{5,1},{6,2},{7,3},{8,12},{9,13},{10,... | collective-permute-start | bytes 221192 | tf_op jit(solution)/shard_map/ppermute | solution.py:36
  64.2 22.9 %collective-permute-start.14 = (bf16[2,48,384]{2,1,0:T(8,128)(2,1)S(1)}, bf16[2,48,384]{2,1,0:T(8,128)(2,1)S(1)}, u32[]{:S(2)}, u32[]{:S(2)}) collective-permute-start(bf16[2,48,384]{2,1,0:T(8,128)(2,1)S(1)} %pad_maximum_fusion.4), channel_id=1, source_target_pairs={{0,2},{1,3},{2,4},{3,5},{4,6},{5,7},{6,0},{7,1},{8,10},{9,11},{10,... | collective-permute-start | bytes 221192 | tf_op jit(solution)/shard_map/ppermute | solution.py:36
  70.4 16.7 %collective-permute-start.15 = (bf16[2,48,384]{2,1,0:T(8,128)(2,1)S(1)}, bf16[2,48,384]{2,1,0:T(8,128)(2,1)S(1)}, u32[]{:S(2)}, u32[]{:S(2)}) collective-permute-start(bf16[2,48,384]{2,1,0:T(8,128)(2,1)S(1)} %pad_maximum_fusion.3), channel_id=1, source_target_pairs={{0,6},{1,7},{2,0},{3,1},{4,2},{5,3},{6,4},{7,5},{8,14},{9,15},{10,... | collective-permute-start | bytes 221192 | tf_op jit(solution)/shard_map/ppermute | solution.py:36
  87.1 3.5 %collective-permute-start.16 = (bf16[4,48,4096]{2,1,0:T(8,128)(2,1)S(1)}, bf16[4,48,4096]{2,1,0:T(8,128)(2,1)S(1)}, u32[]{:S(2)}, u32[]{:S(2)}) collective-permute-start(bf16[4,48,4096]{2,1,0:T(8,128)(2,1)S(1)} %get-tuple-element.32), channel_id=1, source_target_pairs={{0,1},{1,0},{2,3},{3,2},{4,5},{5,4},{6,7},{7,6},{8,9},{9,8},{10,11... | collective-permute-start | bytes 4718600 | tf_op jit(solution)/shard_map/ppermute | solution.py:40
  90.8 20.2 %copy-start.5 = (s32[1,16]{1,0:T(1,128)S(1)}, s32[1,16]{1,0:T(1,128)}, u32[]{:S(2)}) copy-start(s32[1,16]{1,0:T(1,128)} %param.17) | copy-start | bytes 196
  90.8 20.3 %copy-start.6 = (s32[1,16]{1,0:T(1,128)S(1)}, s32[1,16]{1,0:T(1,128)}, u32[]{:S(2)}) copy-start(s32[1,16]{1,0:T(1,128)} %param.16) | copy-start | bytes 196
  90.9 18.7 %collective-permute-start.19 = (bf16[48,4096]{1,0:T(8,128)(2,1)S(1)}, bf16[48,4096]{1,0:T(8,128)(2,1)S(1)}, u32[]{:S(2)}, u32[]{:S(2)}) collective-permute-start(bf16[48,4096]{1,0:T(8,128)(2,1)S(1)} %get-tuple-element.37), channel_id=1, source_target_pairs={{0,6},{1,7},{2,0},{3,1},{4,2},{5,3},{6,4},{7,5},{8,14},{9,15},{10,... | collective-permute-start | bytes 1179656 | tf_op jit(solution)/shard_map/ppermute | solution.py:36
  100.9 29.6 %collective-permute-start.17 = (bf16[48,4096]{1,0:T(8,128)(2,1)S(1)}, bf16[48,4096]{1,0:T(8,128)(2,1)S(1)}, u32[]{:S(2)}, u32[]{:S(2)}) collective-permute-start(bf16[48,4096]{1,0:T(8,128)(2,1)S(1)} %get-tuple-element.36), channel_id=1, source_target_pairs={{8,0},{9,1},{10,2},{11,3},{12,4},{13,5},{14,6},{15,7},{16,8},{17,9... | collective-permute-start | bytes 1179656 | tf_op jit(solution)/shard_map/ppermute | solution.py:50
  102.2 28.3 %collective-permute-start.18 = (bf16[48,4096]{1,0:T(8,128)(2,1)S(1)}, bf16[48,4096]{1,0:T(8,128)(2,1)S(1)}, u32[]{:S(2)}, u32[]{:S(2)}) collective-permute-start(bf16[48,4096]{1,0:T(8,128)(2,1)S(1)} %get-tuple-element.38), channel_id=1, source_target_pairs={{8,2},{9,3},{10,4},{11,5},{12,6},{13,7},{14,0},{15,1},{16,10},{17,... | collective-permute-start | bytes 1179656 | tf_op jit(solution)/shard_map/ppermute | solution.py:50
  109.7 20.8 %collective-permute-start.20 = (bf16[48,4096]{1,0:T(8,128)(2,1)S(1)}, bf16[48,4096]{1,0:T(8,128)(2,1)S(1)}, u32[]{:S(2)}, u32[]{:S(2)}) collective-permute-start(bf16[48,4096]{1,0:T(8,128)(2,1)S(1)} %add_convert_fusion.1), channel_id=1, source_target_pairs={{8,6},{9,7},{10,0},{11,1},{12,2},{13,3},{14,4},{15,5},{16,14},{17,... | collective-permute-start | bytes 1179656 | tf_op jit(solution)/shard_map/ppermute | solution.py:50

commit v4 on v3

--- a/solution.py
+++ b/solution.py
@@ -133,7 +133,7 @@
 
 
 def gradients_kernel(blocks, dh_ref, *refs):
-    given, (lg_ref, lu_ref) = refs[:-2], refs[-2:]
+    given, out_ref = refs[:-1], refs[-1]
     units = dh_ref.shape[1]
     rows = given[0].shape[1]
     padded = given[0].shape[2] // 2
@@ -143,46 +143,46 @@
         gate = given[i][f, :, :units].astype(jnp.float32)
         up = given[i][f, :, padded : padded + units].astype(jnp.float32)
         activated, slope = gelu_pair(gate)
-        lg_ref[part, :] = (wide * up * slope).astype(jnp.bfloat16)
-        lu_ref[part, :] = (wide * activated).astype(jnp.bfloat16)
+        out_ref[part, :units] = (wide * up * slope).astype(jnp.bfloat16)
+        out_ref[part, units:] = (wide * activated).astype(jnp.bfloat16)
 
 
 def local_gradients(dhidden, given, blocks):
-    out = jax.ShapeDtypeStruct(dhidden.shape, jnp.bfloat16)
+    rows, units = dhidden.shape
     return pl.pallas_call(
         functools.partial(gradients_kernel, blocks),
         in_specs=[pl.BlockSpec(memory_space=pltpu.VMEM)] * (1 + len(given)),
-        out_specs=[pl.BlockSpec(memory_space=pltpu.VMEM)] * 2,
-        out_shape=[out, out],
+        out_specs=pl.BlockSpec(memory_space=pltpu.VMEM),
+        out_shape=jax.ShapeDtypeStruct((rows, 2 * units), jnp.bfloat16),
         compiler_params=pltpu.CompilerParams(vmem_limit_bytes=VMEM),
         cost_estimate=COST,
         name="local_gradients",
     )(dhidden, *given)
 
 
-def term_kernel(lg_ref, lu_ref, wg_ref, wu_ref, same_ref, other_ref):
-    term = jnp.dot(lg_ref[...], wg_ref[...], preferred_element_type=jnp.float32)
-    term += jnp.dot(lu_ref[...], wu_ref[...], preferred_element_type=jnp.float32)
+def term_kernel(local_ref, wg_ref, wu_ref, same_ref, other_ref):
+    weight = jnp.concatenate([wg_ref[...], wu_ref[...]], axis=0)
+    term = jnp.dot(local_ref[...], weight, preferred_element_type=jnp.float32)
     term = term.astype(jnp.bfloat16).reshape(2, *same_ref.shape)
     same_ref[...] = term[0]
     other_ref[...] = term[1]
 
 
-def terms(local_gate, local_up, w_gate, w_up, chips, first, width):
-    rows, units = local_gate.shape
-    tile = 4 * LANES
+def terms(local, w_gate, w_up, chips, first, width):
+    rows, units = local.shape[0], w_gate.shape[0]
+    tile = 8 * LANES
     out = (chips, rows // (2 * chips))
     return pl.pallas_call(
         term_kernel,
         grid=(width // tile,),
-        in_specs=[pl.BlockSpec((rows, units), lambda i: (0, 0))] * 2
+        in_specs=[pl.BlockSpec((rows, 2 * units), lambda i: (0, 0))]
         + [pl.BlockSpec((units, tile), lambda i: (0, i + first // tile))] * 2,
         out_specs=[pl.BlockSpec(out + (tile,), lambda i: (0, 0, i))] * 2,
         out_shape=[jax.ShapeDtypeStruct(out + (width,), jnp.bfloat16)] * 2,
         compiler_params=pltpu.CompilerParams(vmem_limit_bytes=VMEM),
         cost_estimate=COST,
         name="terms",
-    )(local_gate, local_up, w_gate, w_up)
+    )(local, w_gate, w_up)
 
 
 def block_kernel(scale, cols_ref, other_ref, *refs):
@@ -248,7 +248,7 @@
     if chips > 2:
         same[chips - 1] = rotated(mine, -1)
     for r in range(chips - 2, 1, -1):
-        same[r] = rotated(after(same[r + 1], same[1]) if r == chips - 2 else same[r + 1], -1)
+        same[r] = rotated(same[r + 1], -1)
 
     slots = hidden_blocks(rows[0], owner[0], gate, up, replicas)
     skip = CAP * LANES
@@ -291,7 +291,7 @@
 
     other = swapped(jnp.stack([same[r] for r in order]))
     dhidden = hidden_grad([after(same[0], *sent)] + [same[r] for r in order[1:]], other, w_down)
-    local_gate, local_up = local_gradients(dhidden, given, blocks)
+    local = local_gradients(dhidden, given, blocks)
     hidden = [both[0][:, :, :skip]]
     hidden += [rotated(after(both[r][:, :, :skip], dhidden), r) for r in order[1:]]
 
@@ -299,7 +299,7 @@
     width = mine.shape[1] // parts
     pieces, earlier = [], hidden[1:]
     for part in range(parts):
-        kept, passed = terms(local_gate, local_up, w_gate, w_up, chips, part * width, width)
+        kept, passed = terms(local, w_gate, w_up, chips, part * width, width)
         passed = swapped(after(passed, *earlier) if earlier else passed)
         sums = {r: summed(kept[i], passed[i]) for i, r in enumerate(order)}
         total, running = [relayed(sums[0], 0)], None

time: 133 us -> 129 us (0.970)
  waiting for transfers between devices: 38.3 us -> 35.3 us
  Pallas kernels: 28.7 us -> 27 us
  starting transfers between devices: 50.8 us -> 52.3 us
    ppermute x7, waiting for transfers between devices: 18.1 us -> 14.4 us  [rotated(): return lax.ppermute(value, 'dp', pairs)]
    pallas_call x1, Pallas kernels: 14.5 us -> 12.8 us  [terms(): pl.pallas_call(term_kernel, grid=(width // tile,), in_specs=[pl.BlockSpec...]
    ppermute x7, starting transfers between devices: 33.3 us -> 34.9 us  [rotated(): return lax.ppermute(value, 'dp', pairs)]
  transfers between devices with their start and end apart: 21 -> 21, of which waited for: 5 -> 6; matrix products, arithmetic and copies ran while one was open for 6% -> 6% of each run, Pallas kernels for 22% -> 21%
where the time goes in v4:
time: 129 us; the launch traced here: 128 us
  starting transfers between devices  52.3 us (41%)
  waiting for transfers between devices  35.3 us (27%)
  Pallas kernels  27 us (21%)
  other arithmetic  6.87 us (5%)
  local copies, waits for them, and re-layouts  5.65 us (4%)
    ppermute x7, starting transfers between devices, rotated(): return lax.ppermute(value, 'dp', pairs)  34.9 us
    ppermute x11, waiting for transfers between devices, moved(): return lax.ppermute(value, ('section', 'dp'), pairs)  17.4 us
    ppermute x11, starting transfers between devices, moved(): return lax.ppermute(value, ('section', 'dp'), pairs)  17.2 us
    ppermute x7, waiting for transfers between devices, rotated(): return lax.ppermute(value, 'dp', pairs)  14.4 us
    pallas_call x1, Pallas kernels, terms(): pl.pallas_call(term_kernel, grid=(width // tile,), in_specs=[pl.BlockSpec...  12.8 us
    pallas_call x1, Pallas kernels, hidden_grad(): pl.pallas_call(hidden_grad_kernel, grid=(width // tile,), in_specs=[pl.Bl...  8.83 us
    unnamed x14, local copies, waits for them, and re-layouts  3.8 us
    ppermute x3, waiting for transfers between devices, swapped(): lax.ppermute(value, 'dp', [(i, i ^ 1) for i in range(lax.axis_size('dp'))])  3.4 us
  transfers between devices with their start and end apart: 21, of which 6 were waited for; matrix products, arithmetic and copies ran while one was open for 6% of the time, Pallas kernels for 21%

profile of v4, /device:TPU:0, one launch (start us, length us, event | category | flops | bytes accessed | tf_op | source)
XLA Modules:
  0.0 128.1 jit_solution(1326187304562337470)
XLA Ops:
  0.6 5.1 %collective-permute-start.2 = (bf16[48,4096]{1,0:T(8,128)(2,1)}, bf16[48,4096]{1,0:T(8,128)(2,1)S(1)}, u32[]{:S(2)}, u32[]{:S(2)}) collective-permute-start(bf16[48,4096]{1,0:T(8,128)(2,1)} %bitcast.76), channel_id=1, source_target_pairs={{0,6},{1,7},{2,0},{3,1},{4,2},{5,3},{6,4},{7,5},{8,14},{9,15},{10,... | collective-permute-start | bytes 1179656 | tf_op jit(solution)/shard_map/ppermute | solution.py:36
  5.7 1.2 copy-done
  7.0 1.2 copy-done.1
  9.5 0.9 hidden_blocks.1
  12.3 1.3 collective-permute-start.5
  13.6 1.3 %collective-permute-start.4 = (bf16[1,48,2816]{2,1,0:T(8,128)(2,1)}, bf16[1,48,2816]{2,1,0:T(8,128)(2,1)}, u32[]{:S(2)}, u32[]{:S(2)}) collective-permute-start(bf16[1,48,2816]{2,1,0:T(8,128)(2,1)} %slice.100), channel_id=1, source_target_pairs={{16,0},{17,1},{18,2},{19,3},{20,4},{21,5},{22,6},{23,7}} | collective-permute-start | bytes 811016 | tf_op jit(solution)/shard_map/ppermute | solution.py:50
  15.0 1.2 pad_maximum_fusion.1
  16.2 0.8 maximum_bitcast_fusion.7
  17.0 0.8 maximum_bitcast_fusion.5
  17.8 3.9 %collective-permute-start.6 = (bf16[48,4096]{1,0:T(8,128)(2,1)S(1)}, bf16[48,4096]{1,0:T(8,128)(2,1)S(1)}, u32[]{:S(2)}, u32[]{:S(2)}) collective-permute-start(bf16[48,4096]{1,0:T(8,128)(2,1)S(1)} %collective-permute-done.2.refs_3_), channel_id=1, source_target_pairs={{0,6},{1,7},{2,0},{3,1},{4,2},{5,3},{6,4},{7,5},{8,14},{9,15},{10,... | collective-permute-start | bytes 1179656 | tf_op jit(solution)/shard_map/ppermute | solution.py:36
  21.7 0.8 maximum_bitcast_fusion
  22.5 1.8 %collective-permute-done.1.refs_2_ = bf16[48,4096]{1,0:T(8,128)(2,1)S(1)} collective-permute-done((bf16[48,4096]{1,0:T(8,128)(2,1)}, bf16[48,4096]{1,0:T(8,128)(2,1)S(1)}, u32[]{:S(2)}, u32[]{:S(2)}) %collective-permute-start.1) | collective-permute-done | bytes 393248 | tf_op jit(solution)/shard_map/ppermute | solution.py:36
  24.3 1.3 collective-permute-start.3
  25.5 6.6 %collective-permute-done.6.refs_1_ = bf16[48,4096]{1,0:T(8,128)(2,1)S(1)} collective-permute-done((bf16[48,4096]{1,0:T(8,128)(2,1)S(1)}, bf16[48,4096]{1,0:T(8,128)(2,1)S(1)}, u32[]{:S(2)}, u32[]{:S(2)}) %collective-permute-start.6) | collective-permute-done | bytes 393248 | tf_op jit(solution)/shard_map/ppermute | solution.py:36
  33.2 1.1 broadcast_select_fusion
  34.5 1.7 %collective-permute-start.12 = (bf16[1,48,2816]{2,1,0:T(8,128)(2,1)S(1)}, bf16[1,48,2816]{2,1,0:T(8,128)(2,1)S(1)}, u32[]{:S(2)}, u32[]{:S(2)}) collective-permute-start(bf16[1,48,2816]{2,1,0:T(8,128)(2,1)S(1)} %get-tuple-element.17), channel_id=1, source_target_pairs={{0,12},{1,13},{2,14},{3,15},{4,8},{5,9},{6,10},{7,11},{16,20},{17,... | collective-permute-start | bytes 811016 | tf_op jit(solution)/shard_map/ppermute | solution.py:50
  36.2 4.7 %collective-permute-start.11 = (bf16[1,48,2816]{2,1,0:T(8,128)(2,1)S(1)}, bf16[1,48,2816]{2,1,0:T(8,128)(2,1)S(1)}, u32[]{:S(2)}, u32[]{:S(2)}) collective-permute-start(bf16[1,48,2816]{2,1,0:T(8,128)(2,1)S(1)} %get-tuple-element.18), channel_id=1, source_target_pairs={{0,20},{1,21},{2,22},{3,23},{4,16},{5,17},{6,18},{7,19},{24,28},{2... | collective-permute-start | bytes 811016 | tf_op jit(solution)/shard_map/ppermute | solution.py:50
  40.9 1.6 %collective-permute-start.10 = (bf16[1,48,2816]{2,1,0:T(8,128)(2,1)S(1)}, bf16[1,48,2816]{2,1,0:T(8,128)(2,1)S(1)}, u32[]{:S(2)}, u32[]{:S(2)}) collective-permute-start(bf16[1,48,2816]{2,1,0:T(8,128)(2,1)S(1)} %get-tuple-element.19), channel_id=1, source_target_pairs={{0,28},{1,29},{2,30},{3,31},{4,24},{5,25},{6,26},{7,27},{8,12},{9,... | collective-permute-start | bytes 811016 | tf_op jit(solution)/shard_map/ppermute | solution.py:50
  44.1 8.8 %hidden_grad.1.dh_ref = bf16[384,1408]{1,0:T(8,128)(2,1)S(1)} custom-call(bf16[48,4096]{1,0:T(8,128)(2,1)S(1)} %bitcast.78, bf16[48,4096]{1,0:T(8,128)(2,1)S(1)} %collective-permute-done.6.refs_1_, bf16[48,4096]{1,0:T(8,128)(2,1)S(1)} %collective-permute-done.1.refs_2_, bf16[48,4096]{1,0:T(8,128)(2,1)S(1)} %collective-permute-done.2.refs_3_, ...), custom_call_target="tpu_custom_call" | custom-call | tf_op jit(solution)/shard_map/hidden_grad/pallas_call | solution.py:121
  52.9 9.6 %collective-permute-start.13 = (bf16[2,48,384]{2,1,0:T(8,128)(2,1)S(1)}, bf16[2,48,384]{2,1,0:T(8,128)(2,1)S(1)}, u32[]{:S(2)}, u32[]{:S(2)}) collective-permute-start(bf16[2,48,384]{2,1,0:T(8,128)(2,1)S(1)} %pad_maximum_fusion.5), channel_id=1, source_target_pairs={{0,4},{1,5},{2,6},{3,7},{4,0},{5,1},{6,2},{7,3},{8,12},{9,13},{10,... | collective-permute-start | bytes 221192 | tf_op jit(solution)/shard_map/ppermute | solution.py:36
  62.6 6.2 %collective-permute-start.14 = (bf16[2,48,384]{2,1,0:T(8,128)(2,1)S(1)}, bf16[2,48,384]{2,1,0:T(8,128)(2,1)S(1)}, u32[]{:S(2)}, u32[]{:S(2)}) collective-permute-start(bf16[2,48,384]{2,1,0:T(8,128)(2,1)S(1)} %pad_maximum_fusion.4), channel_id=1, source_target_pairs={{0,2},{1,3},{2,4},{3,5},{4,6},{5,7},{6,0},{7,1},{8,10},{9,11},{10,... | collective-permute-start | bytes 221192 | tf_op jit(solution)/shard_map/ppermute | solution.py:36
  68.9 2.0 %local_gradients.1.local_ref = bf16[384,2816]{1,0:T(8,128)(2,1)S(1)} custom-call(bf16[384,1408]{1,0:T(8,128)(2,1)S(1)} %hidden_grad.1.dh_ref, bf16[2,48,2816]{2,1,0:T(8,128)(2,1)S(1)} %fusion.refs_0_, bf16[2,48,2816]{2,1,0:T(8,128)(2,1)S(1)} %collective-permute-done.8.refs_1_, bf16[2,48,2816]{2,1,0:T(8,128)(2,1)S(1)} %collective-permute-done.9.refs_2_, ...), custom_call_target="tpu_custom_call" | custom-call | tf_op jit(solution)/shard_map/local_gradients/pallas_call | solution.py:152
  70.9 12.8 %terms.1 = (bf16[4,48,4096]{2,1,0:T(8,128)(2,1)S(1)}, bf16[4,48,4096]{2,1,0:T(8,128)(2,1)S(1)}) custom-call(bf16[384,2816]{1,0:T(8,128)(2,1)S(1)} %local_gradients.1.local_ref, bf16[1408,4096]{1,0:T(8,128)(2,1)} %bitcast.85, bf16[1408,4096]{1,0:T(8,128)(2,1)} %bitcast.86), custom_call_target="tpu_custom_call" | custom-call | tf_op jit(solution)/shard_map/terms/pallas_call | solution.py:175
  83.8 3.4 %collective-permute-done.16 = bf16[4,48,4096]{2,1,0:T(8,128)(2,1)S(1)} collective-permute-done((bf16[4,48,4096]{2,1,0:T(8,128)(2,1)S(1)}, bf16[4,48,4096]{2,1,0:T(8,128)(2,1)S(1)}, u32[]{:S(2)}, u32[]{:S(2)}) %collective-permute-start.16) | collective-permute-done | bytes 1572896 | tf_op jit(solution)/shard_map/ppermute | solution.py:40
  87.5 10.1 %collective-permute-start.19 = (bf16[48,4096]{1,0:T(8,128)(2,1)S(1)}, bf16[48,4096]{1,0:T(8,128)(2,1)S(1)}, u32[]{:S(2)}, u32[]{:S(2)}) collective-permute-start(bf16[48,4096]{1,0:T(8,128)(2,1)S(1)} %get-tuple-element.31), channel_id=1, source_target_pairs={{0,6},{1,7},{2,0},{3,1},{4,2},{5,3},{6,4},{7,5},{8,14},{9,15},{10,... | collective-permute-start | bytes 1179656 | tf_op jit(solution)/shard_map/ppermute | solution.py:36
  97.5 1.3 collective-permute-start.17
  98.8 1.3 %collective-permute-start.18 = (bf16[48,4096]{1,0:T(8,128)(2,1)S(1)}, bf16[48,4096]{1,0:T(8,128)(2,1)S(1)}, u32[]{:S(2)}, u32[]{:S(2)}) collective-permute-start(bf16[48,4096]{1,0:T(8,128)(2,1)S(1)} %get-tuple-element.32), channel_id=1, source_target_pairs={{8,2},{9,3},{10,4},{11,5},{12,6},{13,7},{14,0},{15,1},{16,10},{17,... | collective-permute-start | bytes 1179656 | tf_op jit(solution)/shard_map/ppermute | solution.py:50
  100.1 6.1 %collective-permute-done.19 = bf16[48,4096]{1,0:T(8,128)(2,1)S(1)} collective-permute-done((bf16[48,4096]{1,0:T(8,128)(2,1)S(1)}, bf16[48,4096]{1,0:T(8,128)(2,1)S(1)}, u32[]{:S(2)}, u32[]{:S(2)}) %collective-permute-start.19) | collective-permute-done | bytes 393248 | tf_op jit(solution)/shard_map/ppermute | solution.py:36
  106.4 1.3 %collective-permute-start.20 = (bf16[48,4096]{1,0:T(8,128)(2,1)S(1)}, bf16[48,4096]{1,0:T(8,128)(2,1)S(1)}, u32[]{:S(2)}, u32[]{:S(2)}) collective-permute-start(bf16[48,4096]{1,0:T(8,128)(2,1)S(1)} %add_convert_fusion.1), channel_id=1, source_target_pairs={{8,6},{9,7},{10,0},{11,1},{12,2},{13,3},{14,4},{15,5},{16,14},{17,... | collective-permute-start | bytes 1179656 | tf_op jit(solution)/shard_map/ppermute | solution.py:50
  108.0 2.4 %block_sums.1 = bf16[3,128,128]{2,1,0:T(8,128)(2,1)} custom-call(s32[3]{0:T(128)S(1)} %select_reduce_fusion.cols_ref, bf16[4,48,4096]{2,1,0:T(8,128)(2,1)S(1)} %collective-permute-done.7.refs_4_.other_ref, bf16[48,4096]{1,0:T(8,128)(2,1)S(1)} %bitcast.79, bf16[48,4096]{1,0:T(8,128)(2,1)S(1)} %collective-permute-done.6.refs_1_, ...), custom_call_target="tpu_custom_call" | custom-call | tf_op jit(solution)/shard_map/block_sums/pallas_call | solution.py:199
  110.4 16.8 %collective-permute-done.17 = bf16[48,4096]{1,0:T(8,128)(2,1)S(1)} collective-permute-done((bf16[48,4096]{1,0:T(8,128)(2,1)S(1)}, bf16[48,4096]{1,0:T(8,128)(2,1)S(1)}, u32[]{:S(2)}, u32[]{:S(2)}) %collective-permute-start.17) | collective-permute-done | bytes 393248 | tf_op jit(solution)/shard_map/ppermute | solution.py:50
  127.2 0.9 fusion.7
  (58 shorter events, 6.7 us)
Async XLA Ops:
  0.6 17.2 %collective-permute-start.2 = (bf16[48,4096]{1,0:T(8,128)(2,1)}, bf16[48,4096]{1,0:T(8,128)(2,1)S(1)}, u32[]{:S(2)}, u32[]{:S(2)}) collective-permute-start(bf16[48,4096]{1,0:T(8,128)(2,1)} %bitcast.76), channel_id=1, source_target_pairs={{0,6},{1,7},{2,0},{3,1},{4,2},{5,3},{6,4},{7,5},{8,14},{9,15},{10,... | collective-permute-start | bytes 1179656 | tf_op jit(solution)/shard_map/ppermute | solution.py:36
  5.7 18.5 %collective-permute-start.1 = (bf16[48,4096]{1,0:T(8,128)(2,1)}, bf16[48,4096]{1,0:T(8,128)(2,1)S(1)}, u32[]{:S(2)}, u32[]{:S(2)}) collective-permute-start(bf16[48,4096]{1,0:T(8,128)(2,1)} %bitcast.77), channel_id=1, source_target_pairs={{0,2},{1,3},{2,4},{3,5},{4,6},{5,7},{6,0},{7,1},{8,10},{9,11},{10,... | collective-permute-start | bytes 1179656 | tf_op jit(solution)/shard_map/ppermute | solution.py:36
  5.7 1.2 copy-start
  7.0 1.2 copy-start.1
  8.2 0.7 copy-start.3
  8.9 0.7 copy-start.4
  12.3 20.3 %collective-permute-start.5 = (bf16[1,48,2816]{2,1,0:T(8,128)(2,1)}, bf16[1,48,2816]{2,1,0:T(8,128)(2,1)}, u32[]{:S(2)}, u32[]{:S(2)}) collective-permute-start(bf16[1,48,2816]{2,1,0:T(8,128)(2,1)} %slice.100), channel_id=1, source_target_pairs={{24,0},{25,1},{26,2},{27,3},{28,4},{29,5},{30,6},{31,7}} | collective-permute-start | bytes 811016 | tf_op jit(solution)/shard_map/ppermute | solution.py:50
  13.6 19.0 %collective-permute-start.4 = (bf16[1,48,2816]{2,1,0:T(8,128)(2,1)}, bf16[1,48,2816]{2,1,0:T(8,128)(2,1)}, u32[]{:S(2)}, u32[]{:S(2)}) collective-permute-start(bf16[1,48,2816]{2,1,0:T(8,128)(2,1)} %slice.100), channel_id=1, source_target_pairs={{16,0},{17,1},{18,2},{19,3},{20,4},{21,5},{22,6},{23,7}} | collective-permute-start | bytes 811016 | tf_op jit(solution)/shard_map/ppermute | solution.py:50
  15.0 17.1 %copy-start.2 = (bf16[1,48,4096]{2,1,0:T(8,128)(2,1)S(1)}, bf16[1,48,4096]{2,1,0:T(8,128)(2,1)}, u32[]{:S(2)}) copy-start(bf16[1,48,4096]{2,1,0:T(8,128)(2,1)} %param.9) | copy-start | bytes 1179652
  16.2 16.3 %collective-permute-start = (bf16[4,48,3200]{2,1,0:T(8,128)(2,1)}, bf16[4,48,3200]{2,1,0:T(8,128)(2,1)S(1)}, u32[]{:S(2)}, u32[]{:S(2)}) collective-permute-start(bf16[4,48,3200]{2,1,0:T(8,128)(2,1)} %pad_maximum_fusion.1), channel_id=1, source_target_pairs={{0,1},{1,0},{2,3},{3,2},{4,5},{5,4},{6,7},{7,6},{8,9},{9,8},{10,11... | collective-permute-start | bytes 3686408 | tf_op jit(solution)/shard_map/ppermute | solution.py:40
  17.8 14.3 %collective-permute-start.6 = (bf16[48,4096]{1,0:T(8,128)(2,1)S(1)}, bf16[48,4096]{1,0:T(8,128)(2,1)S(1)}, u32[]{:S(2)}, u32[]{:S(2)}) collective-permute-start(bf16[48,4096]{1,0:T(8,128)(2,1)S(1)} %collective-permute-done.2.refs_3_), channel_id=1, source_target_pairs={{0,6},{1,7},{2,0},{3,1},{4,2},{5,3},{6,4},{7,5},{8,14},{9,15},{10,... | collective-permute-start | bytes 1179656 | tf_op jit(solution)/shard_map/ppermute | solution.py:36
  24.3 9.0 %collective-permute-start.3 = (bf16[1,48,2816]{2,1,0:T(8,128)(2,1)}, bf16[1,48,2816]{2,1,0:T(8,128)(2,1)S(1)}, u32[]{:S(2)}, u32[]{:S(2)}) collective-permute-start(bf16[1,48,2816]{2,1,0:T(8,128)(2,1)} %slice.100), channel_id=1, source_target_pairs={{8,0},{9,1},{10,2},{11,3},{12,4},{13,5},{14,6},{15,7}} | collective-permute-start | bytes 811016 | tf_op jit(solution)/shard_map/ppermute | solution.py:50
  32.3 11.1 %collective-permute-start.7 = (bf16[4,48,4096]{2,1,0:T(8,128)(2,1)S(1)}, bf16[4,48,4096]{2,1,0:T(8,128)(2,1)S(1)}, u32[]{:S(2)}, u32[]{:S(2)}) collective-permute-start(bf16[4,48,4096]{2,1,0:T(8,128)(2,1)S(1)} %pad_maximum_fusion), channel_id=1, source_target_pairs={{0,1},{1,0},{2,3},{3,2},{4,5},{5,4},{6,7},{7,6},{8,9},{9,8},{10,11... | collective-permute-start | bytes 4718600 | tf_op jit(solution)/shard_map/ppermute | solution.py:40
  34.5 18.5 %collective-permute-start.12 = (bf16[1,48,2816]{2,1,0:T(8,128)(2,1)S(1)}, bf16[1,48,2816]{2,1,0:T(8,128)(2,1)S(1)}, u32[]{:S(2)}, u32[]{:S(2)}) collective-permute-start(bf16[1,48,2816]{2,1,0:T(8,128)(2,1)S(1)} %get-tuple-element.17), channel_id=1, source_target_pairs={{0,12},{1,13},{2,14},{3,15},{4,8},{5,9},{6,10},{7,11},{16,20},{17,... | collective-permute-start | bytes 811016 | tf_op jit(solution)/shard_map/ppermute | solution.py:50
  36.2 26.4 %collective-permute-start.11 = (bf16[1,48,2816]{2,1,0:T(8,128)(2,1)S(1)}, bf16[1,48,2816]{2,1,0:T(8,128)(2,1)S(1)}, u32[]{:S(2)}, u32[]{:S(2)}) collective-permute-start(bf16[1,48,2816]{2,1,0:T(8,128)(2,1)S(1)} %get-tuple-element.18), channel_id=1, source_target_pairs={{0,20},{1,21},{2,22},{3,23},{4,16},{5,17},{6,18},{7,19},{24,28},{2... | collective-permute-start | bytes 811016 | tf_op jit(solution)/shard_map/ppermute | solution.py:50
  40.9 27.9 %collective-permute-start.10 = (bf16[1,48,2816]{2,1,0:T(8,128)(2,1)S(1)}, bf16[1,48,2816]{2,1,0:T(8,128)(2,1)S(1)}, u32[]{:S(2)}, u32[]{:S(2)}) collective-permute-start(bf16[1,48,2816]{2,1,0:T(8,128)(2,1)S(1)} %get-tuple-element.19), channel_id=1, source_target_pairs={{0,28},{1,29},{2,30},{3,31},{4,24},{5,25},{6,26},{7,27},{8,12},{9,... | collective-permute-start | bytes 811016 | tf_op jit(solution)/shard_map/ppermute | solution.py:50
  42.6 26.3 %collective-permute-start.8 = (bf16[2,48,2816]{2,1,0:T(8,128)(2,1)S(1)}, bf16[2,48,2816]{2,1,0:T(8,128)(2,1)S(1)}, u32[]{:S(2)}, u32[]{:S(2)}) collective-permute-start(bf16[2,48,2816]{2,1,0:T(8,128)(2,1)S(1)} %fusion.2), channel_id=1, source_target_pairs={{8,10},{9,11},{10,12},{11,13},{12,14},{13,15},{14,8},{15,9},{16,18... | collective-permute-start | bytes 1622024 | tf_op jit(solution)/shard_map/ppermute | solution.py:50
  43.4 25.5 %collective-permute-start.9 = (bf16[2,48,2816]{2,1,0:T(8,128)(2,1)S(1)}, bf16[2,48,2816]{2,1,0:T(8,128)(2,1)S(1)}, u32[]{:S(2)}, u32[]{:S(2)}) collective-permute-start(bf16[2,48,2816]{2,1,0:T(8,128)(2,1)S(1)} %fusion.1), channel_id=1, source_target_pairs={{8,14},{9,15},{10,8},{11,9},{12,10},{13,11},{14,12},{15,13},{16,22... | collective-permute-start | bytes 1622024 | tf_op jit(solution)/shard_map/ppermute | solution.py:50
  52.9 30.7 %collective-permute-start.13 = (bf16[2,48,384]{2,1,0:T(8,128)(2,1)S(1)}, bf16[2,48,384]{2,1,0:T(8,128)(2,1)S(1)}, u32[]{:S(2)}, u32[]{:S(2)}) collective-permute-start(bf16[2,48,384]{2,1,0:T(8,128)(2,1)S(1)} %pad_maximum_fusion.5), channel_id=1, source_target_pairs={{0,4},{1,5},{2,6},{3,7},{4,0},{5,1},{6,2},{7,3},{8,12},{9,13},{10,... | collective-permute-start | bytes 221192 | tf_op jit(solution)/shard_map/ppermute | solution.py:36
  62.6 21.1 %collective-permute-start.14 = (bf16[2,48,384]{2,1,0:T(8,128)(2,1)S(1)}, bf16[2,48,384]{2,1,0:T(8,128)(2,1)S(1)}, u32[]{:S(2)}, u32[]{:S(2)}) collective-permute-start(bf16[2,48,384]{2,1,0:T(8,128)(2,1)S(1)} %pad_maximum_fusion.4), channel_id=1, source_target_pairs={{0,2},{1,3},{2,4},{3,5},{4,6},{5,7},{6,0},{7,1},{8,10},{9,11},{10,... | collective-permute-start | bytes 221192 | tf_op jit(solution)/shard_map/ppermute | solution.py:36
  68.8 14.9 %collective-permute-start.15 = (bf16[2,48,384]{2,1,0:T(8,128)(2,1)S(1)}, bf16[2,48,384]{2,1,0:T(8,128)(2,1)S(1)}, u32[]{:S(2)}, u32[]{:S(2)}) collective-permute-start(bf16[2,48,384]{2,1,0:T(8,128)(2,1)S(1)} %pad_maximum_fusion.3), channel_id=1, source_target_pairs={{0,6},{1,7},{2,0},{3,1},{4,2},{5,3},{6,4},{7,5},{8,14},{9,15},{10,... | collective-permute-start | bytes 221192 | tf_op jit(solution)/shard_map/ppermute | solution.py:36
  83.7 3.5 %collective-permute-start.16 = (bf16[4,48,4096]{2,1,0:T(8,128)(2,1)S(1)}, bf16[4,48,4096]{2,1,0:T(8,128)(2,1)S(1)}, u32[]{:S(2)}, u32[]{:S(2)}) collective-permute-start(bf16[4,48,4096]{2,1,0:T(8,128)(2,1)S(1)} %get-tuple-element.26), channel_id=1, source_target_pairs={{0,1},{1,0},{2,3},{3,2},{4,5},{5,4},{6,7},{7,6},{8,9},{9,8},{10,11... | collective-permute-start | bytes 4718600 | tf_op jit(solution)/shard_map/ppermute | solution.py:40
  87.5 20.2 %copy-start.5 = (s32[1,16]{1,0:T(1,128)S(1)}, s32[1,16]{1,0:T(1,128)}, u32[]{:S(2)}) copy-start(s32[1,16]{1,0:T(1,128)} %param.17) | copy-start | bytes 196
  87.5 20.3 %copy-start.6 = (s32[1,16]{1,0:T(1,128)S(1)}, s32[1,16]{1,0:T(1,128)}, u32[]{:S(2)}) copy-start(s32[1,16]{1,0:T(1,128)} %param.16) | copy-start | bytes 196
  87.5 18.7 %collective-permute-start.19 = (bf16[48,4096]{1,0:T(8,128)(2,1)S(1)}, bf16[48,4096]{1,0:T(8,128)(2,1)S(1)}, u32[]{:S(2)}, u32[]{:S(2)}) collective-permute-start(bf16[48,4096]{1,0:T(8,128)(2,1)S(1)} %get-tuple-element.31), channel_id=1, source_target_pairs={{0,6},{1,7},{2,0},{3,1},{4,2},{5,3},{6,4},{7,5},{8,14},{9,15},{10,... | collective-permute-start | bytes 1179656 | tf_op jit(solution)/shard_map/ppermute | solution.py:36
  97.5 29.6 %collective-permute-start.17 = (bf16[48,4096]{1,0:T(8,128)(2,1)S(1)}, bf16[48,4096]{1,0:T(8,128)(2,1)S(1)}, u32[]{:S(2)}, u32[]{:S(2)}) collective-permute-start(bf16[48,4096]{1,0:T(8,128)(2,1)S(1)} %get-tuple-element.30), channel_id=1, source_target_pairs={{8,0},{9,1},{10,2},{11,3},{12,4},{13,5},{14,6},{15,7},{16,8},{17,9... | collective-permute-start | bytes 1179656 | tf_op jit(solution)/shard_map/ppermute | solution.py:50
  98.8 28.3 %collective-permute-start.18 = (bf16[48,4096]{1,0:T(8,128)(2,1)S(1)}, bf16[48,4096]{1,0:T(8,128)(2,1)S(1)}, u32[]{:S(2)}, u32[]{:S(2)}) collective-permute-start(bf16[48,4096]{1,0:T(8,128)(2,1)S(1)} %get-tuple-element.32), channel_id=1, source_target_pairs={{8,2},{9,3},{10,4},{11,5},{12,6},{13,7},{14,0},{15,1},{16,10},{17,... | collective-permute-start | bytes 1179656 | tf_op jit(solution)/shard_map/ppermute | solution.py:50
  106.4 20.8 %collective-permute-start.20 = (bf16[48,4096]{1,0:T(8,128)(2,1)S(1)}, bf16[48,4096]{1,0:T(8,128)(2,1)S(1)}, u32[]{:S(2)}, u32[]{:S(2)}) collective-permute-start(bf16[48,4096]{1,0:T(8,128)(2,1)S(1)} %add_convert_fusion.1), channel_id=1, source_target_pairs={{8,6},{9,7},{10,0},{11,1},{12,2},{13,3},{14,4},{15,5},{16,14},{17,... | collective-permute-start | bytes 1179656 | tf_op jit(solution)/shard_map/ppermute | solution.py:50

commit v5 on v4

--- a/solution.py
+++ b/solution.py
@@ -137,9 +137,9 @@
     units = dh_ref.shape[1]
     rows = given[0].shape[1]
     padded = given[0].shape[2] // 2
-    for b, (i, f) in enumerate(blocks):
+    for b, (block, i, f) in enumerate(blocks):
         part = slice(b * rows, (b + 1) * rows)
-        wide = dh_ref[part, :].astype(jnp.float32)
+        wide = dh_ref[block * rows : (block + 1) * rows, :].astype(jnp.float32)
         gate = given[i][f, :, :units].astype(jnp.float32)
         up = given[i][f, :, padded : padded + units].astype(jnp.float32)
         activated, slope = gelu_pair(gate)
@@ -148,7 +148,7 @@
 
 
 def local_gradients(dhidden, given, blocks):
-    rows, units = dhidden.shape
+    rows, units = len(blocks) * given[0].shape[1], dhidden.shape[1]
     return pl.pallas_call(
         functools.partial(gradients_kernel, blocks),
         in_specs=[pl.BlockSpec(memory_space=pltpu.VMEM)] * (1 + len(given)),
@@ -160,29 +160,32 @@
     )(dhidden, *given)
 
 
-def term_kernel(local_ref, wg_ref, wu_ref, same_ref, other_ref):
+def term_kernel(near_ref, far_ref, wg_ref, wu_ref, same_ref, other_ref):
     weight = jnp.concatenate([wg_ref[...], wu_ref[...]], axis=0)
-    term = jnp.dot(local_ref[...], weight, preferred_element_type=jnp.float32)
-    term = term.astype(jnp.bfloat16).reshape(2, *same_ref.shape)
-    same_ref[...] = term[0]
-    other_ref[...] = term[1]
-
-
-def terms(local, w_gate, w_up, chips, first, width):
-    rows, units = local.shape[0], w_gate.shape[0]
+    local = jnp.concatenate([near_ref[...], far_ref[...]], axis=0)
+    term = jnp.dot(local, weight, preferred_element_type=jnp.float32).astype(jnp.bfloat16)
+    chips, rows, tile = same_ref.shape
+    near = near_ref.shape[0]
+    for f, ref in enumerate((same_ref, other_ref)):
+        ref[: chips - 1] = term[f * near // 2 : (f + 1) * near // 2].reshape(chips - 1, rows, tile)
+        ref[chips - 1] = term[near + f * rows : near + (f + 1) * rows]
+
+
+def terms(near, far, w_gate, w_up, chips, first, width):
+    units = w_gate.shape[0]
     tile = 8 * LANES
-    out = (chips, rows // (2 * chips))
+    out = (chips, far.shape[0] // 2)
     return pl.pallas_call(
         term_kernel,
         grid=(width // tile,),
-        in_specs=[pl.BlockSpec((rows, 2 * units), lambda i: (0, 0))]
+        in_specs=[pl.BlockSpec(near.shape, lambda i: (0, 0)), pl.BlockSpec(far.shape, lambda i: (0, 0))]
         + [pl.BlockSpec((units, tile), lambda i: (0, i + first // tile))] * 2,
         out_specs=[pl.BlockSpec(out + (tile,), lambda i: (0, 0, i))] * 2,
         out_shape=[jax.ShapeDtypeStruct(out + (width,), jnp.bfloat16)] * 2,
         compiler_params=pltpu.CompilerParams(vmem_limit_bytes=VMEM),
         cost_estimate=COST,
         name="terms",
-    )(local, w_gate, w_up)
+    )(near, far, w_gate, w_up)
 
 
 def block_kernel(scale, cols_ref, other_ref, *refs):
@@ -269,7 +272,7 @@
 
     far = chips // 2
     needed = range(1, sections)
-    order = [0] + list(range(chips - 2, 0, -1)) + ([chips - 1] if chips > 2 else [])
+    order = [r for r in range(chips) if r != far] + [far]
     passing = {s: moved(columns[far][:1], [(s, 0, 0)]) for s in needed}
     sent, arrived = [], {0: columns[0]}
     for r in order[1:]:
@@ -283,15 +286,11 @@
         sent.append(after(value, same[1], same[chips - 1]))
         value = moved(sent[-1], [(0, through, far), (direct, direct, far)])
         halves = [jnp.where(section == s, value, half) for s, half in zip((through, direct), halves)]
-    given = [arrived[r] for r in order if r != far] + halves
-    blocks = []
-    for f in range(2):
-        nth = iter(range(chips))
-        blocks += [(chips - 1 + f, 0) if r == far else (next(nth), f) for r in order]
-
     other = swapped(jnp.stack([same[r] for r in order]))
     dhidden = hidden_grad([after(same[0], *sent)] + [same[r] for r in order[1:]], other, w_down)
-    local = local_gradients(dhidden, given, blocks)
+    near = [(f * chips + i, i, f) for f in range(2) for i in range(chips - 1)]
+    near = local_gradients(dhidden, [arrived[r] for r in order[:-1]], near)
+    last = local_gradients(dhidden, halves, [(f * chips + chips - 1, f, 0) for f in range(2)])
     hidden = [both[0][:, :, :skip]]
     hidden += [rotated(after(both[r][:, :, :skip], dhidden), r) for r in order[1:]]
 
@@ -299,7 +298,7 @@
     width = mine.shape[1] // parts
     pieces, earlier = [], hidden[1:]
     for part in range(parts):
-        kept, passed = terms(local, w_gate, w_up, chips, part * width, width)
+        kept, passed = terms(near, last, w_gate, w_up, chips, part * width, width)
         passed = swapped(after(passed, *earlier) if earlier else passed)
         sums = {r: summed(kept[i], passed[i]) for i, r in enumerate(order)}
         total, running = [relayed(sums[0], 0)], None

time: 129 us -> 128 us (level)
  starting transfers between devices: 52.3 us -> 50.5 us
    ppermute x7, starting transfers between devices: 34.9 us -> 33.1 us  [rotated(): return lax.ppermute(value, 'dp', pairs)]
    ppermute x7, waiting for transfers between devices: 14.4 us -> 15.7 us  [rotated(): return lax.ppermute(value, 'dp', pairs)]
  transfers between devices with their start and end apart: 21 -> 21, of which waited for: 6 -> 7; matrix products, arithmetic and copies ran while one was open for 6% -> 6% of each run, Pallas kernels for 21% -> 21%
where the time goes in v5:
time: 128 us; the launch traced here: 127 us
  starting transfers between devices  50.5 us (39%)
  waiting for transfers between devices  36 us (28%)
  Pallas kernels  27.1 us (21%)
  other arithmetic  6.86 us (5%)
  local copies, waits for them, and re-layouts  5.65 us (4%)
    ppermute x7, starting transfers between devices, rotated(): return lax.ppermute(value, 'dp', pairs)  33.1 us
    ppermute x11, starting transfers between devices, moved(): return lax.ppermute(value, ('section', 'dp'), pairs)  17.2 us
    ppermute x11, waiting for transfers between devices, moved(): return lax.ppermute(value, ('section', 'dp'), pairs)  16.9 us
    ppermute x7, waiting for transfers between devices, rotated(): return lax.ppermute(value, 'dp', pairs)  15.7 us
    pallas_call x1, Pallas kernels, terms(): pl.pallas_call(term_kernel, grid=(width // tile,), in_specs=[pl.BlockSpec...  12.9 us
    pallas_call x1, Pallas kernels, hidden_grad(): pl.pallas_call(hidden_grad_kernel, grid=(width // tile,), in_specs=[pl.Bl...  8.83 us
    unnamed x14, local copies, waits for them, and re-layouts  3.8 us
    ppermute x3, waiting for transfers between devices, swapped(): lax.ppermute(value, 'dp', [(i, i ^ 1) for i in range(lax.axis_size('dp'))])  3.4 us
  transfers between devices with their start and end apart: 21, of which 7 were waited for; matrix products, arithmetic and copies ran while one was open for 6% of the time, Pallas kernels for 21%

profile of v5, /device:TPU:0, one launch (start us, length us, event | category | flops | bytes accessed | tf_op | source)
XLA Modules:
  0.0 127.1 jit_solution(12722202144518791267)
XLA Ops:
  0.6 5.1 %collective-permute-start.2 = (bf16[48,4096]{1,0:T(8,128)(2,1)}, bf16[48,4096]{1,0:T(8,128)(2,1)S(1)}, u32[]{:S(2)}, u32[]{:S(2)}) collective-permute-start(bf16[48,4096]{1,0:T(8,128)(2,1)} %bitcast.76), channel_id=1, source_target_pairs={{0,6},{1,7},{2,0},{3,1},{4,2},{5,3},{6,4},{7,5},{8,14},{9,15},{10,... | collective-permute-start | bytes 1179656 | tf_op jit(solution)/shard_map/ppermute | solution.py:36
  5.7 1.2 copy-done
  7.0 1.2 copy-done.1
  9.5 0.9 hidden_blocks.1
  12.3 1.3 %collective-permute-start.5 = (bf16[1,48,2816]{2,1,0:T(8,128)(2,1)}, bf16[1,48,2816]{2,1,0:T(8,128)(2,1)}, u32[]{:S(2)}, u32[]{:S(2)}) collective-permute-start(bf16[1,48,2816]{2,1,0:T(8,128)(2,1)} %slice.100), channel_id=1, source_target_pairs={{24,0},{25,1},{26,2},{27,3},{28,4},{29,5},{30,6},{31,7}} | collective-permute-start | bytes 811016 | tf_op jit(solution)/shard_map/ppermute | solution.py:50
  13.6 1.3 %collective-permute-start.4 = (bf16[1,48,2816]{2,1,0:T(8,128)(2,1)}, bf16[1,48,2816]{2,1,0:T(8,128)(2,1)}, u32[]{:S(2)}, u32[]{:S(2)}) collective-permute-start(bf16[1,48,2816]{2,1,0:T(8,128)(2,1)} %slice.100), channel_id=1, source_target_pairs={{16,0},{17,1},{18,2},{19,3},{20,4},{21,5},{22,6},{23,7}} | collective-permute-start | bytes 811016 | tf_op jit(solution)/shard_map/ppermute | solution.py:50
  15.0 1.2 pad_maximum_fusion.1
  16.2 0.8 maximum_bitcast_fusion.7
  17.0 0.8 maximum_bitcast_fusion.5
  17.8 3.9 %collective-permute-start.6 = (bf16[48,4096]{1,0:T(8,128)(2,1)S(1)}, bf16[48,4096]{1,0:T(8,128)(2,1)S(1)}, u32[]{:S(2)}, u32[]{:S(2)}) collective-permute-start(bf16[48,4096]{1,0:T(8,128)(2,1)S(1)} %collective-permute-done.2.refs_2_), channel_id=1, source_target_pairs={{0,6},{1,7},{2,0},{3,1},{4,2},{5,3},{6,4},{7,5},{8,14},{9,15},{10,... | collective-permute-start | bytes 1179656 | tf_op jit(solution)/shard_map/ppermute | solution.py:36
  22.5 1.8 %collective-permute-done.1.refs_1_ = bf16[48,4096]{1,0:T(8,128)(2,1)S(1)} collective-permute-done((bf16[48,4096]{1,0:T(8,128)(2,1)}, bf16[48,4096]{1,0:T(8,128)(2,1)S(1)}, u32[]{:S(2)}, u32[]{:S(2)}) %collective-permute-start.1) | collective-permute-done | bytes 393248 | tf_op jit(solution)/shard_map/ppermute | solution.py:36
  24.3 1.3 %collective-permute-start.3 = (bf16[1,48,2816]{2,1,0:T(8,128)(2,1)}, bf16[1,48,2816]{2,1,0:T(8,128)(2,1)S(1)}, u32[]{:S(2)}, u32[]{:S(2)}) collective-permute-start(bf16[1,48,2816]{2,1,0:T(8,128)(2,1)} %slice.100), channel_id=1, source_target_pairs={{8,0},{9,1},{10,2},{11,3},{12,4},{13,5},{14,6},{15,7}} | collective-permute-start | bytes 811016 | tf_op jit(solution)/shard_map/ppermute | solution.py:50
  25.5 6.6 %collective-permute-done.6.refs_3_ = bf16[48,4096]{1,0:T(8,128)(2,1)S(1)} collective-permute-done((bf16[48,4096]{1,0:T(8,128)(2,1)S(1)}, bf16[48,4096]{1,0:T(8,128)(2,1)S(1)}, u32[]{:S(2)}, u32[]{:S(2)}) %collective-permute-start.6) | collective-permute-done | bytes 393248 | tf_op jit(solution)/shard_map/ppermute | solution.py:36
  33.2 1.1 broadcast_select_fusion
  34.5 1.7 %collective-permute-start.12 = (bf16[1,48,2816]{2,1,0:T(8,128)(2,1)S(1)}, bf16[1,48,2816]{2,1,0:T(8,128)(2,1)S(1)}, u32[]{:S(2)}, u32[]{:S(2)}) collective-permute-start(bf16[1,48,2816]{2,1,0:T(8,128)(2,1)S(1)} %get-tuple-element.17), channel_id=1, source_target_pairs={{0,12},{1,13},{2,14},{3,15},{4,8},{5,9},{6,10},{7,11},{16,20},{17,... | collective-permute-start | bytes 811016 | tf_op jit(solution)/shard_map/ppermute | solution.py:50
  36.2 4.7 %collective-permute-start.11 = (bf16[1,48,2816]{2,1,0:T(8,128)(2,1)S(1)}, bf16[1,48,2816]{2,1,0:T(8,128)(2,1)S(1)}, u32[]{:S(2)}, u32[]{:S(2)}) collective-permute-start(bf16[1,48,2816]{2,1,0:T(8,128)(2,1)S(1)} %get-tuple-element.18), channel_id=1, source_target_pairs={{0,20},{1,21},{2,22},{3,23},{4,16},{5,17},{6,18},{7,19},{24,28},{2... | collective-permute-start | bytes 811016 | tf_op jit(solution)/shard_map/ppermute | solution.py:50
  40.9 1.6 %collective-permute-start.10 = (bf16[1,48,2816]{2,1,0:T(8,128)(2,1)S(1)}, bf16[1,48,2816]{2,1,0:T(8,128)(2,1)S(1)}, u32[]{:S(2)}, u32[]{:S(2)}) collective-permute-start(bf16[1,48,2816]{2,1,0:T(8,128)(2,1)S(1)} %get-tuple-element.19), channel_id=1, source_target_pairs={{0,28},{1,29},{2,30},{3,31},{4,24},{5,25},{6,26},{7,27},{8,12},{9,... | collective-permute-start | bytes 811016 | tf_op jit(solution)/shard_map/ppermute | solution.py:50
  44.1 8.8 %hidden_grad.1.dh_ref = bf16[384,1408]{1,0:T(8,128)(2,1)S(1)} custom-call(bf16[48,4096]{1,0:T(8,128)(2,1)S(1)} %bitcast.78, bf16[48,4096]{1,0:T(8,128)(2,1)S(1)} %collective-permute-done.1.refs_1_, bf16[48,4096]{1,0:T(8,128)(2,1)S(1)} %collective-permute-done.2.refs_2_, bf16[48,4096]{1,0:T(8,128)(2,1)S(1)} %collective-permute-done.6.refs_3_, ...), custom_call_target="tpu_custom_call" | custom-call | tf_op jit(solution)/shard_map/hidden_grad/pallas_call | solution.py:121
  52.9 8.5 %collective-permute-start.13 = (bf16[2,48,384]{2,1,0:T(8,128)(2,1)S(1)}, bf16[2,48,384]{2,1,0:T(8,128)(2,1)S(1)}, u32[]{:S(2)}, u32[]{:S(2)}) collective-permute-start(bf16[2,48,384]{2,1,0:T(8,128)(2,1)S(1)} %pad_maximum_fusion.5), channel_id=1, source_target_pairs={{0,2},{1,3},{2,4},{3,5},{4,6},{5,7},{6,0},{7,1},{8,10},{9,11},{10,... | collective-permute-start | bytes 221192 | tf_op jit(solution)/shard_map/ppermute | solution.py:36
  61.4 14.4 %collective-permute-start.15 = (bf16[2,48,384]{2,1,0:T(8,128)(2,1)S(1)}, bf16[2,48,384]{2,1,0:T(8,128)(2,1)S(1)}, u32[]{:S(2)}, u32[]{:S(2)}) collective-permute-start(bf16[2,48,384]{2,1,0:T(8,128)(2,1)S(1)} %pad_maximum_fusion.3), channel_id=1, source_target_pairs={{0,4},{1,5},{2,6},{3,7},{4,0},{5,1},{6,2},{7,3},{8,12},{9,13},{10,... | collective-permute-start | bytes 221192 | tf_op jit(solution)/shard_map/ppermute | solution.py:36
  76.4 1.5 %local_gradients.2.near_ref = bf16[288,2816]{1,0:T(8,128)(2,1)S(1)} custom-call(bf16[384,1408]{1,0:T(8,128)(2,1)S(1)} %hidden_grad.1.dh_ref, bf16[2,48,2816]{2,1,0:T(8,128)(2,1)S(1)} %fusion.refs_0_, bf16[2,48,2816]{2,1,0:T(8,128)(2,1)S(1)} %collective-permute-done.8.refs_1_, bf16[2,48,2816]{2,1,0:T(8,128)(2,1)S(1)} %collective-permute-done.9.refs_2_), custom_call_target="tpu_custom_call" | custom-call | tf_op jit(solution)/shard_map/local_gradients/pallas_call | solution.py:152
  77.9 12.9 %terms.1 = (bf16[4,48,4096]{2,1,0:T(8,128)(2,1)S(1)}, bf16[4,48,4096]{2,1,0:T(8,128)(2,1)S(1)}) custom-call(bf16[288,2816]{1,0:T(8,128)(2,1)S(1)} %local_gradients.2.near_ref, bf16[96,2816]{1,0:T(8,128)(2,1)S(1)} %local_gradients.3.far_ref, bf16[1408,4096]{1,0:T(8,128)(2,1)} %bitcast.85, bf16[1408,4096]{1,0:T(8,128)(2,1)} %bitcast.86), custom_call_target="tpu_custom_call" | custom-call | tf_op jit(solution)/shard_map/terms/pallas_call | solution.py:178
  90.9 3.4 %collective-permute-done.16 = bf16[4,48,4096]{2,1,0:T(8,128)(2,1)S(1)} collective-permute-done((bf16[4,48,4096]{2,1,0:T(8,128)(2,1)S(1)}, bf16[4,48,4096]{2,1,0:T(8,128)(2,1)S(1)}, u32[]{:S(2)}, u32[]{:S(2)}) %collective-permute-start.16) | collective-permute-done | bytes 1572896 | tf_op jit(solution)/shard_map/ppermute | solution.py:40
  94.6 1.2 collective-permute-start.19
  95.9 1.3 %collective-permute-start.17 = (bf16[48,4096]{1,0:T(8,128)(2,1)S(1)}, bf16[48,4096]{1,0:T(8,128)(2,1)S(1)}, u32[]{:S(2)}, u32[]{:S(2)}) collective-permute-start(bf16[48,4096]{1,0:T(8,128)(2,1)S(1)} %get-tuple-element.30), channel_id=1, source_target_pairs={{8,0},{9,1},{10,2},{11,3},{12,4},{13,5},{14,6},{15,7},{16,8},{17,9... | collective-permute-start | bytes 1179656 | tf_op jit(solution)/shard_map/ppermute | solution.py:50
  97.2 1.3 %collective-permute-start.18 = (bf16[48,4096]{1,0:T(8,128)(2,1)S(1)}, bf16[48,4096]{1,0:T(8,128)(2,1)S(1)}, u32[]{:S(2)}, u32[]{:S(2)}) collective-permute-start(bf16[48,4096]{1,0:T(8,128)(2,1)S(1)} %get-tuple-element.32), channel_id=1, source_target_pairs={{8,2},{9,3},{10,4},{11,5},{12,6},{13,7},{14,0},{15,1},{16,10},{17,... | collective-permute-start | bytes 1179656 | tf_op jit(solution)/shard_map/ppermute | solution.py:50
  98.5 7.4 %collective-permute-done.19 = bf16[48,4096]{1,0:T(8,128)(2,1)S(1)} collective-permute-done((bf16[48,4096]{1,0:T(8,128)(2,1)S(1)}, bf16[48,4096]{1,0:T(8,128)(2,1)S(1)}, u32[]{:S(2)}, u32[]{:S(2)}) %collective-permute-start.19) | collective-permute-done | bytes 393248 | tf_op jit(solution)/shard_map/ppermute | solution.py:36
  106.0 1.3 %collective-permute-start.20 = (bf16[48,4096]{1,0:T(8,128)(2,1)S(1)}, bf16[48,4096]{1,0:T(8,128)(2,1)S(1)}, u32[]{:S(2)}, u32[]{:S(2)}) collective-permute-start(bf16[48,4096]{1,0:T(8,128)(2,1)S(1)} %add_convert_fusion.1), channel_id=1, source_target_pairs={{8,6},{9,7},{10,0},{11,1},{12,2},{13,3},{14,4},{15,5},{16,14},{17,... | collective-permute-start | bytes 1179656 | tf_op jit(solution)/shard_map/ppermute | solution.py:50
  107.6 2.4 %block_sums.1 = bf16[3,128,128]{2,1,0:T(8,128)(2,1)} custom-call(s32[3]{0:T(128)S(1)} %select_reduce_fusion.cols_ref, bf16[4,48,4096]{2,1,0:T(8,128)(2,1)S(1)} %collective-permute-done.7.refs_4_.other_ref, bf16[48,4096]{1,0:T(8,128)(2,1)S(1)} %bitcast.79, bf16[48,4096]{1,0:T(8,128)(2,1)S(1)} %collective-permute-done.1.refs_1_, ...), custom_call_target="tpu_custom_call" | custom-call | tf_op jit(solution)/shard_map/block_sums/pallas_call | solution.py:202
  110.0 8.3 %collective-permute-done.18 = bf16[48,4096]{1,0:T(8,128)(2,1)S(1)} collective-permute-done((bf16[48,4096]{1,0:T(8,128)(2,1)S(1)}, bf16[48,4096]{1,0:T(8,128)(2,1)S(1)}, u32[]{:S(2)}, u32[]{:S(2)}) %collective-permute-start.18) | collective-permute-done | bytes 393248 | tf_op jit(solution)/shard_map/ppermute | solution.py:50
  118.3 8.0 %collective-permute-done.20 = bf16[48,4096]{1,0:T(8,128)(2,1)S(1)} collective-permute-done((bf16[48,4096]{1,0:T(8,128)(2,1)S(1)}, bf16[48,4096]{1,0:T(8,128)(2,1)S(1)}, u32[]{:S(2)}, u32[]{:S(2)}) %collective-permute-start.20) | collective-permute-done | bytes 393248 | tf_op jit(solution)/shard_map/ppermute | solution.py:50
  126.3 0.9 fusion.7
  (59 shorter events, 8.0 us)
Async XLA Ops:
  0.6 17.2 %collective-permute-start.2 = (bf16[48,4096]{1,0:T(8,128)(2,1)}, bf16[48,4096]{1,0:T(8,128)(2,1)S(1)}, u32[]{:S(2)}, u32[]{:S(2)}) collective-permute-start(bf16[48,4096]{1,0:T(8,128)(2,1)} %bitcast.76), channel_id=1, source_target_pairs={{0,6},{1,7},{2,0},{3,1},{4,2},{5,3},{6,4},{7,5},{8,14},{9,15},{10,... | collective-permute-start | bytes 1179656 | tf_op jit(solution)/shard_map/ppermute | solution.py:36
  5.7 18.5 %collective-permute-start.1 = (bf16[48,4096]{1,0:T(8,128)(2,1)}, bf16[48,4096]{1,0:T(8,128)(2,1)S(1)}, u32[]{:S(2)}, u32[]{:S(2)}) collective-permute-start(bf16[48,4096]{1,0:T(8,128)(2,1)} %bitcast.77), channel_id=1, source_target_pairs={{0,2},{1,3},{2,4},{3,5},{4,6},{5,7},{6,0},{7,1},{8,10},{9,11},{10,... | collective-permute-start | bytes 1179656 | tf_op jit(solution)/shard_map/ppermute | solution.py:36
  5.7 1.2 copy-start
  7.0 1.2 copy-start.1
  8.2 0.7 copy-start.3
  8.9 0.7 copy-start.4
  12.3 20.3 %collective-permute-start.5 = (bf16[1,48,2816]{2,1,0:T(8,128)(2,1)}, bf16[1,48,2816]{2,1,0:T(8,128)(2,1)}, u32[]{:S(2)}, u32[]{:S(2)}) collective-permute-start(bf16[1,48,2816]{2,1,0:T(8,128)(2,1)} %slice.100), channel_id=1, source_target_pairs={{24,0},{25,1},{26,2},{27,3},{28,4},{29,5},{30,6},{31,7}} | collective-permute-start | bytes 811016 | tf_op jit(solution)/shard_map/ppermute | solution.py:50
  13.6 19.0 %collective-permute-start.4 = (bf16[1,48,2816]{2,1,0:T(8,128)(2,1)}, bf16[1,48,2816]{2,1,0:T(8,128)(2,1)}, u32[]{:S(2)}, u32[]{:S(2)}) collective-permute-start(bf16[1,48,2816]{2,1,0:T(8,128)(2,1)} %slice.100), channel_id=1, source_target_pairs={{16,0},{17,1},{18,2},{19,3},{20,4},{21,5},{22,6},{23,7}} | collective-permute-start | bytes 811016 | tf_op jit(solution)/shard_map/ppermute | solution.py:50
  15.0 17.1 %copy-start.2 = (bf16[1,48,4096]{2,1,0:T(8,128)(2,1)S(1)}, bf16[1,48,4096]{2,1,0:T(8,128)(2,1)}, u32[]{:S(2)}) copy-start(bf16[1,48,4096]{2,1,0:T(8,128)(2,1)} %param.9) | copy-start | bytes 1179652
  16.2 16.3 %collective-permute-start = (bf16[4,48,3200]{2,1,0:T(8,128)(2,1)}, bf16[4,48,3200]{2,1,0:T(8,128)(2,1)S(1)}, u32[]{:S(2)}, u32[]{:S(2)}) collective-permute-start(bf16[4,48,3200]{2,1,0:T(8,128)(2,1)} %pad_maximum_fusion.1), channel_id=1, source_target_pairs={{0,1},{1,0},{2,3},{3,2},{4,5},{5,4},{6,7},{7,6},{8,9},{9,8},{10,11... | collective-permute-start | bytes 3686408 | tf_op jit(solution)/shard_map/ppermute | solution.py:40
  17.8 14.3 %collective-permute-start.6 = (bf16[48,4096]{1,0:T(8,128)(2,1)S(1)}, bf16[48,4096]{1,0:T(8,128)(2,1)S(1)}, u32[]{:S(2)}, u32[]{:S(2)}) collective-permute-start(bf16[48,4096]{1,0:T(8,128)(2,1)S(1)} %collective-permute-done.2.refs_2_), channel_id=1, source_target_pairs={{0,6},{1,7},{2,0},{3,1},{4,2},{5,3},{6,4},{7,5},{8,14},{9,15},{10,... | collective-permute-start | bytes 1179656 | tf_op jit(solution)/shard_map/ppermute | solution.py:36
  24.3 9.0 %collective-permute-start.3 = (bf16[1,48,2816]{2,1,0:T(8,128)(2,1)}, bf16[1,48,2816]{2,1,0:T(8,128)(2,1)S(1)}, u32[]{:S(2)}, u32[]{:S(2)}) collective-permute-start(bf16[1,48,2816]{2,1,0:T(8,128)(2,1)} %slice.100), channel_id=1, source_target_pairs={{8,0},{9,1},{10,2},{11,3},{12,4},{13,5},{14,6},{15,7}} | collective-permute-start | bytes 811016 | tf_op jit(solution)/shard_map/ppermute | solution.py:50
  32.3 11.1 %collective-permute-start.7 = (bf16[4,48,4096]{2,1,0:T(8,128)(2,1)S(1)}, bf16[4,48,4096]{2,1,0:T(8,128)(2,1)S(1)}, u32[]{:S(2)}, u32[]{:S(2)}) collective-permute-start(bf16[4,48,4096]{2,1,0:T(8,128)(2,1)S(1)} %pad_maximum_fusion), channel_id=1, source_target_pairs={{0,1},{1,0},{2,3},{3,2},{4,5},{5,4},{6,7},{7,6},{8,9},{9,8},{10,11... | collective-permute-start | bytes 4718600 | tf_op jit(solution)/shard_map/ppermute | solution.py:40
  34.5 18.5 %collective-permute-start.12 = (bf16[1,48,2816]{2,1,0:T(8,128)(2,1)S(1)}, bf16[1,48,2816]{2,1,0:T(8,128)(2,1)S(1)}, u32[]{:S(2)}, u32[]{:S(2)}) collective-permute-start(bf16[1,48,2816]{2,1,0:T(8,128)(2,1)S(1)} %get-tuple-element.17), channel_id=1, source_target_pairs={{0,12},{1,13},{2,14},{3,15},{4,8},{5,9},{6,10},{7,11},{16,20},{17,... | collective-permute-start | bytes 811016 | tf_op jit(solution)/shard_map/ppermute | solution.py:50
  36.2 25.2 %collective-permute-start.11 = (bf16[1,48,2816]{2,1,0:T(8,128)(2,1)S(1)}, bf16[1,48,2816]{2,1,0:T(8,128)(2,1)S(1)}, u32[]{:S(2)}, u32[]{:S(2)}) collective-permute-start(bf16[1,48,2816]{2,1,0:T(8,128)(2,1)S(1)} %get-tuple-element.18), channel_id=1, source_target_pairs={{0,20},{1,21},{2,22},{3,23},{4,16},{5,17},{6,18},{7,19},{24,28},{2... | collective-permute-start | bytes 811016 | tf_op jit(solution)/shard_map/ppermute | solution.py:50
  40.9 20.5 %collective-permute-start.10 = (bf16[1,48,2816]{2,1,0:T(8,128)(2,1)S(1)}, bf16[1,48,2816]{2,1,0:T(8,128)(2,1)S(1)}, u32[]{:S(2)}, u32[]{:S(2)}) collective-permute-start(bf16[1,48,2816]{2,1,0:T(8,128)(2,1)S(1)} %get-tuple-element.19), channel_id=1, source_target_pairs={{0,28},{1,29},{2,30},{3,31},{4,24},{5,25},{6,26},{7,27},{8,12},{9,... | collective-permute-start | bytes 811016 | tf_op jit(solution)/shard_map/ppermute | solution.py:50
  42.6 33.8 %collective-permute-start.8 = (bf16[2,48,2816]{2,1,0:T(8,128)(2,1)S(1)}, bf16[2,48,2816]{2,1,0:T(8,128)(2,1)S(1)}, u32[]{:S(2)}, u32[]{:S(2)}) collective-permute-start(bf16[2,48,2816]{2,1,0:T(8,128)(2,1)S(1)} %fusion.2), channel_id=1, source_target_pairs={{8,10},{9,11},{10,12},{11,13},{12,14},{13,15},{14,8},{15,9},{16,18... | collective-permute-start | bytes 1622024 | tf_op jit(solution)/shard_map/ppermute | solution.py:50
  43.4 33.0 %collective-permute-start.9 = (bf16[2,48,2816]{2,1,0:T(8,128)(2,1)S(1)}, bf16[2,48,2816]{2,1,0:T(8,128)(2,1)S(1)}, u32[]{:S(2)}, u32[]{:S(2)}) collective-permute-start(bf16[2,48,2816]{2,1,0:T(8,128)(2,1)S(1)} %fusion.1), channel_id=1, source_target_pairs={{8,14},{9,15},{10,8},{11,9},{12,10},{13,11},{14,12},{15,13},{16,22... | collective-permute-start | bytes 1622024 | tf_op jit(solution)/shard_map/ppermute | solution.py:50
  52.9 37.9 %collective-permute-start.13 = (bf16[2,48,384]{2,1,0:T(8,128)(2,1)S(1)}, bf16[2,48,384]{2,1,0:T(8,128)(2,1)S(1)}, u32[]{:S(2)}, u32[]{:S(2)}) collective-permute-start(bf16[2,48,384]{2,1,0:T(8,128)(2,1)S(1)} %pad_maximum_fusion.5), channel_id=1, source_target_pairs={{0,2},{1,3},{2,4},{3,5},{4,6},{5,7},{6,0},{7,1},{8,10},{9,11},{10,... | collective-permute-start | bytes 221192 | tf_op jit(solution)/shard_map/ppermute | solution.py:36
  61.4 29.4 %collective-permute-start.14 = (bf16[2,48,384]{2,1,0:T(8,128)(2,1)S(1)}, bf16[2,48,384]{2,1,0:T(8,128)(2,1)S(1)}, u32[]{:S(2)}, u32[]{:S(2)}) collective-permute-start(bf16[2,48,384]{2,1,0:T(8,128)(2,1)S(1)} %pad_maximum_fusion.4), channel_id=1, source_target_pairs={{0,6},{1,7},{2,0},{3,1},{4,2},{5,3},{6,4},{7,5},{8,14},{9,15},{10,... | collective-permute-start | bytes 221192 | tf_op jit(solution)/shard_map/ppermute | solution.py:36
  61.4 29.4 %collective-permute-start.15 = (bf16[2,48,384]{2,1,0:T(8,128)(2,1)S(1)}, bf16[2,48,384]{2,1,0:T(8,128)(2,1)S(1)}, u32[]{:S(2)}, u32[]{:S(2)}) collective-permute-start(bf16[2,48,384]{2,1,0:T(8,128)(2,1)S(1)} %pad_maximum_fusion.3), channel_id=1, source_target_pairs={{0,4},{1,5},{2,6},{3,7},{4,0},{5,1},{6,2},{7,3},{8,12},{9,13},{10,... | collective-permute-start | bytes 221192 | tf_op jit(solution)/shard_map/ppermute | solution.py:36
  90.8 3.5 %collective-permute-start.16 = (bf16[4,48,4096]{2,1,0:T(8,128)(2,1)S(1)}, bf16[4,48,4096]{2,1,0:T(8,128)(2,1)S(1)}, u32[]{:S(2)}, u32[]{:S(2)}) collective-permute-start(bf16[4,48,4096]{2,1,0:T(8,128)(2,1)S(1)} %get-tuple-element.26), channel_id=1, source_target_pairs={{0,1},{1,0},{2,3},{3,2},{4,5},{5,4},{6,7},{7,6},{8,9},{9,8},{10,11... | collective-permute-start | bytes 4718600 | tf_op jit(solution)/shard_map/ppermute | solution.py:40
  94.6 12.7 %copy-start.5 = (s32[1,16]{1,0:T(1,128)S(1)}, s32[1,16]{1,0:T(1,128)}, u32[]{:S(2)}) copy-start(s32[1,16]{1,0:T(1,128)} %param.17) | copy-start | bytes 196
  94.6 12.8 %copy-start.6 = (s32[1,16]{1,0:T(1,128)S(1)}, s32[1,16]{1,0:T(1,128)}, u32[]{:S(2)}) copy-start(s32[1,16]{1,0:T(1,128)} %param.16) | copy-start | bytes 196
  94.6 11.2 %collective-permute-start.19 = (bf16[48,4096]{1,0:T(8,128)(2,1)S(1)}, bf16[48,4096]{1,0:T(8,128)(2,1)S(1)}, u32[]{:S(2)}, u32[]{:S(2)}) collective-permute-start(bf16[48,4096]{1,0:T(8,128)(2,1)S(1)} %get-tuple-element.31), channel_id=1, source_target_pairs={{0,6},{1,7},{2,0},{3,1},{4,2},{5,3},{6,4},{7,5},{8,14},{9,15},{10,... | collective-permute-start | bytes 1179656 | tf_op jit(solution)/shard_map/ppermute | solution.py:36
  95.9 14.1 %collective-permute-start.17 = (bf16[48,4096]{1,0:T(8,128)(2,1)S(1)}, bf16[48,4096]{1,0:T(8,128)(2,1)S(1)}, u32[]{:S(2)}, u32[]{:S(2)}) collective-permute-start(bf16[48,4096]{1,0:T(8,128)(2,1)S(1)} %get-tuple-element.30), channel_id=1, source_target_pairs={{8,0},{9,1},{10,2},{11,3},{12,4},{13,5},{14,6},{15,7},{16,8},{17,9... | collective-permute-start | bytes 1179656 | tf_op jit(solution)/shard_map/ppermute | solution.py:50
  97.2 21.1 %collective-permute-start.18 = (bf16[48,4096]{1,0:T(8,128)(2,1)S(1)}, bf16[48,4096]{1,0:T(8,128)(2,1)S(1)}, u32[]{:S(2)}, u32[]{:S(2)}) collective-permute-start(bf16[48,4096]{1,0:T(8,128)(2,1)S(1)} %get-tuple-element.32), channel_id=1, source_target_pairs={{8,2},{9,3},{10,4},{11,5},{12,6},{13,7},{14,0},{15,1},{16,10},{17,... | collective-permute-start | bytes 1179656 | tf_op jit(solution)/shard_map/ppermute | solution.py:50
  106.0 20.3 %collective-permute-start.20 = (bf16[48,4096]{1,0:T(8,128)(2,1)S(1)}, bf16[48,4096]{1,0:T(8,128)(2,1)S(1)}, u32[]{:S(2)}, u32[]{:S(2)}) collective-permute-start(bf16[48,4096]{1,0:T(8,128)(2,1)S(1)} %add_convert_fusion.1), channel_id=1, source_target_pairs={{8,6},{9,7},{10,0},{11,1},{12,2},{13,3},{14,4},{15,5},{16,14},{17,... | collective-permute-start | bytes 1179656 | tf_op jit(solution)/shard_map/ppermute | solution.py:50

commit v6 on v5

--- a/solution.py
+++ b/solution.py
@@ -9,7 +9,7 @@
 
 CAP = 3
 LANES = 128
-VMEM = 40 * 1024 * 1024
+VMEM = 16 * 1024 * 1024
 COST = pl.CostEstimate(flops=0, bytes_accessed=0, transcendentals=0)
 
 
@@ -182,7 +182,7 @@
         + [pl.BlockSpec((units, tile), lambda i: (0, i + first // tile))] * 2,
         out_specs=[pl.BlockSpec(out + (tile,), lambda i: (0, 0, i))] * 2,
         out_shape=[jax.ShapeDtypeStruct(out + (width,), jnp.bfloat16)] * 2,
-        compiler_params=pltpu.CompilerParams(vmem_limit_bytes=VMEM),
+        compiler_params=pltpu.CompilerParams(vmem_limit_bytes=2 * VMEM),
         cost_estimate=COST,
         name="terms",
     )(near, far, w_gate, w_up)

time: 128 us -> 127 us (level)
  local copies, waits for them, and re-layouts: 5.65 us -> 10.9 us
  starting transfers between devices: 50.5 us -> 46.5 us
  Pallas kernels: 27.1 us -> 25.2 us
    unnamed x14 -> x26, local copies, waits for them, and re-layouts: 3.8 us -> 9.04 us
    ppermute x7, starting transfers between devices: 33.1 us -> 29 us  [rotated(): return lax.ppermute(value, 'dp', pairs)]
  transfers between devices with their start and end apart: 21 -> 21, of which waited for: 7 -> 7; matrix products, arithmetic and copies ran while one was open for 6% -> 6% of each run, Pallas kernels for 21% -> 20%
where the time goes in v6:
time: 127 us; the launch traced here: 126 us
  starting transfers between devices  46.5 us (37%)
  waiting for transfers between devices  35.7 us (28%)
  Pallas kernels  25.2 us (20%)
  local copies, waits for them, and re-layouts  10.9 us (9%)
  other arithmetic  6.86 us (5%)
    ppermute x7, starting transfers between devices, rotated(): return lax.ppermute(value, 'dp', pairs)  29 us
    ppermute x11, starting transfers between devices, moved(): return lax.ppermute(value, ('section', 'dp'), pairs)  17.3 us
    ppermute x11, waiting for transfers between devices, moved(): return lax.ppermute(value, ('section', 'dp'), pairs)  17.3 us
    ppermute x7, waiting for transfers between devices, rotated(): return lax.ppermute(value, 'dp', pairs)  15.1 us
    pallas_call x1, Pallas kernels, terms(): pl.pallas_call(term_kernel, grid=(width // tile,), in_specs=[pl.BlockSpec...  12.2 us
    unnamed x26, local copies, waits for them, and re-layouts  9.04 us
    pallas_call x1, Pallas kernels, hidden_grad(): pl.pallas_call(hidden_grad_kernel, grid=(width // tile,), in_specs=[pl.Bl...  7.62 us
    ppermute x3, waiting for transfers between devices, swapped(): lax.ppermute(value, 'dp', [(i, i ^ 1) for i in range(lax.axis_size('dp'))])  3.4 us
  transfers between devices with their start and end apart: 21, of which 7 were waited for; matrix products, arithmetic and copies ran while one was open for 6% of the time, Pallas kernels for 20%

profile of v6, /device:TPU:0, one launch (start us, length us, event | category | flops | bytes accessed | tf_op | source)
XLA Modules:
  0.0 126.3 jit_solution(4730675906003291916)
XLA Ops:
  0.6 5.1 %collective-permute-start.2 = (bf16[48,4096]{1,0:T(8,128)(2,1)}, bf16[48,4096]{1,0:T(8,128)(2,1)S(1)}, u32[]{:S(2)}, u32[]{:S(2)}) collective-permute-start(bf16[48,4096]{1,0:T(8,128)(2,1)} %bitcast.80), channel_id=1, source_target_pairs={{0,6},{1,7},{2,0},{3,1},{4,2},{5,3},{6,4},{7,5},{8,14},{9,15},{10,... | collective-permute-start | bytes 1179656 | tf_op jit(solution)/shard_map/ppermute | solution.py:36
  5.7 1.2 copy-done.1
  7.0 1.2 copy-done.3
  9.5 0.9 hidden_blocks.1
  12.9 1.3 %collective-permute-start.5 = (bf16[1,48,2816]{2,1,0:T(8,128)(2,1)}, bf16[1,48,2816]{2,1,0:T(8,128)(2,1)}, u32[]{:S(2)}, u32[]{:S(2)}) collective-permute-start(bf16[1,48,2816]{2,1,0:T(8,128)(2,1)} %slice.100), channel_id=1, source_target_pairs={{24,0},{25,1},{26,2},{27,3},{28,4},{29,5},{30,6},{31,7}} | collective-permute-start | bytes 811016 | tf_op jit(solution)/shard_map/ppermute | solution.py:50
  14.1 1.3 %collective-permute-start.4 = (bf16[1,48,2816]{2,1,0:T(8,128)(2,1)}, bf16[1,48,2816]{2,1,0:T(8,128)(2,1)}, u32[]{:S(2)}, u32[]{:S(2)}) collective-permute-start(bf16[1,48,2816]{2,1,0:T(8,128)(2,1)} %slice.100), channel_id=1, source_target_pairs={{16,0},{17,1},{18,2},{19,3},{20,4},{21,5},{22,6},{23,7}} | collective-permute-start | bytes 811016 | tf_op jit(solution)/shard_map/ppermute | solution.py:50
  15.6 1.2 pad_maximum_fusion.1
  18.4 3.9 %collective-permute-start.6 = (bf16[48,4096]{1,0:T(8,128)(2,1)S(1)}, bf16[48,4096]{1,0:T(8,128)(2,1)S(1)}, u32[]{:S(2)}, u32[]{:S(2)}) collective-permute-start(bf16[48,4096]{1,0:T(8,128)(2,1)S(1)} %collective-permute-done.2.refs_2_), channel_id=1, source_target_pairs={{0,6},{1,7},{2,0},{3,1},{4,2},{5,3},{6,4},{7,5},{8,14},{9,15},{10,... | collective-permute-start | bytes 1179656 | tf_op jit(solution)/shard_map/ppermute | solution.py:36
  23.8 1.3 %collective-permute-start.3 = (bf16[1,48,2816]{2,1,0:T(8,128)(2,1)}, bf16[1,48,2816]{2,1,0:T(8,128)(2,1)S(1)}, u32[]{:S(2)}, u32[]{:S(2)}) collective-permute-start(bf16[1,48,2816]{2,1,0:T(8,128)(2,1)} %slice.100), channel_id=1, source_target_pairs={{8,0},{9,1},{10,2},{11,3},{12,4},{13,5},{14,6},{15,7}} | collective-permute-start | bytes 811016 | tf_op jit(solution)/shard_map/ppermute | solution.py:50
  25.1 7.0 %collective-permute-done.6.refs_3_ = bf16[48,4096]{1,0:T(8,128)(2,1)S(1)} collective-permute-done((bf16[48,4096]{1,0:T(8,128)(2,1)S(1)}, bf16[48,4096]{1,0:T(8,128)(2,1)S(1)}, u32[]{:S(2)}, u32[]{:S(2)}) %collective-permute-start.6) | collective-permute-done | bytes 393248 | tf_op jit(solution)/shard_map/ppermute | solution.py:36
  32.6 1.2 collective-permute-done.3
  33.8 1.1 broadcast_select_fusion
  35.1 1.3 %collective-permute-start.12 = (bf16[1,48,2816]{2,1,0:T(8,128)(2,1)S(1)}, bf16[1,48,2816]{2,1,0:T(8,128)(2,1)S(1)}, u32[]{:S(2)}, u32[]{:S(2)}) collective-permute-start(bf16[1,48,2816]{2,1,0:T(8,128)(2,1)S(1)} %get-tuple-element.17), channel_id=1, source_target_pairs={{0,12},{1,13},{2,14},{3,15},{4,8},{5,9},{6,10},{7,11},{16,20},{17,... | collective-permute-start | bytes 811016 | tf_op jit(solution)/shard_map/ppermute | solution.py:50
  36.4 5.2 %collective-permute-start.11 = (bf16[1,48,2816]{2,1,0:T(8,128)(2,1)S(1)}, bf16[1,48,2816]{2,1,0:T(8,128)(2,1)S(1)}, u32[]{:S(2)}, u32[]{:S(2)}) collective-permute-start(bf16[1,48,2816]{2,1,0:T(8,128)(2,1)S(1)} %get-tuple-element.18), channel_id=1, source_target_pairs={{0,20},{1,21},{2,22},{3,23},{4,16},{5,17},{6,18},{7,19},{24,28},{2... | collective-permute-start | bytes 811016 | tf_op jit(solution)/shard_map/ppermute | solution.py:50
  41.6 1.6 %collective-permute-start.10 = (bf16[1,48,2816]{2,1,0:T(8,128)(2,1)S(1)}, bf16[1,48,2816]{2,1,0:T(8,128)(2,1)S(1)}, u32[]{:S(2)}, u32[]{:S(2)}) collective-permute-start(bf16[1,48,2816]{2,1,0:T(8,128)(2,1)S(1)} %get-tuple-element.19), channel_id=1, source_target_pairs={{0,28},{1,29},{2,30},{3,31},{4,24},{5,25},{6,26},{7,27},{8,12},{9,... | collective-permute-start | bytes 811016 | tf_op jit(solution)/shard_map/ppermute | solution.py:50
  44.0 0.8 collective-permute-start.9
  44.9 4.6 %copy-done = bf16[1,1408,4096]{2,1,0:T(8,128)(2,1)S(1)} copy-done((bf16[1,1408,4096]{2,1,0:T(8,128)(2,1)S(1)}, bf16[1,1408,4096]{2,1,0:T(8,128)(2,1)}, u32[]{:S(2)}) %copy-start) | copy-done | bytes 11534360
  49.5 7.6 %hidden_grad.1.dh_ref = bf16[384,1408]{1,0:T(8,128)(2,1)S(1)} custom-call(bf16[48,4096]{1,0:T(8,128)(2,1)S(1)} %bitcast.82, bf16[48,4096]{1,0:T(8,128)(2,1)S(1)} %collective-permute-done.1.refs_1_, bf16[48,4096]{1,0:T(8,128)(2,1)S(1)} %collective-permute-done.2.refs_2_, bf16[48,4096]{1,0:T(8,128)(2,1)S(1)} %collective-permute-done.6.refs_3_, ...), custom_call_target="tpu_custom_call" | custom-call | tf_op jit(solution)/shard_map/hidden_grad/pallas_call | solution.py:121
  57.1 4.4 %collective-permute-start.13 = (bf16[2,48,384]{2,1,0:T(8,128)(2,1)S(1)}, bf16[2,48,384]{2,1,0:T(8,128)(2,1)S(1)}, u32[]{:S(2)}, u32[]{:S(2)}) collective-permute-start(bf16[2,48,384]{2,1,0:T(8,128)(2,1)S(1)} %pad_maximum_fusion.5), channel_id=1, source_target_pairs={{0,2},{1,3},{2,4},{3,5},{4,6},{5,7},{6,0},{7,1},{8,10},{9,11},{10,... | collective-permute-start | bytes 221192 | tf_op jit(solution)/shard_map/ppermute | solution.py:36
  61.6 14.3 %collective-permute-start.15 = (bf16[2,48,384]{2,1,0:T(8,128)(2,1)S(1)}, bf16[2,48,384]{2,1,0:T(8,128)(2,1)S(1)}, u32[]{:S(2)}, u32[]{:S(2)}) collective-permute-start(bf16[2,48,384]{2,1,0:T(8,128)(2,1)S(1)} %pad_maximum_fusion.3), channel_id=1, source_target_pairs={{0,4},{1,5},{2,6},{3,7},{4,0},{5,1},{6,2},{7,3},{8,12},{9,13},{10,... | collective-permute-start | bytes 221192 | tf_op jit(solution)/shard_map/ppermute | solution.py:36
  76.5 1.5 %local_gradients.2.near_ref = bf16[288,2816]{1,0:T(8,128)(2,1)S(1)} custom-call(bf16[384,1408]{1,0:T(8,128)(2,1)S(1)} %hidden_grad.1.dh_ref, bf16[2,48,2816]{2,1,0:T(8,128)(2,1)S(1)} %fusion.refs_0_, bf16[2,48,2816]{2,1,0:T(8,128)(2,1)S(1)} %collective-permute-done.8.refs_1_, bf16[2,48,2816]{2,1,0:T(8,128)(2,1)S(1)} %collective-permute-done.9.refs_2_), custom_call_target="tpu_custom_call" | custom-call | tf_op jit(solution)/shard_map/local_gradients/pallas_call | solution.py:152
  78.0 12.2 %terms.1 = (bf16[4,48,4096]{2,1,0:T(8,128)(2,1)S(1)}, bf16[4,48,4096]{2,1,0:T(8,128)(2,1)S(1)}) custom-call(bf16[288,2816]{1,0:T(8,128)(2,1)S(1)} %local_gradients.2.near_ref, bf16[96,2816]{1,0:T(8,128)(2,1)S(1)} %local_gradients.3.far_ref, bf16[1408,4096]{1,0:T(8,128)(2,1)S(1)} %bitcast.76, bf16[1408,4096]{1,0:T(8,128)(2,1)} %bitcast.89), custom_call_target="tpu_custom_call" | custom-call | tf_op jit(solution)/shard_map/terms/pallas_call | solution.py:178
  90.3 3.4 %collective-permute-done.16 = bf16[4,48,4096]{2,1,0:T(8,128)(2,1)S(1)} collective-permute-done((bf16[4,48,4096]{2,1,0:T(8,128)(2,1)S(1)}, bf16[4,48,4096]{2,1,0:T(8,128)(2,1)S(1)}, u32[]{:S(2)}, u32[]{:S(2)}) %collective-permute-start.16) | collective-permute-done | bytes 1572896 | tf_op jit(solution)/shard_map/ppermute | solution.py:40
  94.0 1.3 %collective-permute-start.19 = (bf16[48,4096]{1,0:T(8,128)(2,1)S(1)}, bf16[48,4096]{1,0:T(8,128)(2,1)S(1)}, u32[]{:S(2)}, u32[]{:S(2)}) collective-permute-start(bf16[48,4096]{1,0:T(8,128)(2,1)S(1)} %get-tuple-element.31), channel_id=1, source_target_pairs={{0,6},{1,7},{2,0},{3,1},{4,2},{5,3},{6,4},{7,5},{8,14},{9,15},{10,... | collective-permute-start | bytes 1179656 | tf_op jit(solution)/shard_map/ppermute | solution.py:36
  95.3 1.3 %collective-permute-start.17 = (bf16[48,4096]{1,0:T(8,128)(2,1)S(1)}, bf16[48,4096]{1,0:T(8,128)(2,1)S(1)}, u32[]{:S(2)}, u32[]{:S(2)}) collective-permute-start(bf16[48,4096]{1,0:T(8,128)(2,1)S(1)} %get-tuple-element.30), channel_id=1, source_target_pairs={{8,0},{9,1},{10,2},{11,3},{12,4},{13,5},{14,6},{15,7},{16,8},{17,9... | collective-permute-start | bytes 1179656 | tf_op jit(solution)/shard_map/ppermute | solution.py:50
  96.6 1.3 %collective-permute-start.18 = (bf16[48,4096]{1,0:T(8,128)(2,1)S(1)}, bf16[48,4096]{1,0:T(8,128)(2,1)S(1)}, u32[]{:S(2)}, u32[]{:S(2)}) collective-permute-start(bf16[48,4096]{1,0:T(8,128)(2,1)S(1)} %get-tuple-element.32), channel_id=1, source_target_pairs={{8,2},{9,3},{10,4},{11,5},{12,6},{13,7},{14,0},{15,1},{16,10},{17,... | collective-permute-start | bytes 1179656 | tf_op jit(solution)/shard_map/ppermute | solution.py:50
  97.9 7.3 %collective-permute-done.19 = bf16[48,4096]{1,0:T(8,128)(2,1)S(1)} collective-permute-done((bf16[48,4096]{1,0:T(8,128)(2,1)S(1)}, bf16[48,4096]{1,0:T(8,128)(2,1)S(1)}, u32[]{:S(2)}, u32[]{:S(2)}) %collective-permute-start.19) | collective-permute-done | bytes 393248 | tf_op jit(solution)/shard_map/ppermute | solution.py:36
  105.4 1.3 %collective-permute-start.20 = (bf16[48,4096]{1,0:T(8,128)(2,1)S(1)}, bf16[48,4096]{1,0:T(8,128)(2,1)S(1)}, u32[]{:S(2)}, u32[]{:S(2)}) collective-permute-start(bf16[48,4096]{1,0:T(8,128)(2,1)S(1)} %add_convert_fusion.1), channel_id=1, source_target_pairs={{8,6},{9,7},{10,0},{11,1},{12,2},{13,3},{14,4},{15,5},{16,14},{17,... | collective-permute-start | bytes 1179656 | tf_op jit(solution)/shard_map/ppermute | solution.py:50
  106.9 2.4 %block_sums.1 = bf16[3,128,128]{2,1,0:T(8,128)(2,1)} custom-call(s32[3]{0:T(128)S(1)} %select_reduce_fusion.cols_ref, bf16[4,48,4096]{2,1,0:T(8,128)(2,1)S(1)} %collective-permute-done.7.refs_4_.other_ref, bf16[48,4096]{1,0:T(8,128)(2,1)S(1)} %bitcast.83, bf16[48,4096]{1,0:T(8,128)(2,1)S(1)} %collective-permute-done.1.refs_1_, ...), custom_call_target="tpu_custom_call" | custom-call | tf_op jit(solution)/shard_map/block_sums/pallas_call | solution.py:202
  109.4 8.4 %collective-permute-done.18 = bf16[48,4096]{1,0:T(8,128)(2,1)S(1)} collective-permute-done((bf16[48,4096]{1,0:T(8,128)(2,1)S(1)}, bf16[48,4096]{1,0:T(8,128)(2,1)S(1)}, u32[]{:S(2)}, u32[]{:S(2)}) %collective-permute-start.18) | collective-permute-done | bytes 393248 | tf_op jit(solution)/shard_map/ppermute | solution.py:50
  117.7 7.6 %collective-permute-done.20 = bf16[48,4096]{1,0:T(8,128)(2,1)S(1)} collective-permute-done((bf16[48,4096]{1,0:T(8,128)(2,1)S(1)}, bf16[48,4096]{1,0:T(8,128)(2,1)S(1)}, u32[]{:S(2)}, u32[]{:S(2)}) %collective-permute-start.20) | collective-permute-done | bytes 393248 | tf_op jit(solution)/shard_map/ppermute | solution.py:50
  125.4 0.9 fusion.7
  (72 shorter events, 9.6 us)
Async XLA Ops:
  0.6 17.8 %collective-permute-start.2 = (bf16[48,4096]{1,0:T(8,128)(2,1)}, bf16[48,4096]{1,0:T(8,128)(2,1)S(1)}, u32[]{:S(2)}, u32[]{:S(2)}) collective-permute-start(bf16[48,4096]{1,0:T(8,128)(2,1)} %bitcast.80), channel_id=1, source_target_pairs={{0,6},{1,7},{2,0},{3,1},{4,2},{5,3},{6,4},{7,5},{8,14},{9,15},{10,... | collective-permute-start | bytes 1179656 | tf_op jit(solution)/shard_map/ppermute | solution.py:36
  5.7 18.1 %collective-permute-start.1 = (bf16[48,4096]{1,0:T(8,128)(2,1)}, bf16[48,4096]{1,0:T(8,128)(2,1)S(1)}, u32[]{:S(2)}, u32[]{:S(2)}) collective-permute-start(bf16[48,4096]{1,0:T(8,128)(2,1)} %bitcast.81), channel_id=1, source_target_pairs={{0,2},{1,3},{2,4},{3,5},{4,6},{5,7},{6,0},{7,1},{8,10},{9,11},{10,... | collective-permute-start | bytes 1179656 | tf_op jit(solution)/shard_map/ppermute | solution.py:36
  5.7 1.2 copy-start.1
  7.0 1.2 copy-start.3
  9.5 1.2 copy-start.2
  9.5 1.6 %copy-start.4 = (bf16[1,48,11264]{2,1,0:T(8,128)(2,1)S(1)}, bf16[1,48,11264]{2,1,0:T(8,128)(2,1)}, u32[]{:S(2)}) copy-start(bf16[1,48,11264]{2,1,0:T(8,128)(2,1)} %param.13) | copy-start | bytes 3244036
  12.9 19.7 %collective-permute-start.5 = (bf16[1,48,2816]{2,1,0:T(8,128)(2,1)}, bf16[1,48,2816]{2,1,0:T(8,128)(2,1)}, u32[]{:S(2)}, u32[]{:S(2)}) collective-permute-start(bf16[1,48,2816]{2,1,0:T(8,128)(2,1)} %slice.100), channel_id=1, source_target_pairs={{24,0},{25,1},{26,2},{27,3},{28,4},{29,5},{30,6},{31,7}} | collective-permute-start | bytes 811016 | tf_op jit(solution)/shard_map/ppermute | solution.py:50
  14.1 18.4 %collective-permute-start.4 = (bf16[1,48,2816]{2,1,0:T(8,128)(2,1)}, bf16[1,48,2816]{2,1,0:T(8,128)(2,1)}, u32[]{:S(2)}, u32[]{:S(2)}) collective-permute-start(bf16[1,48,2816]{2,1,0:T(8,128)(2,1)} %slice.100), channel_id=1, source_target_pairs={{16,0},{17,1},{18,2},{19,3},{20,4},{21,5},{22,6},{23,7}} | collective-permute-start | bytes 811016 | tf_op jit(solution)/shard_map/ppermute | solution.py:50
  15.6 16.6 %copy-start.5 = (bf16[1,48,4096]{2,1,0:T(8,128)(2,1)S(1)}, bf16[1,48,4096]{2,1,0:T(8,128)(2,1)}, u32[]{:S(2)}) copy-start(bf16[1,48,4096]{2,1,0:T(8,128)(2,1)} %param.9) | copy-start | bytes 1179652
  16.8 15.6 %collective-permute-start = (bf16[4,48,3200]{2,1,0:T(8,128)(2,1)}, bf16[4,48,3200]{2,1,0:T(8,128)(2,1)S(1)}, u32[]{:S(2)}, u32[]{:S(2)}) collective-permute-start(bf16[4,48,3200]{2,1,0:T(8,128)(2,1)} %pad_maximum_fusion.1), channel_id=1, source_target_pairs={{0,1},{1,0},{2,3},{3,2},{4,5},{5,4},{6,7},{7,6},{8,9},{9,8},{10,11... | collective-permute-start | bytes 3686408 | tf_op jit(solution)/shard_map/ppermute | solution.py:40
  18.4 13.7 %collective-permute-start.6 = (bf16[48,4096]{1,0:T(8,128)(2,1)S(1)}, bf16[48,4096]{1,0:T(8,128)(2,1)S(1)}, u32[]{:S(2)}, u32[]{:S(2)}) collective-permute-start(bf16[48,4096]{1,0:T(8,128)(2,1)S(1)} %collective-permute-done.2.refs_2_), channel_id=1, source_target_pairs={{0,6},{1,7},{2,0},{3,1},{4,2},{5,3},{6,4},{7,5},{8,14},{9,15},{10,... | collective-permute-start | bytes 1179656 | tf_op jit(solution)/shard_map/ppermute | solution.py:36
  23.8 10.0 %collective-permute-start.3 = (bf16[1,48,2816]{2,1,0:T(8,128)(2,1)}, bf16[1,48,2816]{2,1,0:T(8,128)(2,1)S(1)}, u32[]{:S(2)}, u32[]{:S(2)}) collective-permute-start(bf16[1,48,2816]{2,1,0:T(8,128)(2,1)} %slice.100), channel_id=1, source_target_pairs={{8,0},{9,1},{10,2},{11,3},{12,4},{13,5},{14,6},{15,7}} | collective-permute-start | bytes 811016 | tf_op jit(solution)/shard_map/ppermute | solution.py:50
  32.3 11.7 %collective-permute-start.7 = (bf16[4,48,4096]{2,1,0:T(8,128)(2,1)S(1)}, bf16[4,48,4096]{2,1,0:T(8,128)(2,1)S(1)}, u32[]{:S(2)}, u32[]{:S(2)}) collective-permute-start(bf16[4,48,4096]{2,1,0:T(8,128)(2,1)S(1)} %pad_maximum_fusion), channel_id=1, source_target_pairs={{0,1},{1,0},{2,3},{3,2},{4,5},{5,4},{6,7},{7,6},{8,9},{9,8},{10,11... | collective-permute-start | bytes 4718600 | tf_op jit(solution)/shard_map/ppermute | solution.py:40
  35.1 22.1 %collective-permute-start.12 = (bf16[1,48,2816]{2,1,0:T(8,128)(2,1)S(1)}, bf16[1,48,2816]{2,1,0:T(8,128)(2,1)S(1)}, u32[]{:S(2)}, u32[]{:S(2)}) collective-permute-start(bf16[1,48,2816]{2,1,0:T(8,128)(2,1)S(1)} %get-tuple-element.17), channel_id=1, source_target_pairs={{0,12},{1,13},{2,14},{3,15},{4,8},{5,9},{6,10},{7,11},{16,20},{17,... | collective-permute-start | bytes 811016 | tf_op jit(solution)/shard_map/ppermute | solution.py:50
  36.4 25.2 %collective-permute-start.11 = (bf16[1,48,2816]{2,1,0:T(8,128)(2,1)S(1)}, bf16[1,48,2816]{2,1,0:T(8,128)(2,1)S(1)}, u32[]{:S(2)}, u32[]{:S(2)}) collective-permute-start(bf16[1,48,2816]{2,1,0:T(8,128)(2,1)S(1)} %get-tuple-element.18), channel_id=1, source_target_pairs={{0,20},{1,21},{2,22},{3,23},{4,16},{5,17},{6,18},{7,19},{24,28},{2... | collective-permute-start | bytes 811016 | tf_op jit(solution)/shard_map/ppermute | solution.py:50
  41.6 20.0 %collective-permute-start.10 = (bf16[1,48,2816]{2,1,0:T(8,128)(2,1)S(1)}, bf16[1,48,2816]{2,1,0:T(8,128)(2,1)S(1)}, u32[]{:S(2)}, u32[]{:S(2)}) collective-permute-start(bf16[1,48,2816]{2,1,0:T(8,128)(2,1)S(1)} %get-tuple-element.19), channel_id=1, source_target_pairs={{0,28},{1,29},{2,30},{3,31},{4,24},{5,25},{6,26},{7,27},{8,12},{9,... | collective-permute-start | bytes 811016 | tf_op jit(solution)/shard_map/ppermute | solution.py:50
  43.2 33.2 %collective-permute-start.8 = (bf16[2,48,2816]{2,1,0:T(8,128)(2,1)S(1)}, bf16[2,48,2816]{2,1,0:T(8,128)(2,1)S(1)}, u32[]{:S(2)}, u32[]{:S(2)}) collective-permute-start(bf16[2,48,2816]{2,1,0:T(8,128)(2,1)S(1)} %fusion.2), channel_id=1, source_target_pairs={{8,10},{9,11},{10,12},{11,13},{12,14},{13,15},{14,8},{15,9},{16,18... | collective-permute-start | bytes 1622024 | tf_op jit(solution)/shard_map/ppermute | solution.py:50
  44.0 34.0 %slice-start = ((s8[11534336]{0:T(1024)(128)(4,1)}), s8[4194304]{0:T(1024)(128)(4,1)S(1)}, s32[]{:S(2)}) async-start(s8[11534336]{0:T(1024)(128)(4,1)} %bitcast.74), calls=%async_computation | async-start | bytes 8388608
  44.0 32.4 %collective-permute-start.9 = (bf16[2,48,2816]{2,1,0:T(8,128)(2,1)S(1)}, bf16[2,48,2816]{2,1,0:T(8,128)(2,1)S(1)}, u32[]{:S(2)}, u32[]{:S(2)}) collective-permute-start(bf16[2,48,2816]{2,1,0:T(8,128)(2,1)S(1)} %fusion.1), channel_id=1, source_target_pairs={{8,14},{9,15},{10,8},{11,9},{12,10},{13,11},{14,12},{15,13},{16,22... | collective-permute-start | bytes 1622024 | tf_op jit(solution)/shard_map/ppermute | solution.py:50
  44.9 4.6 %copy-start = (bf16[1,1408,4096]{2,1,0:T(8,128)(2,1)S(1)}, bf16[1,1408,4096]{2,1,0:T(8,128)(2,1)}, u32[]{:S(2)}) copy-start(bf16[1,1408,4096]{2,1,0:T(8,128)(2,1)} %param.10) | copy-start | bytes 34603012
  49.5 28.5 %slice-start.1 = ((s8[11534336]{0:T(1024)(128)(4,1)}), s8[4194304]{0:T(1024)(128)(4,1)S(1)}, s32[]{:S(2)}) async-start(s8[11534336]{0:T(1024)(128)(4,1)} %bitcast.74), calls=%async_computation.1 | async-start | bytes 8388608
  49.5 28.5 %slice-start.2 = ((s8[11534336]{0:T(1024)(128)(4,1)}), s8[3145728]{0:T(1024)(128)(4,1)S(1)}, s32[]{:S(2)}) async-start(s8[11534336]{0:T(1024)(128)(4,1)} %bitcast.74), calls=%async_computation.2 | async-start | bytes 6291456
  57.1 33.0 %collective-permute-start.13 = (bf16[2,48,384]{2,1,0:T(8,128)(2,1)S(1)}, bf16[2,48,384]{2,1,0:T(8,128)(2,1)S(1)}, u32[]{:S(2)}, u32[]{:S(2)}) collective-permute-start(bf16[2,48,384]{2,1,0:T(8,128)(2,1)S(1)} %pad_maximum_fusion.5), channel_id=1, source_target_pairs={{0,2},{1,3},{2,4},{3,5},{4,6},{5,7},{6,0},{7,1},{8,10},{9,11},{10,... | collective-permute-start | bytes 221192 | tf_op jit(solution)/shard_map/ppermute | solution.py:36
  61.5 28.7 %collective-permute-start.14 = (bf16[2,48,384]{2,1,0:T(8,128)(2,1)S(1)}, bf16[2,48,384]{2,1,0:T(8,128)(2,1)S(1)}, u32[]{:S(2)}, u32[]{:S(2)}) collective-permute-start(bf16[2,48,384]{2,1,0:T(8,128)(2,1)S(1)} %pad_maximum_fusion.4), channel_id=1, source_target_pairs={{0,6},{1,7},{2,0},{3,1},{4,2},{5,3},{6,4},{7,5},{8,14},{9,15},{10,... | collective-permute-start | bytes 221192 | tf_op jit(solution)/shard_map/ppermute | solution.py:36
  61.6 28.7 %collective-permute-start.15 = (bf16[2,48,384]{2,1,0:T(8,128)(2,1)S(1)}, bf16[2,48,384]{2,1,0:T(8,128)(2,1)S(1)}, u32[]{:S(2)}, u32[]{:S(2)}) collective-permute-start(bf16[2,48,384]{2,1,0:T(8,128)(2,1)S(1)} %pad_maximum_fusion.3), channel_id=1, source_target_pairs={{0,4},{1,5},{2,6},{3,7},{4,0},{5,1},{6,2},{7,3},{8,12},{9,13},{10,... | collective-permute-start | bytes 221192 | tf_op jit(solution)/shard_map/ppermute | solution.py:36
  90.2 3.5 %collective-permute-start.16 = (bf16[4,48,4096]{2,1,0:T(8,128)(2,1)S(1)}, bf16[4,48,4096]{2,1,0:T(8,128)(2,1)S(1)}, u32[]{:S(2)}, u32[]{:S(2)}) collective-permute-start(bf16[4,48,4096]{2,1,0:T(8,128)(2,1)S(1)} %get-tuple-element.26), channel_id=1, source_target_pairs={{0,1},{1,0},{2,3},{3,2},{4,5},{5,4},{6,7},{7,6},{8,9},{9,8},{10,11... | collective-permute-start | bytes 4718600 | tf_op jit(solution)/shard_map/ppermute | solution.py:40
  94.0 12.7 %copy-start.8 = (s32[1,16]{1,0:T(1,128)S(1)}, s32[1,16]{1,0:T(1,128)}, u32[]{:S(2)}) copy-start(s32[1,16]{1,0:T(1,128)} %param.17) | copy-start | bytes 196
  94.0 12.8 %copy-start.9 = (s32[1,16]{1,0:T(1,128)S(1)}, s32[1,16]{1,0:T(1,128)}, u32[]{:S(2)}) copy-start(s32[1,16]{1,0:T(1,128)} %param.16) | copy-start | bytes 196
  94.0 11.2 %collective-permute-start.19 = (bf16[48,4096]{1,0:T(8,128)(2,1)S(1)}, bf16[48,4096]{1,0:T(8,128)(2,1)S(1)}, u32[]{:S(2)}, u32[]{:S(2)}) collective-permute-start(bf16[48,4096]{1,0:T(8,128)(2,1)S(1)} %get-tuple-element.31), channel_id=1, source_target_pairs={{0,6},{1,7},{2,0},{3,1},{4,2},{5,3},{6,4},{7,5},{8,14},{9,15},{10,... | collective-permute-start | bytes 1179656 | tf_op jit(solution)/shard_map/ppermute | solution.py:36
  95.3 14.1 %collective-permute-start.17 = (bf16[48,4096]{1,0:T(8,128)(2,1)S(1)}, bf16[48,4096]{1,0:T(8,128)(2,1)S(1)}, u32[]{:S(2)}, u32[]{:S(2)}) collective-permute-start(bf16[48,4096]{1,0:T(8,128)(2,1)S(1)} %get-tuple-element.30), channel_id=1, source_target_pairs={{8,0},{9,1},{10,2},{11,3},{12,4},{13,5},{14,6},{15,7},{16,8},{17,9... | collective-permute-start | bytes 1179656 | tf_op jit(solution)/shard_map/ppermute | solution.py:50
  96.6 21.2 %collective-permute-start.18 = (bf16[48,4096]{1,0:T(8,128)(2,1)S(1)}, bf16[48,4096]{1,0:T(8,128)(2,1)S(1)}, u32[]{:S(2)}, u32[]{:S(2)}) collective-permute-start(bf16[48,4096]{1,0:T(8,128)(2,1)S(1)} %get-tuple-element.32), channel_id=1, source_target_pairs={{8,2},{9,3},{10,4},{11,5},{12,6},{13,7},{14,0},{15,1},{16,10},{17,... | collective-permute-start | bytes 1179656 | tf_op jit(solution)/shard_map/ppermute | solution.py:50
  105.4 20.0 %collective-permute-start.20 = (bf16[48,4096]{1,0:T(8,128)(2,1)S(1)}, bf16[48,4096]{1,0:T(8,128)(2,1)S(1)}, u32[]{:S(2)}, u32[]{:S(2)}) collective-permute-start(bf16[48,4096]{1,0:T(8,128)(2,1)S(1)} %add_convert_fusion.1), channel_id=1, source_target_pairs={{8,6},{9,7},{10,0},{11,1},{12,2},{13,3},{14,4},{15,5},{16,14},{17,... | collective-permute-start | bytes 1179656 | tf_op jit(solution)/shard_map/ppermute | solution.py:50
  (2 other events, 1.3 us)
